TPU v7x, 32 devices: a whole 2x2x4 slice. The times are simulated.
32 devices in a mesh: gx: 2 (over x), gy: 4 (over y, core), gz: 4 (over z).
Axes of the slice: x: 2, y: 2, z: 4, core: 2. Of those that a mesh axis runs over, the one named last changes fastest.
Arguments:
- positions: float32 [3, 16384], P(None, ('gx', 'gy', 'gz')), may hold values from 0 to 1
- features: bfloat16 [64, 16384], P(None, ('gx', 'gy', 'gz')), may hold values from -6 to 6
- species: int32 [16384], P(('gx', 'gy', 'gz')), may hold values from 0 to 3
- species_scale: bfloat16 [4], replicated, may hold values from 0.5 to 2
- w_first: bfloat16 [64, 64], replicated, may hold values from -0.75 to 0.75
- w_second: bfloat16 [64, 64], replicated, may hold values from -0.75 to 0.75
- w_radial: float32 [64, 8], replicated, may hold values from -4 to 4
- w_mid: bfloat16 [64, 64], replicated, may hold values from -0.75 to 0.75
- w_last: bfloat16 [64, 64], replicated, may hold values from -0.75 to 0.75
- w_out: float32 [64], replicated, may hold values from -0.75 to 0.75
- ghost_send: int32 [8192], P(('gx', 'gy', 'gz')), may hold values from 0 to 511
- local_first: int32 [655360], P(('gx', 'gy', 'gz')), may hold values from 0 to 511
- local_second: int32 [655360], P(('gx', 'gy', 'gz')), may hold values from 0 to 511
- local_mask: int32 [655360], P(('gx', 'gy', 'gz')), may hold values 0 or 1
- ghost_owner: int32 [393216], P(('gx', 'gy', 'gz')), may hold values from 0 to 511
- ghost_index: int32 [393216], P(('gx', 'gy', 'gz')), may hold values from 0 to 1791
- ghost_mask: int32 [393216], P(('gx', 'gy', 'gz')), may hold values 0 or 1
Outputs:
- forces: float32 [3, 16384], P(None, ('gx', 'gy', 'gz'))
- atom_energy: float32 [16384], P(('gx', 'gy', 'gz'))
Inputs may be any that keep to these rules, and one draw needn't show every extreme that they name: `ghost_send`: rows of the domain's own atoms. `local_first`: owned atoms of the domain. `local_second`: owned atoms of the domain. `ghost_owner`: owned atoms of the domain. `ghost_index`: ghost rows of the domain.
All inputs are finite; a program needn't handle non-finite values. No bound on the sum of `local_mask` or of `ghost_mask` on one device may be relied on, other than what follows from the above.
Results may differ from a plain program's by a relative error of at most 0.0085.
Values may be sent and summed in bfloat16 or wider, within the bound.
No kernel may reach another device: no remote copies, remote signals or barrier semaphores. Data moves between devices by JAX's collectives and lax.ppermute only.
A program may use at most 64 MiB of HBM per device.

v0:
```python
import math

import jax
import jax.numpy as jnp
from jax import lax
from jax.sharding import PartitionSpec as P

basis_width = 24.0
domain_edge = 1.0
ghost_offsets = ((1, 0, 0), (0, 1, 0), (0, 0, 1), (1, 1, 0), (1, 0, 1), (0, 1, 1), (1, 1, 1))
scatter_dims = (((1,), (1,)), ((), ()))


def from_behind(value, axis, steps):
    count = lax.axis_size(axis)
    pairs = [(source, (source + steps) % count) for source in range(count)]
    return lax.ppermute(value, axis, pairs)


def pair_energy(squared, left_proj, right_proj, weights, w_radial, w_mid, w_last, w_out):
    basis_count = w_radial.shape[1]
    centers = jnp.arange(basis_count, dtype=jnp.float32) / (basis_count - 1)
    radial_basis = jnp.exp(-basis_width * (squared[None, :] - centers[:, None]) ** 2)
    radial = jnp.dot(
        w_radial, radial_basis, precision=lax.Precision.HIGHEST, preferred_element_type=jnp.float32
    )
    hidden_one = jax.nn.silu(
        left_proj.astype(jnp.float32) + right_proj.astype(jnp.float32) + radial
    ).astype(jnp.bfloat16)
    hidden_two = jax.nn.silu(jnp.dot(w_mid, hidden_one, preferred_element_type=jnp.float32)).astype(
        jnp.bfloat16
    )
    hidden_three = jax.nn.silu(jnp.dot(w_last, hidden_two, preferred_element_type=jnp.float32))
    readout = jnp.dot(
        w_out, hidden_three, precision=lax.Precision.HIGHEST, preferred_element_type=jnp.float32
    )
    envelope = jnp.maximum(1.0 - squared, 0.0) ** 2
    return weights * envelope * readout


def one_hot_cols(rows_in, count):
    return rows_in[None, :] == jnp.arange(count, dtype=jnp.int32)[:, None]


def pair_terms(
    owners,
    partners,
    slot_mask,
    own_table,
    left_all,
    right_table,
    partner_table,
    w_radial,
    w_mid,
    w_last,
    w_out,
):
    total = owners.shape[0]
    own_count = own_table.shape[1]
    partner_count = partner_table.shape[1]
    block_size = math.gcd(total, 2048)
    step_count = total // block_size

    def one_block(carry, pieces):
        owner_sum, partner_sum = carry
        owner_rows, partner_rows, live = pieces
        owner_hot = one_hot_cols(owner_rows, own_count)
        partner_hot = one_hot_cols(partner_rows, partner_count)
        owner_float = owner_hot.astype(jnp.float32)
        partner_float = partner_hot.astype(jnp.float32)
        own_vals = jnp.dot(
            own_table,
            owner_float,
            precision=lax.Precision.HIGHEST,
            preferred_element_type=jnp.float32,
        )
        partner_vals = jnp.dot(
            partner_table,
            partner_float,
            precision=lax.Precision.HIGHEST,
            preferred_element_type=jnp.float32,
        )
        left_proj = jnp.dot(
            left_all, owner_hot.astype(jnp.bfloat16), preferred_element_type=jnp.float32
        ).astype(jnp.bfloat16)
        right_proj = jnp.dot(
            right_table, partner_hot.astype(jnp.bfloat16), preferred_element_type=jnp.float32
        ).astype(jnp.bfloat16)
        displace = partner_vals[:3] - own_vals[:3]
        squared = jnp.sum(displace * displace, axis=0)
        weights = live.astype(jnp.float32) * own_vals[3] * partner_vals[3]

        def energy_of(squared_in):
            return pair_energy(
                squared_in, left_proj, right_proj, weights, w_radial, w_mid, w_last, w_out
            )

        energy, pullback = jax.vjp(energy_of, squared)
        slope = pullback(jnp.ones_like(energy))[0]
        push = 2.0 * displace * slope[None, :]
        owner_vals = jnp.concatenate([push, energy[None, :]], 0)
        owner_sum = owner_sum + lax.dot_general(
            owner_vals,
            owner_float,
            scatter_dims,
            precision=lax.Precision.HIGHEST,
            preferred_element_type=jnp.float32,
        )
        partner_sum = partner_sum + lax.dot_general(
            push,
            partner_float,
            scatter_dims,
            precision=lax.Precision.HIGHEST,
            preferred_element_type=jnp.float32,
        )
        return ((owner_sum, partner_sum), None)

    start = (jnp.zeros((4, own_count), jnp.float32), jnp.zeros((3, partner_count), jnp.float32))
    pieces = (
        owners.reshape(step_count, block_size),
        partners.reshape(step_count, block_size),
        slot_mask.reshape(step_count, block_size),
    )
    sums, unused = lax.scan(one_block, start, pieces)
    return sums


def on_device(
    positions,
    features,
    species,
    species_scale,
    w_first,
    w_second,
    w_radial,
    w_mid,
    w_last,
    w_out,
    ghost_send,
    local_first,
    local_second,
    local_mask,
    ghost_owner,
    ghost_index,
    ghost_mask,
):
    own_count = positions.shape[1]
    send_count = ghost_send.shape[0]
    channels = features.shape[0]
    species_count = species_scale.shape[0]
    onehot = (species[None, :] == jnp.arange(species_count, dtype=jnp.int32)[:, None]).astype(
        species_scale.dtype
    )
    atom_gain = jnp.dot(species_scale, onehot, preferred_element_type=jnp.float32)
    coord_high = positions.astype(jnp.bfloat16)
    coord_low = (positions - coord_high.astype(jnp.float32)).astype(jnp.bfloat16)
    payload = jnp.concatenate(
        [features, coord_high, coord_low, atom_gain.astype(jnp.bfloat16)[None, :]], 0
    )
    send_hot = one_hot_cols(ghost_send, own_count)
    offered = jnp.dot(
        payload, send_hot.astype(jnp.bfloat16), preferred_element_type=jnp.float32
    ).astype(jnp.bfloat16)
    from_z = from_behind(offered, "gz", -1)
    pair_zy = from_behind(jnp.stack([offered, from_z], 1), "gy", -1)
    four_x = from_behind(jnp.stack([offered, from_z, pair_zy[:, 0], pair_zy[:, 1]], 1), "gx", -1)
    blocks = [
        four_x[:, 0],
        pair_zy[:, 0],
        from_z,
        four_x[:, 2],
        four_x[:, 1],
        pair_zy[:, 1],
        four_x[:, 3],
    ]
    own_table = jnp.concatenate([positions, atom_gain[None, :]], 0)
    left_all = jnp.dot(w_first, features, preferred_element_type=jnp.float32).astype(jnp.bfloat16)
    right_own = jnp.dot(w_second, features, preferred_element_type=jnp.float32).astype(jnp.bfloat16)
    local_owner, local_partner = pair_terms(
        local_first,
        local_second,
        local_mask,
        own_table,
        left_all,
        right_own,
        own_table,
        w_radial,
        w_mid,
        w_last,
        w_out,
    )
    ghosts = jnp.stack(blocks, 1).reshape(channels + 7, 7 * send_count)
    shifts = domain_edge * jnp.array(ghost_offsets, dtype=jnp.float32).T
    ghost_feat = ghosts[:channels]
    ghost_high = ghosts[channels : channels + 3].astype(jnp.float32)
    ghost_low = ghosts[channels + 3 : channels + 6].astype(jnp.float32)
    ghost_coords = (
        (ghost_high + ghost_low).reshape(3, 7, send_count) + shifts[:, :, None]
    ).reshape(3, 7 * send_count)
    ghost_gain = ghosts[channels + 6].astype(jnp.float32)
    ghost_table = jnp.concatenate([ghost_coords, ghost_gain[None, :]], 0)
    right_ghost = jnp.dot(w_second, ghost_feat, preferred_element_type=jnp.float32).astype(
        jnp.bfloat16
    )
    ghost_own_sum, ghost_partner = pair_terms(
        ghost_owner,
        ghost_index,
        ghost_mask,
        own_table,
        left_all,
        right_ghost,
        ghost_table,
        w_radial,
        w_mid,
        w_last,
        w_out,
    )
    atom_energy = local_owner[3] + ghost_own_sum[3]
    forces = local_owner[:3] - local_partner + ghost_own_sum[:3]
    ghost_force = -ghost_partner
    slot_forces = ghost_force.reshape(3, 7, send_count)
    upward_z = from_behind(
        jnp.stack([slot_forces[:, 2], slot_forces[:, 4], slot_forces[:, 5], slot_forces[:, 6]], 1),
        "gz",
        1,
    )
    slot_x = slot_forces[:, 0] + upward_z[:, 1]
    slot_y = slot_forces[:, 1] + upward_z[:, 2]
    slot_xy = slot_forces[:, 3] + upward_z[:, 3]
    upward_y = from_behind(jnp.stack([slot_y, slot_xy], 1), "gy", 1)
    upward_x = from_behind(slot_x + upward_y[:, 1], "gx", 1)
    incoming = upward_z[:, 0] + upward_y[:, 0] + upward_x
    forces = forces + lax.dot_general(
        incoming,
        send_hot.astype(jnp.float32),
        scatter_dims,
        precision=lax.Precision.HIGHEST,
        preferred_element_type=jnp.float32,
    )
    return (forces, atom_energy)


def solution(mesh):
    in_specs = (
        P(None, ("gx", "gy", "gz")),
        P(None, ("gx", "gy", "gz")),
        P(("gx", "gy", "gz")),
        P(),
        P(),
        P(),
        P(),
        P(),
        P(),
        P(),
        P(("gx", "gy", "gz")),
        P(("gx", "gy", "gz")),
        P(("gx", "gy", "gz")),
        P(("gx", "gy", "gz")),
        P(("gx", "gy", "gz")),
        P(("gx", "gy", "gz")),
        P(("gx", "gy", "gz")),
    )
    out_specs = (P(None, ("gx", "gy", "gz")), P(("gx", "gy", "gz")))
    return jax.shard_map(
        on_device, mesh=mesh, in_specs=in_specs, out_specs=out_specs, check_vma=False
    )
```

profile of v0, /device:TPU:0, one launch (start us, length us, event | category | flops | bytes accessed | tf_op | source)
XLA Modules:
  0.0 271.8 jit_solution(1359788345705231863)
XLA Ops:
  3.4 5.1 %collective-permute-start = (bf16[71,256]{1,0:T(8,128)(2,1)S(1)}, bf16[71,256]{1,0:T(8,128)(2,1)S(1)}, u32[]{:S(2)}, u32[]{:S(2)}) collective-permute-start(bf16[71,256]{1,0:T(8,128)(2,1)S(1)} %convolution_convert_fusion.7), channel_id=1, source_target_pairs={{0,3},{1,0},{2,1},{3,2},{4,7},{5,4},{6,5},{7,6},{8,11},{9,8},{10,9... | collective-permute-start | bytes 109064 | tf_op jit(solution)/shard_map/ppermute | solution.py:17
  8.5 1.6 collective-permute-done
  10.3 2.0 collective-permute-done.1
  12.3 1.6 collective-permute-start.2
  14.1 4.4 %collective-permute-done.2 = bf16[71,4,256]{2,0,1:T(8,128)(2,1)S(1)} collective-permute-done((bf16[71,4,256]{2,0,1:T(8,128)(2,1)S(1)}, bf16[71,4,256]{2,0,1:T(8,128)(2,1)S(1)}, u32[]{:S(2)}, u32[]{:S(2)}) %collective-permute-start.2) | collective-permute-done | bytes 145440 | tf_op jit(solution)/shard_map/ppermute | solution.py:17
  19.7 126.1 %while.27 = (s32[]{:T(128)}, f32[4,512]{1,0:T(4,128)S(1)}, f32[3,1792]{1,0:T(4,128)S(1)}, s32[6,2048]{1,0:T(8,128)S(1)}, f32[4,1792]{1,0:T(4,128)S(1)}, /*index=...) while((s32[]{:T(128)}, f32[4,512]{1,0:T(4,128)S(1)}, ...), condition=%wide.region_7.8_spmd.clone, body=%wide.region_4.7_spmd.clone.sunk | while | flops 1128016384 | bytes 8792840 | solution.py:124
  21.1 4.6 %fusion.313 = f32[4,2048]{1,0:T(4,128)S(1)} fusion(f32[4,1792]{1,0:T(4,128)S(1)} %get-tuple-element.517, s32[2048]{0:T(1024)S(1)} %bitcast.288), kind=kOutput, calls=%fused_computation.128.clone.1 | convolution fusion | flops 179830784 | bytes 69632 | tf_op jit(solution)/shard_map/while/body/eval_jaxpr/dot_general | solution.py:77
  25.7 2.6 fusion.310
  32.2 6.5 %fusion.320 = f32[3,1792]{1,0:T(4,128)S(1)} fusion(f32[3,2048]{1,0:T(4,128)S(1)} %broadcast_multiply_fusion.5, s32[2048]{0:T(1024)S(1)} %bitcast.290, f32[3,1792]{1,0:T(4,128)S(1)} %get-tuple-element.499, pred[]{:T(512)S(6)} %compare.7), kind=kOutput, calls=%fused_computation.126.clone.1 | convolution fusion | flops 135801344 | bytes 75777 | tf_op jit(solution)/shard_map/while/body/eval_jaxpr/dot_general | solution.py:109
  38.7 1.9 fusion.319
  42.1 4.6 %fusion.313 = f32[4,2048]{1,0:T(4,128)S(1)} fusion(f32[4,1792]{1,0:T(4,128)S(1)} %get-tuple-element.517, s32[2048]{0:T(1024)S(1)} %bitcast.288), kind=kOutput, calls=%fused_computation.128.clone.1 | convolution fusion | flops 179830784 | bytes 69632 | tf_op jit(solution)/shard_map/while/body/eval_jaxpr/dot_general | solution.py:77
  46.7 2.6 fusion.310
  53.2 6.5 %fusion.320 = f32[3,1792]{1,0:T(4,128)S(1)} fusion(f32[3,2048]{1,0:T(4,128)S(1)} %broadcast_multiply_fusion.5, s32[2048]{0:T(1024)S(1)} %bitcast.290, f32[3,1792]{1,0:T(4,128)S(1)} %get-tuple-element.499, pred[]{:T(512)S(6)} %compare.7), kind=kOutput, calls=%fused_computation.126.clone.1 | convolution fusion | flops 135801344 | bytes 75777 | tf_op jit(solution)/shard_map/while/body/eval_jaxpr/dot_general | solution.py:109
  59.7 1.9 fusion.319
  63.1 4.6 %fusion.313 = f32[4,2048]{1,0:T(4,128)S(1)} fusion(f32[4,1792]{1,0:T(4,128)S(1)} %get-tuple-element.517, s32[2048]{0:T(1024)S(1)} %bitcast.288), kind=kOutput, calls=%fused_computation.128.clone.1 | convolution fusion | flops 179830784 | bytes 69632 | tf_op jit(solution)/shard_map/while/body/eval_jaxpr/dot_general | solution.py:77
  67.7 2.6 fusion.310
  74.2 6.5 %fusion.320 = f32[3,1792]{1,0:T(4,128)S(1)} fusion(f32[3,2048]{1,0:T(4,128)S(1)} %broadcast_multiply_fusion.5, s32[2048]{0:T(1024)S(1)} %bitcast.290, f32[3,1792]{1,0:T(4,128)S(1)} %get-tuple-element.499, pred[]{:T(512)S(6)} %compare.7), kind=kOutput, calls=%fused_computation.126.clone.1 | convolution fusion | flops 135801344 | bytes 75777 | tf_op jit(solution)/shard_map/while/body/eval_jaxpr/dot_general | solution.py:109
  80.7 1.9 fusion.319
  84.1 4.6 %fusion.313 = f32[4,2048]{1,0:T(4,128)S(1)} fusion(f32[4,1792]{1,0:T(4,128)S(1)} %get-tuple-element.517, s32[2048]{0:T(1024)S(1)} %bitcast.288), kind=kOutput, calls=%fused_computation.128.clone.1 | convolution fusion | flops 179830784 | bytes 69632 | tf_op jit(solution)/shard_map/while/body/eval_jaxpr/dot_general | solution.py:77
  88.7 2.6 fusion.310
  95.2 6.5 %fusion.320 = f32[3,1792]{1,0:T(4,128)S(1)} fusion(f32[3,2048]{1,0:T(4,128)S(1)} %broadcast_multiply_fusion.5, s32[2048]{0:T(1024)S(1)} %bitcast.290, f32[3,1792]{1,0:T(4,128)S(1)} %get-tuple-element.499, pred[]{:T(512)S(6)} %compare.7), kind=kOutput, calls=%fused_computation.126.clone.1 | convolution fusion | flops 135801344 | bytes 75777 | tf_op jit(solution)/shard_map/while/body/eval_jaxpr/dot_general | solution.py:109
  101.7 1.9 fusion.319
  105.1 4.6 %fusion.313 = f32[4,2048]{1,0:T(4,128)S(1)} fusion(f32[4,1792]{1,0:T(4,128)S(1)} %get-tuple-element.517, s32[2048]{0:T(1024)S(1)} %bitcast.288), kind=kOutput, calls=%fused_computation.128.clone.1 | convolution fusion | flops 179830784 | bytes 69632 | tf_op jit(solution)/shard_map/while/body/eval_jaxpr/dot_general | solution.py:77
  109.7 2.6 fusion.310
  116.2 6.5 %fusion.320 = f32[3,1792]{1,0:T(4,128)S(1)} fusion(f32[3,2048]{1,0:T(4,128)S(1)} %broadcast_multiply_fusion.5, s32[2048]{0:T(1024)S(1)} %bitcast.290, f32[3,1792]{1,0:T(4,128)S(1)} %get-tuple-element.499, pred[]{:T(512)S(6)} %compare.7), kind=kOutput, calls=%fused_computation.126.clone.1 | convolution fusion | flops 135801344 | bytes 75777 | tf_op jit(solution)/shard_map/while/body/eval_jaxpr/dot_general | solution.py:109
  122.7 1.9 fusion.319
  126.1 4.6 %fusion.313 = f32[4,2048]{1,0:T(4,128)S(1)} fusion(f32[4,1792]{1,0:T(4,128)S(1)} %get-tuple-element.517, s32[2048]{0:T(1024)S(1)} %bitcast.288), kind=kOutput, calls=%fused_computation.128.clone.1 | convolution fusion | flops 179830784 | bytes 69632 | tf_op jit(solution)/shard_map/while/body/eval_jaxpr/dot_general | solution.py:77
  130.7 2.6 fusion.310
  137.2 6.5 %fusion.320 = f32[3,1792]{1,0:T(4,128)S(1)} fusion(f32[3,2048]{1,0:T(4,128)S(1)} %broadcast_multiply_fusion.5, s32[2048]{0:T(1024)S(1)} %bitcast.290, f32[3,1792]{1,0:T(4,128)S(1)} %get-tuple-element.499, pred[]{:T(512)S(6)} %compare.7), kind=kOutput, calls=%fused_computation.126.clone.1 | convolution fusion | flops 135801344 | bytes 75777 | tf_op jit(solution)/shard_map/while/body/eval_jaxpr/dot_general | solution.py:109
  143.7 1.9 fusion.319
  146.7 4.8 %collective-permute-done.3 = f32[3,4,256]{2,0,1:T(4,128)S(1)} collective-permute-done((f32[3,4,256]{2,0,1:T(4,128)S(1)}, f32[3,4,256]{2,0,1:T(4,128)S(1)}, u32[]{:S(2)}, u32[]{:S(2)}) %collective-permute-start.3) | collective-permute-done | bytes 12320 | tf_op jit(solution)/shard_map/ppermute | solution.py:17
  151.6 115.4 %while.26 = (s32[]{:T(128)}, f32[4,512]{1,0:T(4,128)S(1)}, f32[3,512]{1,0:T(4,128)S(1)}, s32[10,2048]{1,0:T(8,128)S(1)}, f32[4,512]{1,0:T(4,128)S(1)}, /*index=5...) while((s32[]{:T(128)}, f32[4,512]{1,0:T(4,128)S(1)}, ...), condition=%wide.region_3.4_spmd.clone, body=%wide.region_0.3_spmd.clone.sunk | while | flops 564399104 | bytes 8577792 | solution.py:124
  153.0 1.4 fusion.284
  159.2 1.9 fusion.291
  161.2 1.9 fusion.290
  164.6 1.4 fusion.284
  170.8 1.9 fusion.291
  172.7 1.9 fusion.290
  176.1 1.4 fusion.284
  182.3 1.9 fusion.291
  184.3 1.9 fusion.290
  187.7 1.4 fusion.284
  193.9 1.9 fusion.291
  195.8 1.9 fusion.290
  199.2 1.4 fusion.284
  205.4 1.9 fusion.291
  207.4 1.9 fusion.290
  210.7 1.4 fusion.284
  217.0 1.9 fusion.291
  218.9 1.9 fusion.290
  222.3 1.4 fusion.284
  228.5 1.9 fusion.291
  230.5 1.9 fusion.290
  233.8 1.4 fusion.284
  240.1 1.9 fusion.291
  242.0 1.9 fusion.290
  245.4 1.4 fusion.284
  251.6 1.9 fusion.291
  253.5 1.9 fusion.290
  256.9 1.4 fusion.284
  263.2 1.9 fusion.291
  265.1 1.9 fusion.290
  267.1 1.6 collective-permute-start.5
  269.3 1.5 collective-permute-done.5
  (332 shorter events, 100.5 us)
Async XLA Ops:
  0.6 18.7 %copy-start = (bf16[64,64]{1,0:T(8,128)(2,1)S(1)}, bf16[64,64]{1,0:T(8,128)(2,1)}, u32[]{:S(2)}) copy-start(bf16[64,64]{1,0:T(8,128)(2,1)} %param.27) | copy-start | bytes 24580
  0.6 13.2 %copy-start.2 = (bf16[64,512]{1,0:T(8,128)(2,1)S(1)}, bf16[64,512]{1,0:T(8,128)(2,1)}, u32[]{:S(2)}) copy-start(bf16[64,512]{1,0:T(8,128)(2,1)} %param.23) | copy-start | bytes 196612
  0.7 13.2 %copy-start.10 = (bf16[64,64]{1,0:T(8,128)(2,1)S(1)}, bf16[64,64]{1,0:T(8,128)(2,1)}, u32[]{:S(2)}) copy-start(bf16[64,64]{1,0:T(8,128)(2,1)} %param.26) | copy-start | bytes 24580
  2.3 11.8 %copy-start.6 = (s32[12288]{0:T(1024)S(1)}, s32[12288]{0:T(1024)}, u32[]{:S(2)}) copy-start(s32[12288]{0:T(1024)} %param.37) | copy-start | bytes 147460
  2.3 11.8 %copy-start.7 = (s32[12288]{0:T(1024)S(1)}, s32[12288]{0:T(1024)}, u32[]{:S(2)}) copy-start(s32[12288]{0:T(1024)} %param.36) | copy-start | bytes 147460
  3.4 10.7 %copy-start.8 = (s32[12288]{0:T(1024)S(1)}, s32[12288]{0:T(1024)}, u32[]{:S(2)}) copy-start(s32[12288]{0:T(1024)} %param.38) | copy-start | bytes 147460
  3.4 10.7 %copy-start.9 = (f32[3,512]{1,0:T(4,128)S(1)}, f32[3,512]{1,0:T(4,128)}, u32[]{:S(2)}) copy-start(f32[3,512]{1,0:T(4,128)} %param.22) | copy-start | bytes 18436
  3.4 6.7 %collective-permute-start = (bf16[71,256]{1,0:T(8,128)(2,1)S(1)}, bf16[71,256]{1,0:T(8,128)(2,1)S(1)}, u32[]{:S(2)}, u32[]{:S(2)}) collective-permute-start(bf16[71,256]{1,0:T(8,128)(2,1)S(1)} %convolution_convert_fusion.7), channel_id=1, source_target_pairs={{0,3},{1,0},{2,1},{3,2},{4,7},{5,4},{6,5},{7,6},{8,11},{9,8},{10,9... | collective-permute-start | bytes 109064 | tf_op jit(solution)/shard_map/ppermute | solution.py:17
  10.2 2.1 collective-permute-start.1
  12.3 6.2 %collective-permute-start.2 = (bf16[71,4,256]{2,0,1:T(8,128)(2,1)S(1)}, bf16[71,4,256]{2,0,1:T(8,128)(2,1)S(1)}, u32[]{:S(2)}, u32[]{:S(2)}) collective-permute-start(bf16[71,4,256]{2,0,1:T(8,128)(2,1)S(1)} %pad_maximum_fusion), channel_id=1, source_target_pairs={{0,16},{16,0},{1,17},{17,1},{2,18},{18,2},{3,19},{19,3},{4,20},{20... | collective-permute-start | bytes 436232 | tf_op jit(solution)/shard_map/ppermute | solution.py:17
  18.6 0.7 copy-start.11
  18.7 0.9 copy-start.1
  18.7 0.9 copy-start.12
  18.7 0.9 copy-start.13
  18.7 0.9 copy-start.15
  19.6 126.5 %copy-start.3 = (s32[20480]{0:T(1024)S(1)}, s32[20480]{0:T(1024)}, u32[]{:S(2)}) copy-start(s32[20480]{0:T(1024)} %param.34) | copy-start | bytes 245764
  145.7 0.9 copy-start.4
  145.8 0.9 copy-start.5
  145.8 5.7 %collective-permute-start.3 = (f32[3,4,256]{2,0,1:T(4,128)S(1)}, f32[3,4,256]{2,0,1:T(4,128)S(1)}, u32[]{:S(2)}, u32[]{:S(2)}) collective-permute-start(f32[3,4,256]{2,0,1:T(4,128)S(1)} %pad_maximum_fusion.3), channel_id=1, source_target_pairs={{0,1},{1,2},{2,3},{3,0},{4,5},{5,6},{6,7},{7,4},{8,9},{9,10},{10,1... | collective-permute-start | bytes 36872 | tf_op jit(solution)/shard_map/ppermute | solution.py:17
  151.5 115.6 %collective-permute-start.4 = (f32[3,2,256]{2,0,1:T(4,128)S(1)}, f32[3,2,256]{2,0,1:T(4,128)S(1)}, u32[]{:S(2)}, u32[]{:S(2)}) collective-permute-start(f32[3,2,256]{2,0,1:T(4,128)S(1)} %pad_maximum_fusion.5), channel_id=1, source_target_pairs={{0,4},{4,8},{8,12},{12,0},{1,5},{5,9},{9,13},{13,1},{2,6},{6,10},{... | collective-permute-start | bytes 18440 | tf_op jit(solution)/shard_map/ppermute | solution.py:17
  151.6 119.2 %copy-start.14 = (s32[256]{0:T(256)S(1)}, s32[256]{0:T(256)}, u32[]{:S(2)}) copy-start(s32[256]{0:T(256)} %param.32) | copy-start | bytes 3076
  267.1 3.7 %collective-permute-start.5 = (f32[3,256]{1,0:T(4,128)S(1)}, f32[3,256]{1,0:T(4,128)S(1)}, u32[]{:S(2)}, u32[]{:S(2)}) collective-permute-start(f32[3,256]{1,0:T(4,128)S(1)} %bitcast.299), channel_id=1, source_target_pairs={{0,16},{16,0},{1,17},{17,1},{2,18},{18,2},{3,19},{19,3},{4,20},{20... | collective-permute-start | bytes 9224 | tf_op jit(solution)/shard_map/ppermute | solution.py:17
where the time goes:
time: 272 us
  matrix products  241 us (89%)
  waiting for transfers between devices  14.4 us (5%)
  starting transfers between devices  8.57 us (3%)
  other arithmetic  3.2 us (1%)
    dot_general x16, matrix products, one_block(): lax.dot_general(push, partner_float, scatter_dims, precision=lax.Precisio...  58.3 us
    dot_general x16, matrix products, one_block(): jnp.dot(partner_table, partner_float, precision=lax.Precision.HIGHEST, pr...  41.2 us
    dot_general x16, matrix products, one_block(): lax.dot_general(owner_vals, owner_float, scatter_dims, precision=lax.Prec...  31.2 us
    dot_general x16, matrix products, one_block(): jnp.dot(right_table, partner_hot.astype(jnp.bfloat16), preferred_element_...  24 us
    dot_general x16, matrix products, one_block(): jnp.dot(own_table, owner_float, precision=lax.Precision.HIGHEST, preferre...  22.1 us
    dot_general x32, matrix products, pair_energy(): jnp.dot(w_radial, radial_basis, precision=lax.Precision.HIGHEST, preferre...  19.5 us
    dot_general x32, matrix products, pair_energy(): jnp.dot(w_mid, hidden_one, preferred_element_type=jnp.float32)  15.2 us
    ppermute x6, waiting for transfers between devices, from_behind(): return lax.ppermute(value, axis, pairs)  14.4 us
  transfers between devices with their start and end apart: 6, of which 5 were waited for; matrix products, arithmetic and copies ran while one was open for 43% of the time, Pallas kernels for 0%

commit v1 on v0

v1 whole, which is shorter than its diff:
```python
import functools
import math

import jax
import jax.numpy as jnp
from jax import lax
from jax.experimental import pallas as pl
from jax.experimental.pallas import tpu as pltpu
from jax.sharding import PartitionSpec as P

basis_width = 24.0
domain_edge = 1.0
ghost_offsets = ((1, 0, 0), (0, 1, 0), (0, 0, 1), (1, 1, 0), (1, 0, 1), (0, 1, 1), (1, 1, 1))

EXTRA = 16
GROUP = 256
LANES = 128
CHUNK = 256
VMEM_LIMIT = 48 * 1024 * 1024

NT = (((1,), (1,)), ((), ()))
f32 = jnp.float32
bf16 = jnp.bfloat16


def dot(left, right):
    return jnp.dot(left, right, preferred_element_type=f32)


def dot_nt(left, right):
    return lax.dot_general(left, right, NT, preferred_element_type=f32)


def iota(shape, dim):
    return lax.broadcasted_iota(jnp.int32, shape, dim)


def one_hot(row, count):
    return jnp.where(iota((count, row.shape[1]), 0) == row, 1.0, 0.0).astype(bf16)


def split_two(value):
    high = value.astype(bf16).astype(f32)
    return high, value - high


def coord_rows(coords, gain):
    high, low = split_two(coords)
    none = jnp.zeros((1, coords.shape[1]), f32)
    return jnp.concatenate([high, none, gain, none, none, none, low, none, none, none, none, none], 0)


def eye(count):
    return (iota((count, count), 0) == iota((count, count), 1)).astype(bf16)


def prep_kernel(
    positions_ref,
    features_ref,
    species_ref,
    scale_ref,
    w_first_ref,
    w_second_ref,
    w_radial_ref,
    w_mid_ref,
    w_last_ref,
    w_out_ref,
    send_ref,
    own_ref,
    right_ref,
    offered_ref,
    mats_ref,
    radial_ref,
    radial_t_ref,
    out_ref,
):
    channels = features_ref.shape[0]
    count = features_ref.shape[1]
    rows = channels + EXTRA
    species = species_ref[...]
    gain = jnp.zeros((1, count), f32)
    for kind in range(scale_ref.shape[1]):
        scale = scale_ref[:, kind : kind + 1].astype(f32)
        gain = jnp.where(species == kind, scale, gain)
    extra = coord_rows(positions_ref[...], gain).astype(bf16)
    left = dot(w_first_ref[...], features_ref[...]).astype(bf16).astype(f32)
    right = dot(w_second_ref[...], features_ref[...]).astype(bf16).astype(f32)
    left = (0.5 * left).astype(bf16)
    right = (0.5 * right).astype(bf16)
    groups = count // GROUP
    for group in range(groups):
        cols = slice(group * GROUP, (group + 1) * GROUP)
        own_ref[group * rows : group * rows + channels, :] = left[:, cols]
        own_ref[group * rows + channels : (group + 1) * rows, :] = extra[:, cols]
        right_ref[group * rows : group * rows + channels, :] = right[:, cols]
        right_ref[group * rows + channels : (group + 1) * rows, :] = extra[:, cols]
    send = send_ref[...]
    picked = dot(right_ref[...], one_hot(send & (GROUP - 1), GROUP))
    chosen = picked[:rows]
    for group in range(1, groups):
        chosen = jnp.where(send // GROUP == group, picked[group * rows : (group + 1) * rows], chosen)
    offered_ref[...] = chosen.astype(bf16)

    unit = eye(channels)
    mid = w_mid_ref[...].astype(f32)
    last = w_last_ref[...].astype(f32)
    mats_ref[0:channels, :] = (0.5 * mid).astype(bf16)
    mats_ref[channels : 2 * channels, :] = (0.5 * last).astype(bf16)
    mats_ref[2 * channels : 3 * channels, :] = (0.5 * dot_nt(unit, w_last_ref[...])).astype(bf16)
    mats_ref[3 * channels : 4 * channels, :] = (0.5 * dot_nt(unit, w_mid_ref[...])).astype(bf16)
    bases = w_radial_ref.shape[1]
    high, low = split_two(w_radial_ref[...])
    spread = (iota((bases, 4 * bases), 0) == iota((bases, 4 * bases), 1) % bases).astype(bf16)
    wide_high = dot(high.astype(bf16), spread)
    wide_low = dot(low.astype(bf16), spread)
    lane = iota((channels, 4 * bases), 1)
    radial_ref[...] = (0.5 * jnp.where(lane < 2 * bases, wide_high, wide_low)).astype(bf16)
    unit = eye(bases)
    radial_t_ref[0:bases, :] = dot_nt(unit, high.astype(bf16))
    radial_t_ref[bases : 2 * bases, :] = dot_nt(unit, low.astype(bf16))
    w_out = w_out_ref[...]
    diagonal = jnp.where(iota((channels, channels), 0) == iota((channels, channels), 1), w_out, 0.0)
    out_ref[...] = jnp.broadcast_to(jnp.sum(diagonal, axis=1, keepdims=True), (channels, LANES))


def group_pick(values, high, rows, groups):
    chosen = values[:rows]
    for group in range(1, groups):
        chosen = jnp.where(high == group, values[group * rows : (group + 1) * rows], chosen)
    return chosen


def spread_groups(values, high, groups):
    pieces = [jnp.where(high == group, values, 0.0) for group in range(groups)]
    if groups % 2:
        pieces.append(jnp.zeros_like(values))
    return jnp.concatenate(pieces, 0).astype(bf16)


def pair_body(
    per_step,
    own_groups,
    partner_groups,
    channels,
    bases,
    owner_ref,
    partner_ref,
    mask_ref,
    own_ref,
    right_ref,
    mats_ref,
    radial_ref,
    radial_t_ref,
    out_ref,
    own_acc,
    partner_acc,
    hot_own,
    hot_partner,
    slope_one,
    slope_two,
):
    rows = channels + EXTRA
    steps = owner_ref.shape[0] * LANES // (per_step * CHUNK)
    line = CHUNK // LANES
    w_mid = mats_ref[0:channels, :]
    w_last = mats_ref[channels : 2 * channels, :]
    w_last_t = mats_ref[2 * channels : 3 * channels, :]
    w_mid_t = mats_ref[3 * channels : 4 * channels, :]
    w_radial = radial_ref[...]
    w_radial_t = radial_t_ref[...].astype(bf16)
    w_out = jnp.concatenate([out_ref[...]] * line, 1)
    centers = iota((bases, CHUNK), 0).astype(f32) * (1.0 / (bases - 1))
    sub = iota((8, CHUNK), 0)

    def chunk(base, number):
        def row_of(ref):
            block = ref[pl.ds(base, per_step * line), :]
            return jnp.concatenate(
                [block[number * line + part : number * line + part + 1, :] for part in range(line)], 1
            )

        owner = row_of(owner_ref)
        partner = row_of(partner_ref)
        live = row_of(mask_ref).astype(f32)
        own_high = owner // GROUP
        partner_high = partner // GROUP
        hot_own[number] = one_hot(owner & (GROUP - 1), GROUP)
        hot_partner[number] = one_hot(partner & (GROUP - 1), GROUP)
        yield
        own_vals = group_pick(dot(own_ref[...], hot_own[number]), own_high, rows, own_groups)
        partner_vals = group_pick(
            dot(right_ref[...], hot_partner[number]), partner_high, rows, partner_groups
        )
        yield
        projected = own_vals[:channels] + partner_vals[:channels]
        own_coords = own_vals[channels : channels + 8] + own_vals[channels + 8 :]
        partner_coords = partner_vals[channels : channels + 8] + partner_vals[channels + 8 :]
        shift = partner_coords - own_coords
        square = shift * shift
        squared = square[0:1] + square[1:2] + square[2:3]
        weight = live * own_coords[4:5] * partner_coords[4:5]
        away = squared - centers
        basis = jnp.exp(-basis_width * (away * away))
        basis_slope = (-2.0 * basis_width) * away * basis
        basis_high, basis_low = split_two(basis)
        stacked = jnp.concatenate([basis_high, basis_low, basis_high, basis_low], 0).astype(bf16)
        radial = dot(w_radial, stacked)
        yield
        half = projected + radial
        grow = jnp.tanh(half)
        plus = 1.0 + grow
        hidden = half * plus
        slope_one[number] = plus + hidden * (1.0 - grow)
        hidden = hidden.astype(bf16)
        yield
        half = dot(w_mid, hidden)
        yield
        grow = jnp.tanh(half)
        plus = 1.0 + grow
        hidden = half * plus
        slope_two[number] = plus + hidden * (1.0 - grow)
        hidden = hidden.astype(bf16)
        yield
        half = dot(w_last, hidden)
        yield
        grow = jnp.tanh(half)
        plus = 1.0 + grow
        hidden = half * plus
        readout = jnp.sum(w_out * hidden, axis=0, keepdims=True)
        back = ((0.5 * w_out) * (plus + hidden * (1.0 - grow))).astype(bf16)
        yield
        back = dot(w_last_t, back)
        yield
        back = (back * slope_two[number]).astype(bf16)
        yield
        back = dot(w_mid_t, back)
        yield
        back = (back * slope_one[number]).astype(bf16)
        yield
        back = dot(w_radial_t, back)
        back = back[:bases] + back[bases:]
        yield
        readout_slope = jnp.sum(back * basis_slope, axis=0, keepdims=True)
        near = jnp.maximum(1.0 - squared, 0.0)
        weight_near = weight * near
        energy = weight_near * near * readout
        slope = weight_near * (near * readout_slope - 2.0 * readout)
        push = (2.0 * slope) * shift
        high, low = split_two(jnp.where(sub == 3, energy, push))
        values = jnp.concatenate([high[:4], low[:4]], 0)
        own_part = spread_groups(values, own_high, own_groups)
        partner_part = spread_groups(values, partner_high, partner_groups)
        yield
        own_acc[...] += dot_nt(own_part, hot_own[number])
        partner_acc[...] += dot_nt(partner_part, hot_partner[number])

    def step(index, unused):
        base = pl.multiple_of(index * (per_step * line), per_step * line)
        running = []
        waiting = [chunk(base, number) for number in range(per_step)]
        while running or waiting:
            if waiting:
                running.append(waiting.pop(0))
            running = [task for task in running if next(task, task) is not task]
        return unused

    lax.fori_loop(0, steps, step, 0)


def local_kernel(per_step, channels, bases, with_start, *refs):
    if with_start:
        (owner, partner, mask, own, right, mats, radial, radial_t, out, own_in, partner_in) = refs[:11]
        own_acc, partner_acc, *scratch = refs[11:]
        own_acc[...] = own_in[...]
        partner_acc[...] = partner_in[...]
    else:
        (owner, partner, mask, own, right, mats, radial, radial_t, out) = refs[:9]
        own_acc, partner_acc, *scratch = refs[9:]
        own_acc[...] = jnp.zeros_like(own_acc)
        partner_acc[...] = jnp.zeros_like(partner_acc)
    groups = own.shape[0] // (channels + EXTRA)
    pair_body(
        per_step,
        groups,
        groups,
        channels,
        bases,
        owner,
        partner,
        mask,
        own,
        right,
        mats,
        radial,
        radial_t,
        out,
        own_acc,
        partner_acc,
        *scratch,
    )


def ghost_kernel(per_step, channels, bases, *refs):
    blocks = len(ghost_offsets)
    (owner, partner, mask, own, mats, radial, radial_t, out, own_in) = refs[:9]
    arrived = refs[9 : 9 + blocks]
    own_acc = refs[9 + blocks]
    forces = refs[10 + blocks : 10 + 2 * blocks]
    table, partner_acc, *scratch = refs[10 + 2 * blocks :]
    rows = channels + EXTRA
    groups = own.shape[0] // rows
    own_acc[...] = own_in[...]
    partner_acc[...] = jnp.zeros_like(partner_acc)
    for block, offset in enumerate(ghost_offsets):
        start = block * rows
        table[start : start + channels, :] = arrived[block][0:channels, :]
        extra = arrived[block][channels:rows, :].astype(f32)
        coords = extra[0:8] + extra[8:16]
        moved = jnp.concatenate(
            [coords[axis : axis + 1] + domain_edge * offset[axis] for axis in range(3)], 0
        )
        table[start + channels : start + rows, :] = coord_rows(moved, coords[4:5]).astype(bf16)
    pair_body(
        per_step,
        groups,
        blocks,
        channels,
        bases,
        owner,
        partner,
        mask,
        own,
        table,
        mats,
        radial,
        radial_t,
        out,
        own_acc,
        partner_acc,
        *scratch,
    )
    for block in range(blocks):
        part = partner_acc[block * 8 : block * 8 + 8, :]
        forces[block][...] = -(part + jnp.concatenate([part[4:], part[:4]], 0))


def final_kernel(blocks, *refs):
    own_ref, partner_ref, send_ref = refs[:3]
    arrived = refs[3 : 3 + blocks]
    forces_ref, energy_ref = refs[3 + blocks :]
    incoming = arrived[0][...]
    for block in range(1, blocks):
        incoming = incoming + arrived[block][...]
    high, low = split_two(incoming)
    send = send_ref[...]
    groups = own_ref.shape[0] // 8
    values = spread_groups(jnp.concatenate([high[:4], low[:4]], 0), send // GROUP, groups)
    back = dot_nt(values, one_hot(send & (GROUP - 1), GROUP))
    for group in range(groups):
        part = slice(group * 8, group * 8 + 8)
        total = own_ref[part, :] - partner_ref[part, :] + back[part]
        total = total[:4] + total[4:]
        cols = slice(group * GROUP, (group + 1) * GROUP)
        forces_ref[:, cols] = total[:3]
        energy = own_ref[group * 8 + 3 : group * 8 + 4, :] + own_ref[group * 8 + 7 : group * 8 + 8, :]
        energy_ref[:, cols] = energy


def whole(shape, dtype):
    return jax.ShapeDtypeStruct(shape, dtype)


def call(kernel, outs, name, scratch=(), specs=None, cost=None):
    more = {} if specs is None else dict(in_specs=specs, grid=(1,))
    if cost is not None:
        more["cost_estimate"] = cost
    return pl.pallas_call(
        kernel,
        out_shape=outs,
        scratch_shapes=list(scratch),
        compiler_params=pltpu.CompilerParams(vmem_limit_bytes=VMEM_LIMIT),
        name=name,
        **more,
    )


def shifted(value, offset, sizes, sign):
    names = ("gx", "gy", "gz")
    used = tuple(name for name, step in zip(names, offset) if step)
    dims = [sizes[name] for name in used]
    pairs = []
    for flat in range(math.prod(dims)):
        place, rest = [], flat
        for size in reversed(dims):
            place.insert(0, rest % size)
            rest //= size
        target = 0
        for at, size in zip(place, dims):
            target = target * size + (at - sign) % size
        pairs.append((flat, target))
    return lax.ppermute(value, used, pairs)


def on_device(
    sizes,
    positions,
    features,
    species,
    species_scale,
    w_first,
    w_second,
    w_radial,
    w_mid,
    w_last,
    w_out,
    ghost_send,
    local_first,
    local_second,
    local_mask,
    ghost_owner,
    ghost_index,
    ghost_mask,
):
    channels, own_count = features.shape
    send_count = ghost_send.shape[0]
    bases = w_radial.shape[1]
    rows = channels + EXTRA
    groups = own_count // GROUP
    blocks = len(ghost_offsets)
    send = ghost_send.reshape(1, send_count)
    own, right, offered, mats, radial, radial_t, out = call(
        prep_kernel,
        (
            whole((groups * rows, GROUP), bf16),
            whole((groups * rows, GROUP), bf16),
            whole((rows, send_count), bf16),
            whole((4 * channels, channels), bf16),
            whole((channels, 4 * bases), bf16),
            whole((2 * bases, channels), f32),
            whole((channels, LANES), f32),
        ),
        "tables",
    )(
        positions,
        features,
        species.reshape(1, own_count),
        species_scale.reshape(1, species_scale.shape[0]),
        w_first,
        w_second,
        w_radial,
        w_mid,
        w_last,
        w_out.reshape(1, channels),
        send,
    )
    arrived = [shifted(offered, offset, sizes, 1) for offset in ghost_offsets]

    def tiles(value):
        return value.reshape(value.shape[0] // LANES, LANES)

    per_step = 8

    def scratch(partner_groups):
        return [
            pltpu.VMEM((per_step, GROUP, CHUNK), bf16),
            pltpu.VMEM((per_step, GROUP, CHUNK), bf16),
            pltpu.VMEM((per_step, channels, CHUNK), f32),
            pltpu.VMEM((per_step, channels, CHUNK), f32),
        ]

    def cost(slots):
        return pl.CostEstimate(
            flops=slots * 400000, bytes_accessed=slots * 12, transcendentals=slots * 200
        )

    local = [tiles(value) for value in (local_first, local_second, local_mask)]
    parts = 2
    part_rows = local[0].shape[0] // parts
    weights = (mats, radial, radial_t, out)
    whole_spec = pl.BlockSpec(memory_space=pltpu.VMEM)

    def local_call(part, start):
        cut = pl.BlockSpec((part_rows, LANES), lambda step: (part, 0))
        operands = [*local, own, right, *weights, *start]
        return call(
            functools.partial(local_kernel, per_step, channels, bases, bool(start)),
            (whole((groups * 8, GROUP), f32), whole((groups * 8, GROUP), f32)),
            "local_pairs",
            scratch(groups),
            [cut] * 3 + [whole_spec] * (len(operands) - 3),
            cost(part_rows * LANES),
        )(*operands)

    own_sum, partner_sum = local_call(0, ())
    own_sum, *ghost_forces = call(
        functools.partial(ghost_kernel, per_step, channels, bases),
        (whole((groups * 8, GROUP), f32),) + (whole((8, send_count), f32),) * blocks,
        "ghost_pairs",
        [pltpu.VMEM((blocks * rows, GROUP), bf16), pltpu.VMEM(((blocks + blocks % 2) * 8, GROUP), f32)]
        + scratch(blocks),
        None,
        cost(ghost_owner.shape[0]),
    )(*[tiles(value) for value in (ghost_owner, ghost_index, ghost_mask)], own, *weights, own_sum, *arrived)
    returned = [
        shifted(force, offset, sizes, -1) for force, offset in zip(ghost_forces, ghost_offsets)
    ]
    own_sum, partner_sum = local_call(1, (own_sum, partner_sum))
    forces, energy = call(
        functools.partial(final_kernel, blocks),
        (whole((3, own_count), f32), whole((1, own_count), f32)),
        "totals",
    )(own_sum, partner_sum, send, *returned)
    return forces, energy.reshape(own_count)


def solution(mesh):
    names = ("gx", "gy", "gz")
    sizes = {name: mesh.shape[name] for name in names}
    split = P(names)
    cols = P(None, names)
    in_specs = (
        (cols, cols, split) + (P(),) * 7 + (split,) * 7
    )
    return jax.shard_map(
        functools.partial(on_device, sizes),
        mesh=mesh,
        in_specs=in_specs,
        out_specs=(cols, split),
        check_vma=False,
    )
```

time: 272 us -> 80.5 us (0.30)
  matrix products: 241 us -> 0 us
  Pallas kernels: 0 us -> 53.8 us
  waiting for transfers between devices: 14.4 us -> 0.42 us
  starting transfers between devices: 8.57 us -> 19.7 us
  local copies, waits for them, and re-layouts: 1.99 us -> 5.29 us
  other arithmetic: 3.2 us -> 0 us
    dot_general x198 -> x0, matrix products: 241 us -> none  [the longest x16 58.3 us: one_block(): lax.dot_general(push, partner_float, scatter_dims, precision=lax.Precisio...]
    pallas_call x0 -> x5, Pallas kernels: none -> 53.8 us  [the longest x2 29.7 us: local_call(): call(functools.partial(local_kernel, per_step, channels, bases, bool(star...]
    ppermute x6 -> x14, waiting for transfers between devices: 14.4 us -> 0.42 us  [shifted(): return lax.ppermute(value, used, pairs)]
    ppermute x6 -> x14, starting transfers between devices: 8.57 us -> 19.7 us  [shifted(): return lax.ppermute(value, used, pairs)]
    unnamed x40 -> x35, local copies, waits for them, and re-layouts: 1.17 us -> 5.29 us
  transfers between devices with their start and end apart: 6 -> 14, of which waited for: 5 -> 1; matrix products, arithmetic and copies ran while one was open for 43% -> 0% of each run, Pallas kernels for 0% -> 37%
where the time goes in v1:
time: 80.5 us; the launch traced here: 80.1 us
  Pallas kernels  53.8 us (67%)
  starting transfers between devices  19.7 us (24%)
  local copies, waits for them, and re-layouts  5.29 us (7%)
  between operations  0.83 us (1%)
    pallas_call x2, Pallas kernels, local_call(): call(functools.partial(local_kernel, per_step, channels, bases, bool(star...  29.7 us
    pallas_call x1, Pallas kernels, on_device(): call(functools.partial(ghost_kernel, per_step, channels, bases), (whole((...  23 us
    ppermute x14, starting transfers between devices, shifted(): return lax.ppermute(value, used, pairs)  19.7 us
    unnamed x35, local copies, waits for them, and re-layouts  5.29 us
  transfers between devices with their start and end apart: 14, of which 1 were waited for; matrix products, arithmetic and copies ran while one was open for 0% of the time, Pallas kernels for 37%

profile of v1, /device:TPU:0, one launch (start us, length us, event | category | flops | bytes accessed | tf_op | source)
XLA Modules:
  0.0 80.1 jit_solution(14549874815219830726)
XLA Ops:
  0.6 0.0 copy-start.2
  0.6 0.0 copy-start.1
  0.7 0.0 copy-start.5
  0.7 0.8 copy.19.w_radial_ref
  1.4 0.0 copy-start.7
  1.5 0.0 copy-start.6
  1.5 0.0 copy-start.8
  1.5 0.0 copy-done.2
  1.5 0.0 copy-done.1
  1.5 0.0 copy-done.5
  1.5 0.6 copy-done.7
  2.1 0.0 copy-done.6
  2.1 0.0 copy-done.8
  2.1 0.8 %copy-done = bf16[64,512]{1,0:T(8,128)(2,1)S(1)} copy-done((bf16[64,512]{1,0:T(8,128)(2,1)S(1)}, bf16[64,512]{1,0:T(8,128)(2,1)}, u32[]{:S(2)}) %copy-start) | copy-done | bytes 65560
  3.0 0.0 copy-start.3
  3.0 0.7 copy-done.3
  3.7 0.0 copy-start.4
  3.7 0.7 copy-done.4
  4.4 0.0 copy-start.9
  4.4 0.7 copy-done.9
  5.1 0.0 copy-start.10
  5.1 0.0 copy-start.11
  5.1 0.3 tables.1
  5.4 6.4 %collective-permute-start.6 = (bf16[80,256]{1,0:T(8,128)(2,1)S(1)}, bf16[80,256]{1,0:T(8,128)(2,1)S(1)}, u32[]{:S(2)}, u32[]{:S(2)}) collective-permute-start(bf16[80,256]{1,0:T(8,128)(2,1)S(1)} %get-tuple-element.30), channel_id=1, source_target_pairs={{0,31},{1,28},{2,29},{3,30},{4,19},{5,16},{6,17},{7,18},{8,23},{9,... | collective-permute-start | bytes 122888 | tf_op jit(solution)/shard_map/ppermute | solution.py:401
  11.8 0.7 collective-permute-start.5
  12.6 0.4 collective-permute-start.4
  13.0 0.8 collective-permute-start.3
  13.7 0.4 collective-permute-start.2
  14.2 0.0 collective-permute-done.6.refs_15_
  14.2 0.7 collective-permute-start.1
  14.9 0.4 collective-permute-done.5.refs_14_
  15.3 0.5 collective-permute-start
  15.8 0.0 copy-done.10
  15.8 0.0 copy-done.11
  15.8 0.0 copy-start.12
  15.8 0.9 %copy-done.12 = s32[20480]{0:T(1024)S(1)} copy-done((s32[20480]{0:T(1024)S(1)}, s32[20480]{0:T(1024)}, u32[]{:S(2)}) %copy-start.12) | copy-done | bytes 81944
  16.7 14.9 %local_pairs.2 = (f32[16,256]{1,0:T(8,128)S(1)}, f32[16,256]{1,0:T(8,128)S(1)}) custom-call(s32[160,128]{1,0:T(8,128)S(1)} %bitcast.16, s32[160,128]{1,0:T(8,128)S(1)} %bitcast.18, s32[160,128]{1,0:T(8,128)S(1)} %bitcast.20, bf16[160,256]{1,0:T(8,128)(2,1)S(1)} %get-tuple-element.23.refs_3_, bf16[160,256]{1,0:T(8,128)(2,1)S(1)} %get-tuple-element.24.refs_4_, ...), custom_call_target="tpu_custom_call" | custom-call | flops 4096000000 | bytes 122880 | tf_op jit(solution)/shard_map/local_pairs/pallas_call | solution.py:485
  31.6 0.0 collective-permute-done.4.refs_13_
  31.6 0.0 collective-permute-done.3.refs_12_
  31.6 0.0 collective-permute-done.2.refs_11_
  31.6 0.0 collective-permute-done.1.refs_10_
  31.6 0.0 collective-permute-done.refs_9_
  31.6 0.0 copy-done.14
  31.6 0.0 copy-done.15
  31.6 0.0 copy-done.16
  31.6 0.0 copy-start.13
  31.6 23.0 %ghost_pairs.1 = (f32[16,256]{1,0:T(8,128)S(1)}, f32[8,256]{1,0:T(8,128)S(1)}, f32[8,256]{1,0:T(8,128)S(1)}, f32[8,256]{1,0:T(8,128)S(1)}, f32[8,256]{1,0:T(8,12...) custom-call(s32[96,128]{1,0:T(8,128)S(1)} %bitcast.22, s32[96,128]{1,0:T(8,128)S(1)} %bitcast.23, ...), custom_call_target="tpu_custom_call" | custom-call | flops 4915200000 | bytes 147456 | tf_op jit(solution)/shard_map/ghost_pairs/pallas_call | solution.py:495
  54.6 1.6 %collective-permute-start.7 = (f32[8,256]{1,0:T(8,128)S(1)}, f32[8,256]{1,0:T(8,128)S(1)}, u32[]{:S(2)}, u32[]{:S(2)}) collective-permute-start(f32[8,256]{1,0:T(8,128)S(1)} %get-tuple-element.35), channel_id=1, source_target_pairs={{0,16},{16,0},{1,17},{17,1},{2,18},{18,2},{3,19},{19,3},{4,20},{20... | collective-permute-start | bytes 24584 | tf_op jit(solution)/shard_map/ppermute | solution.py:401
  56.2 0.1 collective-permute-start.8
  56.2 1.1 %collective-permute-start.9 = (f32[8,256]{1,0:T(8,128)S(1)}, f32[8,256]{1,0:T(8,128)S(1)}, u32[]{:S(2)}, u32[]{:S(2)}) collective-permute-start(f32[8,256]{1,0:T(8,128)S(1)} %get-tuple-element.37), channel_id=1, source_target_pairs={{0,1},{1,2},{2,3},{3,0},{4,5},{5,6},{6,7},{7,4},{8,9},{9,10},{10,1... | collective-permute-start | bytes 24584 | tf_op jit(solution)/shard_map/ppermute | solution.py:401
  57.4 1.5 %collective-permute-start.10 = (f32[8,256]{1,0:T(8,128)S(1)}, f32[8,256]{1,0:T(8,128)S(1)}, u32[]{:S(2)}, u32[]{:S(2)}) collective-permute-start(f32[8,256]{1,0:T(8,128)S(1)} %get-tuple-element.38), channel_id=1, source_target_pairs={{0,20},{4,24},{8,28},{12,16},{16,4},{20,8},{24,12},{28,0},{1,21},{... | collective-permute-start | bytes 24584 | tf_op jit(solution)/shard_map/ppermute | solution.py:401
  58.9 2.5 %collective-permute-start.11 = (f32[8,256]{1,0:T(8,128)S(1)}, f32[8,256]{1,0:T(8,128)S(1)}, u32[]{:S(2)}, u32[]{:S(2)}) collective-permute-start(f32[8,256]{1,0:T(8,128)S(1)} %get-tuple-element.39), channel_id=1, source_target_pairs={{0,17},{1,18},{2,19},{3,16},{16,1},{17,2},{18,3},{19,0},{4,21},{5,... | collective-permute-start | bytes 24584 | tf_op jit(solution)/shard_map/ppermute | solution.py:401
  61.4 0.0 collective-permute-done.7.refs_3_
  61.4 1.0 %collective-permute-start.12 = (f32[8,256]{1,0:T(8,128)S(1)}, f32[8,256]{1,0:T(8,128)S(1)}, u32[]{:S(2)}, u32[]{:S(2)}) collective-permute-start(f32[8,256]{1,0:T(8,128)S(1)} %get-tuple-element.40), channel_id=1, source_target_pairs={{0,5},{1,6},{2,7},{3,4},{4,9},{5,10},{6,11},{7,8},{8,13},{9,14},{1... | collective-permute-start | bytes 24584 | tf_op jit(solution)/shard_map/ppermute | solution.py:401
  62.4 0.0 collective-permute-done.8.refs_4_
  62.4 2.0 %collective-permute-start.13 = (f32[8,256]{1,0:T(8,128)S(1)}, f32[8,256]{1,0:T(8,128)S(1)}, u32[]{:S(2)}, u32[]{:S(2)}) collective-permute-start(f32[8,256]{1,0:T(8,128)S(1)} %get-tuple-element.41), channel_id=1, source_target_pairs={{0,21},{1,22},{2,23},{3,20},{4,25},{5,26},{6,27},{7,24},{8,29},{9,... | collective-permute-start | bytes 24584 | tf_op jit(solution)/shard_map/ppermute | solution.py:401
  64.4 0.0 copy-done.13
  64.4 14.8 %local_pairs.3 = (f32[16,256]{1,0:T(8,128)S(1)}, f32[16,256]{1,0:T(8,128)S(1)}) custom-call(s32[160,128]{1,0:T(8,128)S(1)} %bitcast.17, s32[160,128]{1,0:T(8,128)S(1)} %bitcast.19, s32[160,128]{1,0:T(8,128)S(1)} %bitcast.21, bf16[160,256]{1,0:T(8,128)(2,1)S(1)} %get-tuple-element.23.refs_3_, bf16[160,256]{1,0:T(8,128)(2,1)S(1)} %get-tuple-element.24.refs_4_, ...), custom_call_target="tpu_custom_call" | custom-call | flops 4096000000 | bytes 122880 | tf_op jit(solution)/shard_map/local_pairs/pallas_call | solution.py:485
  79.2 0.0 collective-permute-done.9.refs_5_
  79.2 0.0 collective-permute-done.10.refs_6_
  79.2 0.0 collective-permute-done.11.refs_7_
  79.2 0.0 collective-permute-done.12.refs_8_
  79.2 0.0 collective-permute-done.13.refs_9_
  79.3 0.8 %totals.1 = (f32[3,512]{1,0:T(4,128)}, f32[1,512]{1,0:T(1,128)}) custom-call(f32[16,256]{1,0:T(8,128)S(1)} %get-tuple-element.33.refs_0_, f32[16,256]{1,0:T(8,128)S(1)} %get-tuple-element.34.refs_1_, s32[1,256]{1,0:T(1,128)S(1)} %bitcast.12, f32[8,256]{1,0:T(8,128)S(1)} %collective-permute-done.7.refs_3_, f32[8,256]{1,0:T(8,128)S(1)} %collective-permute-done.8.refs_4_, ...), custom_call_target="tpu_custom_call" | custom-call | tf_op jit(solution)/shard_map/totals/pallas_call | solution.py:508
  (4 shorter events, 0.0 us)
Async XLA Ops:
  0.6 0.8 %copy-start.2 = (bf16[64,64]{1,0:T(8,128)(2,1)S(1)}, bf16[64,64]{1,0:T(8,128)(2,1)}, u32[]{:S(2)}) copy-start(bf16[64,64]{1,0:T(8,128)(2,1)} %w_second_ref.1) | copy-start | bytes 24580
  0.6 0.8 %copy-start.1 = (bf16[64,64]{1,0:T(8,128)(2,1)S(1)}, bf16[64,64]{1,0:T(8,128)(2,1)}, u32[]{:S(2)}) copy-start(bf16[64,64]{1,0:T(8,128)(2,1)} %w_first_ref.1) | copy-start | bytes 24580
  0.7 0.8 %copy-start.5 = (f32[3,512]{1,0:T(4,128)S(1)}, f32[3,512]{1,0:T(4,128)}, u32[]{:S(2)}) copy-start(f32[3,512]{1,0:T(4,128)} %positions_ref.1) | copy-start | bytes 18436
  1.4 0.7 copy-start.7
  1.5 0.7 copy-start.6
  1.5 0.7 copy-start.8
  2.1 0.8 %copy-start = (bf16[64,512]{1,0:T(8,128)(2,1)S(1)}, bf16[64,512]{1,0:T(8,128)(2,1)}, u32[]{:S(2)}) copy-start(bf16[64,512]{1,0:T(8,128)(2,1)} %features_ref.1) | copy-start | bytes 196612
  3.0 0.7 copy-start.3
  3.7 0.7 copy-start.4
  4.4 0.7 copy-start.9
  5.1 10.7 %copy-start.10 = (s32[20480]{0:T(1024)S(1)}, s32[20480]{0:T(1024)}, u32[]{:S(2)}) copy-start(s32[20480]{0:T(1024)} %param.28) | copy-start | bytes 245764
  5.1 10.7 %copy-start.11 = (s32[20480]{0:T(1024)S(1)}, s32[20480]{0:T(1024)}, u32[]{:S(2)}) copy-start(s32[20480]{0:T(1024)} %param.29) | copy-start | bytes 245764
  5.4 8.8 %collective-permute-start.6 = (bf16[80,256]{1,0:T(8,128)(2,1)S(1)}, bf16[80,256]{1,0:T(8,128)(2,1)S(1)}, u32[]{:S(2)}, u32[]{:S(2)}) collective-permute-start(bf16[80,256]{1,0:T(8,128)(2,1)S(1)} %get-tuple-element.30), channel_id=1, source_target_pairs={{0,31},{1,28},{2,29},{3,30},{4,19},{5,16},{6,17},{7,18},{8,23},{9,... | collective-permute-start | bytes 122888 | tf_op jit(solution)/shard_map/ppermute | solution.py:401
  11.8 3.4 %collective-permute-start.5 = (bf16[80,256]{1,0:T(8,128)(2,1)S(1)}, bf16[80,256]{1,0:T(8,128)(2,1)S(1)}, u32[]{:S(2)}, u32[]{:S(2)}) collective-permute-start(bf16[80,256]{1,0:T(8,128)(2,1)S(1)} %get-tuple-element.30), channel_id=1, source_target_pairs={{0,15},{1,12},{2,13},{3,14},{4,3},{5,0},{6,1},{7,2},{8,7},{9,4},{1... | collective-permute-start | bytes 122888 | tf_op jit(solution)/shard_map/ppermute | solution.py:401
  12.6 19.0 %collective-permute-start.4 = (bf16[80,256]{1,0:T(8,128)(2,1)S(1)}, bf16[80,256]{1,0:T(8,128)(2,1)S(1)}, u32[]{:S(2)}, u32[]{:S(2)}) collective-permute-start(bf16[80,256]{1,0:T(8,128)(2,1)S(1)} %get-tuple-element.30), channel_id=1, source_target_pairs={{0,19},{1,16},{2,17},{3,18},{16,3},{17,0},{18,1},{19,2},{4,23},{5,... | collective-permute-start | bytes 122888 | tf_op jit(solution)/shard_map/ppermute | solution.py:401
  13.0 18.6 %collective-permute-start.3 = (bf16[80,256]{1,0:T(8,128)(2,1)S(1)}, bf16[80,256]{1,0:T(8,128)(2,1)S(1)}, u32[]{:S(2)}, u32[]{:S(2)}) collective-permute-start(bf16[80,256]{1,0:T(8,128)(2,1)S(1)} %get-tuple-element.30), channel_id=1, source_target_pairs={{0,28},{4,16},{8,20},{12,24},{16,12},{20,0},{24,4},{28,8},{1,29},{... | collective-permute-start | bytes 122888 | tf_op jit(solution)/shard_map/ppermute | solution.py:401
  13.7 17.8 %collective-permute-start.2 = (bf16[80,256]{1,0:T(8,128)(2,1)S(1)}, bf16[80,256]{1,0:T(8,128)(2,1)S(1)}, u32[]{:S(2)}, u32[]{:S(2)}) collective-permute-start(bf16[80,256]{1,0:T(8,128)(2,1)S(1)} %get-tuple-element.30), channel_id=1, source_target_pairs={{0,3},{1,0},{2,1},{3,2},{4,7},{5,4},{6,5},{7,6},{8,11},{9,8},{10,9... | collective-permute-start | bytes 122888 | tf_op jit(solution)/shard_map/ppermute | solution.py:401
  14.2 17.4 %collective-permute-start.1 = (bf16[80,256]{1,0:T(8,128)(2,1)S(1)}, bf16[80,256]{1,0:T(8,128)(2,1)S(1)}, u32[]{:S(2)}, u32[]{:S(2)}) collective-permute-start(bf16[80,256]{1,0:T(8,128)(2,1)S(1)} %get-tuple-element.30), channel_id=1, source_target_pairs={{0,12},{4,0},{8,4},{12,8},{1,13},{5,1},{9,5},{13,9},{2,14},{6,2},{... | collective-permute-start | bytes 122888 | tf_op jit(solution)/shard_map/ppermute | solution.py:401
  15.3 16.3 %collective-permute-start = (bf16[80,256]{1,0:T(8,128)(2,1)S(1)}, bf16[80,256]{1,0:T(8,128)(2,1)S(1)}, u32[]{:S(2)}, u32[]{:S(2)}) collective-permute-start(bf16[80,256]{1,0:T(8,128)(2,1)S(1)} %get-tuple-element.30), channel_id=1, source_target_pairs={{0,16},{16,0},{1,17},{17,1},{2,18},{18,2},{3,19},{19,3},{4,20},{20... | collective-permute-start | bytes 122888 | tf_op jit(solution)/shard_map/ppermute | solution.py:401
  15.8 0.9 %copy-start.12 = (s32[20480]{0:T(1024)S(1)}, s32[20480]{0:T(1024)}, u32[]{:S(2)}) copy-start(s32[20480]{0:T(1024)} %param.30) | copy-start | bytes 245764
  16.7 14.9 %copy-start.14 = (s32[12288]{0:T(1024)S(1)}, s32[12288]{0:T(1024)}, u32[]{:S(2)}) copy-start(s32[12288]{0:T(1024)} %param.31) | copy-start | bytes 147460
  16.7 14.9 %copy-start.15 = (s32[12288]{0:T(1024)S(1)}, s32[12288]{0:T(1024)}, u32[]{:S(2)}) copy-start(s32[12288]{0:T(1024)} %param.32) | copy-start | bytes 147460
  16.7 14.9 %copy-start.16 = (s32[12288]{0:T(1024)S(1)}, s32[12288]{0:T(1024)}, u32[]{:S(2)}) copy-start(s32[12288]{0:T(1024)} %param.33) | copy-start | bytes 147460
  31.6 32.7 %copy-start.13 = (s32[20480]{0:T(1024)S(1)}, s32[20480]{0:T(1024)}, u32[]{:S(2)}) copy-start(s32[20480]{0:T(1024)} %param.30) | copy-start | bytes 245764
  54.6 6.7 %collective-permute-start.7 = (f32[8,256]{1,0:T(8,128)S(1)}, f32[8,256]{1,0:T(8,128)S(1)}, u32[]{:S(2)}, u32[]{:S(2)}) collective-permute-start(f32[8,256]{1,0:T(8,128)S(1)} %get-tuple-element.35), channel_id=1, source_target_pairs={{0,16},{16,0},{1,17},{17,1},{2,18},{18,2},{3,19},{19,3},{4,20},{20... | collective-permute-start | bytes 24584 | tf_op jit(solution)/shard_map/ppermute | solution.py:401
  56.2 6.2 %collective-permute-start.8 = (f32[8,256]{1,0:T(8,128)S(1)}, f32[8,256]{1,0:T(8,128)S(1)}, u32[]{:S(2)}, u32[]{:S(2)}) collective-permute-start(f32[8,256]{1,0:T(8,128)S(1)} %get-tuple-element.36), channel_id=1, source_target_pairs={{0,4},{4,8},{8,12},{12,0},{1,5},{5,9},{9,13},{13,1},{2,6},{6,10},{... | collective-permute-start | bytes 24584 | tf_op jit(solution)/shard_map/ppermute | solution.py:401
  56.2 23.0 %collective-permute-start.9 = (f32[8,256]{1,0:T(8,128)S(1)}, f32[8,256]{1,0:T(8,128)S(1)}, u32[]{:S(2)}, u32[]{:S(2)}) collective-permute-start(f32[8,256]{1,0:T(8,128)S(1)} %get-tuple-element.37), channel_id=1, source_target_pairs={{0,1},{1,2},{2,3},{3,0},{4,5},{5,6},{6,7},{7,4},{8,9},{9,10},{10,1... | collective-permute-start | bytes 24584 | tf_op jit(solution)/shard_map/ppermute | solution.py:401
  57.4 21.8 %collective-permute-start.10 = (f32[8,256]{1,0:T(8,128)S(1)}, f32[8,256]{1,0:T(8,128)S(1)}, u32[]{:S(2)}, u32[]{:S(2)}) collective-permute-start(f32[8,256]{1,0:T(8,128)S(1)} %get-tuple-element.38), channel_id=1, source_target_pairs={{0,20},{4,24},{8,28},{12,16},{16,4},{20,8},{24,12},{28,0},{1,21},{... | collective-permute-start | bytes 24584 | tf_op jit(solution)/shard_map/ppermute | solution.py:401
  58.9 20.4 %collective-permute-start.11 = (f32[8,256]{1,0:T(8,128)S(1)}, f32[8,256]{1,0:T(8,128)S(1)}, u32[]{:S(2)}, u32[]{:S(2)}) collective-permute-start(f32[8,256]{1,0:T(8,128)S(1)} %get-tuple-element.39), channel_id=1, source_target_pairs={{0,17},{1,18},{2,19},{3,16},{16,1},{17,2},{18,3},{19,0},{4,21},{5,... | collective-permute-start | bytes 24584 | tf_op jit(solution)/shard_map/ppermute | solution.py:401
  61.4 17.9 %collective-permute-start.12 = (f32[8,256]{1,0:T(8,128)S(1)}, f32[8,256]{1,0:T(8,128)S(1)}, u32[]{:S(2)}, u32[]{:S(2)}) collective-permute-start(f32[8,256]{1,0:T(8,128)S(1)} %get-tuple-element.40), channel_id=1, source_target_pairs={{0,5},{1,6},{2,7},{3,4},{4,9},{5,10},{6,11},{7,8},{8,13},{9,14},{1... | collective-permute-start | bytes 24584 | tf_op jit(solution)/shard_map/ppermute | solution.py:401
  62.4 16.9 %collective-permute-start.13 = (f32[8,256]{1,0:T(8,128)S(1)}, f32[8,256]{1,0:T(8,128)S(1)}, u32[]{:S(2)}, u32[]{:S(2)}) collective-permute-start(f32[8,256]{1,0:T(8,128)S(1)} %get-tuple-element.41), channel_id=1, source_target_pairs={{0,21},{1,22},{2,23},{3,20},{4,25},{5,26},{6,27},{7,24},{8,29},{9,... | collective-permute-start | bytes 24584 | tf_op jit(solution)/shard_map/ppermute | solution.py:401

commit v2 on v1

v2 whole, which is shorter than its diff:
```python
import functools
import math

import jax
import jax.numpy as jnp
from jax import lax
from jax.experimental import pallas as pl
from jax.experimental.pallas import tpu as pltpu
from jax.sharding import PartitionSpec as P

basis_width = 24.0
domain_edge = 1.0
ghost_offsets = ((1, 0, 0), (0, 1, 0), (0, 0, 1), (1, 1, 0), (1, 0, 1), (0, 1, 1), (1, 1, 1))

EXTRA = 16
GROUP = 256
LANES = 128
CHUNK = 256
QUAD = 4
VMEM_LIMIT = 48 * 1024 * 1024

NT = (((1,), (1,)), ((), ()))
f32 = jnp.float32
bf16 = jnp.bfloat16


def dot(left, right):
    return jnp.dot(left, right, preferred_element_type=f32)


def dot_nt(left, right):
    return lax.dot_general(left, right, NT, preferred_element_type=f32)


def iota(shape, dim):
    return lax.broadcasted_iota(jnp.int32, shape, dim)


def one_hot(row, count):
    return jnp.where(iota((count, row.shape[1]), 0) == row, 1.0, 0.0).astype(bf16)


def split_two(value):
    high = value.astype(bf16).astype(f32)
    return high, value - high


def coord_rows(coords, gain):
    high, low = split_two(coords)
    none = jnp.zeros((1, coords.shape[1]), f32)
    return jnp.concatenate([high, none, gain, none, none, none, low, none, none, none, none, none], 0)


def eye(count):
    return (iota((count, count), 0) == iota((count, count), 1)).astype(bf16)


def prep_kernel(
    positions_ref,
    features_ref,
    species_ref,
    scale_ref,
    w_first_ref,
    w_second_ref,
    radial_w_ref,
    w_mid_ref,
    w_last_ref,
    w_out_ref,
    send_ref,
    own_ref,
    right_ref,
    offered_ref,
    mats_ref,
    radial_ref,
    radial_t_ref,
    out_ref,
):
    channels = features_ref.shape[0]
    count = features_ref.shape[1]
    rows = channels + EXTRA
    species = species_ref[...]
    gain = jnp.zeros((1, count), f32)
    for kind in range(scale_ref.shape[1]):
        scale = scale_ref[:, kind : kind + 1].astype(f32)
        gain = jnp.where(species == kind, scale, gain)
    extra = coord_rows(positions_ref[...], gain).astype(bf16)
    left = dot(w_first_ref[...], features_ref[...]).astype(bf16).astype(f32)
    right = dot(w_second_ref[...], features_ref[...]).astype(bf16).astype(f32)
    left = (0.5 * left).astype(bf16)
    right = (0.5 * right).astype(bf16)
    groups = count // GROUP
    for group in range(groups):
        cols = slice(group * GROUP, (group + 1) * GROUP)
        own_ref[group * rows : group * rows + channels, :] = left[:, cols]
        own_ref[group * rows + channels : (group + 1) * rows, :] = extra[:, cols]
        right_ref[group * rows : group * rows + channels, :] = right[:, cols]
        right_ref[group * rows + channels : (group + 1) * rows, :] = extra[:, cols]
    send = send_ref[...]
    picked = dot(right_ref[...], one_hot(send & (GROUP - 1), GROUP))
    chosen = picked[:rows]
    for group in range(1, groups):
        chosen = jnp.where(send // GROUP == group, picked[group * rows : (group + 1) * rows], chosen)
    offered_ref[...] = chosen.astype(bf16)

    unit = eye(channels)
    w_mid = w_mid_ref[...]
    w_last = w_last_ref[...]
    last_t = dot_nt(unit, w_last).astype(bf16)
    mid_t = dot_nt(unit, w_mid).astype(bf16)
    wide = QUAD * channels
    for place, matrix in enumerate((w_mid, w_last, last_t, mid_t)):
        mats_ref[place * wide : (place + 1) * wide, :] = (0.5 * diagonal_copies(matrix)).astype(bf16)
    bases = radial_w_ref.shape[0]
    high, low = split_two(radial_w_ref[...])
    high = high.astype(bf16)
    low = low.astype(bf16)
    spread = dot_nt(unit, jnp.concatenate([high, high, low, low], 0)).astype(bf16)
    radial_ref[...] = (0.5 * diagonal_copies(spread)).astype(bf16)
    radial_t_ref[...] = diagonal_copies(jnp.concatenate([high, low], 0)).astype(bf16)
    w_out = w_out_ref[...]
    diagonal = jnp.where(iota((channels, channels), 0) == iota((channels, channels), 1), w_out, 0.0)
    out_ref[...] = jnp.broadcast_to(jnp.sum(diagonal, axis=1, keepdims=True), (channels, LANES))


def diagonal_copies(matrix):
    high, wide = matrix.shape
    repeat = (iota((wide, QUAD * wide), 0) == iota((wide, QUAD * wide), 1) % wide).astype(bf16)
    row = dot(matrix, repeat)
    full = jnp.concatenate([row] * QUAD, 0)
    return jnp.where(iota(full.shape, 0) // high == iota(full.shape, 1) // wide, full, 0.0)


def group_pick(values, high, rows, groups):
    chosen = values[:rows]
    for group in range(1, groups):
        chosen = jnp.where(high == group, values[group * rows : (group + 1) * rows], chosen)
    return chosen


def spread_groups(values, high, groups):
    pieces = [jnp.where(high == group, values, 0.0) for group in range(groups)]
    if groups % 2:
        pieces.append(jnp.zeros_like(values))
    return jnp.concatenate(pieces, 0).astype(bf16)


def pair_body(
    per_step,
    own_groups,
    partner_groups,
    channels,
    bases,
    owner_ref,
    partner_ref,
    mask_ref,
    own_ref,
    right_ref,
    mats_ref,
    radial_ref,
    radial_t_ref,
    out_ref,
    own_acc,
    partner_acc,
    hot_own,
    hot_partner,
    slope_one,
    slope_two,
):
    rows = channels + EXTRA
    line = CHUNK // LANES
    block = QUAD * line
    wide = QUAD * channels
    steps = owner_ref.shape[0] // (per_step * block)
    w_out = jnp.concatenate([out_ref[...]] * line, 1)
    centers = iota((bases, CHUNK), 0).astype(f32) * (1.0 / (bases - 1))
    sub = iota((8, CHUNK), 0)
    quads = range(QUAD)

    def matrix(place):
        return mats_ref[place * wide : (place + 1) * wide, :]

    def part(values, number, size=channels):
        return values[number * size : (number + 1) * size]

    def silu_pair(half):
        grow = jnp.tanh(half)
        plus = 1.0 + grow
        hidden = half * plus
        return hidden, plus + hidden * (1.0 - grow)

    def chunk(base, number):
        at = pl.multiple_of(base + number * block, block)
        owner_rows = owner_ref[pl.ds(at, block), :]
        partner_rows = partner_ref[pl.ds(at, block), :]
        live_rows = mask_ref[pl.ds(at, block), :].astype(f32)

        def row_of(values, quad):
            return jnp.concatenate(
                [values[quad * line + piece : quad * line + piece + 1, :] for piece in range(line)], 1
            )

        own_high, partner_high, projected, shifts, squares, weights, stacks, slopes = ([] for _ in range(8))
        for quad in quads:
            cols = slice(quad * CHUNK, (quad + 1) * CHUNK)
            owner = row_of(owner_rows, quad)
            partner = row_of(partner_rows, quad)
            own_high.append(owner // GROUP)
            partner_high.append(partner // GROUP)
            hot_own[number, :, cols] = one_hot(owner & (GROUP - 1), GROUP)
            hot_partner[number, :, cols] = one_hot(partner & (GROUP - 1), GROUP)
            yield
        for quad in quads:
            cols = slice(quad * CHUNK, (quad + 1) * CHUNK)
            own_vals = group_pick(
                dot(own_ref[...], hot_own[number, :, cols]), own_high[quad], rows, own_groups
            )
            partner_vals = group_pick(
                dot(right_ref[...], hot_partner[number, :, cols]), partner_high[quad], rows, partner_groups
            )
            projected.append(own_vals[:channels] + partner_vals[:channels])
            own_coords = own_vals[channels : channels + 8] + own_vals[channels + 8 :]
            partner_coords = partner_vals[channels : channels + 8] + partner_vals[channels + 8 :]
            shift = partner_coords - own_coords
            square = shift * shift
            squared = square[0:1] + square[1:2] + square[2:3]
            weights.append(row_of(live_rows, quad) * own_coords[4:5] * partner_coords[4:5])
            away = squared - centers
            basis = jnp.exp(-basis_width * (away * away))
            basis_high, basis_low = split_two(basis)
            stacks.append(jnp.concatenate([basis_high, basis_low, basis_high, basis_low], 0).astype(bf16))
            slopes.append((-2.0 * basis_width) * away * basis)
            shifts.append(shift)
            squares.append(squared)
            yield
        radial = dot(radial_ref[...], jnp.concatenate(stacks, 0))
        yield
        pieces = []
        for quad in quads:
            hidden, slope_one[number, quad] = silu_pair(projected[quad] + part(radial, quad))
            pieces.append(hidden.astype(bf16))
        yield
        half = dot(matrix(0), jnp.concatenate(pieces, 0))
        yield
        pieces = []
        for quad in quads:
            hidden, slope_two[number, quad] = silu_pair(part(half, quad))
            pieces.append(hidden.astype(bf16))
        yield
        half = dot(matrix(1), jnp.concatenate(pieces, 0))
        yield
        pieces = []
        readouts = []
        for quad in quads:
            hidden, slope = silu_pair(part(half, quad))
            readouts.append(jnp.sum(w_out * hidden, axis=0, keepdims=True))
            pieces.append(((0.5 * w_out) * slope).astype(bf16))
        yield
        back = dot(matrix(2), jnp.concatenate(pieces, 0))
        yield
        pieces = [(part(back, quad) * slope_two[number, quad]).astype(bf16) for quad in quads]
        back = dot(matrix(3), jnp.concatenate(pieces, 0))
        yield
        pieces = [(part(back, quad) * slope_one[number, quad]).astype(bf16) for quad in quads]
        back = dot(radial_t_ref[...], jnp.concatenate(pieces, 0))
        yield
        own_parts = []
        partner_parts = []
        for quad in quads:
            two = part(back, quad, 2 * bases)
            readout_slope = jnp.sum((two[:bases] + two[bases:]) * slopes[quad], axis=0, keepdims=True)
            near = jnp.maximum(1.0 - squares[quad], 0.0)
            weight_near = weights[quad] * near
            energy = weight_near * near * readouts[quad]
            slope = weight_near * (near * readout_slope - 2.0 * readouts[quad])
            push = (2.0 * slope) * shifts[quad]
            high, low = split_two(jnp.where(sub == 3, energy, push))
            values = jnp.concatenate([high[:4], low[:4]], 0)
            own_parts.append(spread_groups(values, own_high[quad], own_groups))
            partner_parts.append(spread_groups(values, partner_high[quad], partner_groups))
        yield
        own_acc[...] += dot_nt(jnp.concatenate(own_parts, 1), hot_own[number])
        partner_acc[...] += dot_nt(jnp.concatenate(partner_parts, 1), hot_partner[number])

    def step(index, unused):
        base = pl.multiple_of(index * (per_step * block), per_step * block)
        running = []
        waiting = [chunk(base, number) for number in range(per_step)]
        while running or waiting:
            if waiting:
                running.append(waiting.pop(0))
            for _ in range(2):
                running = [task for task in running if next(task, task) is not task]
        return unused

    lax.fori_loop(0, steps, step, 0)


def local_kernel(per_step, channels, bases, with_start, *refs):
    if with_start:
        (owner, partner, mask, own, right, mats, radial, radial_t, out, own_in, partner_in) = refs[:11]
        own_acc, partner_acc, *scratch = refs[11:]
        own_acc[...] = own_in[...]
        partner_acc[...] = partner_in[...]
    else:
        (owner, partner, mask, own, right, mats, radial, radial_t, out) = refs[:9]
        own_acc, partner_acc, *scratch = refs[9:]
        own_acc[...] = jnp.zeros_like(own_acc)
        partner_acc[...] = jnp.zeros_like(partner_acc)
    groups = own.shape[0] // (channels + EXTRA)
    pair_body(
        per_step,
        groups,
        groups,
        channels,
        bases,
        owner,
        partner,
        mask,
        own,
        right,
        mats,
        radial,
        radial_t,
        out,
        own_acc,
        partner_acc,
        *scratch,
    )


def neighbour(sizes, offset, sign):
    flat = 0
    for (name, size), step in zip(sizes, offset):
        place = lax.axis_index(name)
        if step:
            place = lax.rem(place + (sign % size), size)
        flat = flat * size + place
    return flat


def fetch(sizes, sign, gathered, landed, arrived):
    copies = [
        pltpu.make_async_copy(
            gathered.at[neighbour(sizes, offset, sign)], landed.at[block], arrived.at[block]
        )
        for block, offset in enumerate(ghost_offsets)
    ]
    for copy in copies:
        copy.start()
    for copy in copies:
        copy.wait()


def ghost_kernel(per_step, channels, bases, sizes, *refs):
    blocks = len(ghost_offsets)
    (owner, partner, mask, own, mats, radial, radial_t, out, own_in, gathered) = refs[:10]
    own_acc, forces, landed, arrived, table, partner_acc, *scratch = refs[10:]
    rows = channels + EXTRA
    groups = own.shape[0] // rows
    fetch(sizes, 1, gathered, landed, arrived)
    own_acc[...] = own_in[...]
    partner_acc[...] = jnp.zeros_like(partner_acc)
    for block, offset in enumerate(ghost_offsets):
        start = block * rows
        table[start : start + channels, :] = landed[block, 0:channels, :]
        extra = landed[block, channels:rows, :].astype(f32)
        coords = extra[0:8] + extra[8:16]
        moved = jnp.concatenate(
            [coords[axis : axis + 1] + domain_edge * offset[axis] for axis in range(3)], 0
        )
        table[start + channels : start + rows, :] = coord_rows(moved, coords[4:5]).astype(bf16)
    pair_body(
        per_step,
        groups,
        blocks,
        channels,
        bases,
        owner,
        partner,
        mask,
        own,
        table,
        mats,
        radial,
        radial_t,
        out,
        own_acc,
        partner_acc,
        *scratch,
    )
    forces[...] = jnp.zeros_like(forces)
    for block in range(blocks):
        both = partner_acc[block * 8 : block * 8 + 8, :]
        forces[3 * block : 3 * block + 3, :] = -(both[:3] + both[4:7])


def final_kernel(sizes, *refs):
    own_ref, partner_ref, send_ref, gathered, forces_ref, energy_ref, landed, arrived = refs
    fetch(sizes, -1, gathered, landed, arrived)
    incoming = landed[0, 0:3, :]
    for block in range(1, len(ghost_offsets)):
        incoming = incoming + landed[block, 3 * block : 3 * block + 3, :]
    high, low = split_two(jnp.concatenate([incoming, jnp.zeros_like(incoming[:1])], 0))
    send = send_ref[...]
    groups = own_ref.shape[0] // 8
    values = spread_groups(jnp.concatenate([high, low], 0), send // GROUP, groups)
    back = dot_nt(values, one_hot(send & (GROUP - 1), GROUP))
    for group in range(groups):
        part = slice(group * 8, group * 8 + 8)
        total = own_ref[part, :] - partner_ref[part, :] + back[part]
        total = total[:4] + total[4:]
        cols = slice(group * GROUP, (group + 1) * GROUP)
        forces_ref[:, cols] = total[:3]
        energy = own_ref[group * 8 + 3 : group * 8 + 4, :] + own_ref[group * 8 + 7 : group * 8 + 8, :]
        energy_ref[:, cols] = energy


def whole(shape, dtype):
    return jax.ShapeDtypeStruct(shape, dtype)


def call(kernel, outs, name, scratch=(), specs=None, cost=None):
    more = {} if cost is None else dict(cost_estimate=cost)
    return pl.pallas_call(
        kernel,
        grid=(1,),
        in_specs=specs,
        out_specs=tuple(pl.BlockSpec(memory_space=pltpu.VMEM) for _ in outs),
        out_shape=outs,
        scratch_shapes=list(scratch),
        compiler_params=pltpu.CompilerParams(vmem_limit_bytes=VMEM_LIMIT),
        name=name,
        **more,
    )


def on_device(
    sizes,
    positions,
    features,
    species,
    species_scale,
    w_first,
    w_second,
    w_radial,
    w_mid,
    w_last,
    w_out,
    ghost_send,
    local_first,
    local_second,
    local_mask,
    ghost_owner,
    ghost_index,
    ghost_mask,
):
    channels, own_count = features.shape
    send_count = ghost_send.shape[0]
    bases = w_radial.shape[1]
    rows = channels + EXTRA
    groups = own_count // GROUP
    blocks = len(ghost_offsets)
    names = tuple(name for name, size in sizes)
    send = ghost_send.reshape(1, send_count)
    whole_spec = pl.BlockSpec(memory_space=pltpu.VMEM)
    remain = pl.BlockSpec(memory_space=pl.ANY)
    own, right, offered, mats, radial, radial_t, out = call(
        prep_kernel,
        (
            whole((groups * rows, GROUP), bf16),
            whole((groups * rows, GROUP), bf16),
            whole((rows, send_count), bf16),
            whole((4 * QUAD * channels, QUAD * channels), bf16),
            whole((QUAD * channels, QUAD * 4 * bases), bf16),
            whole((QUAD * 2 * bases, QUAD * channels), bf16),
            whole((channels, LANES), f32),
        ),
        "tables",
        specs=[whole_spec] * 11,
    )(
        positions,
        features,
        species.reshape(1, own_count),
        species_scale.reshape(1, species_scale.shape[0]),
        w_first,
        w_second,
        w_radial.T,
        w_mid,
        w_last,
        w_out.reshape(1, channels),
        send,
    )
    gathered = lax.all_gather(offered, names)

    def tiles(value):
        return value.reshape(value.shape[0] // LANES, LANES)

    def scratch(per_step):
        return [
            pltpu.VMEM((per_step, GROUP, QUAD * CHUNK), bf16),
            pltpu.VMEM((per_step, GROUP, QUAD * CHUNK), bf16),
            pltpu.VMEM((per_step, QUAD, channels, CHUNK), f32),
            pltpu.VMEM((per_step, QUAD, channels, CHUNK), f32),
        ]

    def cost(slots):
        return pl.CostEstimate(flops=slots * 400000, bytes_accessed=slots * 12, transcendentals=slots * 200)

    local = [tiles(value) for value in (local_first, local_second, local_mask)]
    parts = 2
    part_rows = local[0].shape[0] // parts
    weights = (mats, radial, radial_t, out)
    local_step = math.gcd(part_rows * LANES // (QUAD * CHUNK), 5)

    def local_call(part, start):
        cut = pl.BlockSpec((part_rows, LANES), lambda step: (part, 0))
        operands = [*local, own, right, *weights, *start]
        return call(
            functools.partial(local_kernel, local_step, channels, bases, bool(start)),
            (whole((groups * 8, GROUP), f32), whole((groups * 8, GROUP), f32)),
            "local_pairs",
            scratch(local_step),
            [cut] * 3 + [whole_spec] * (len(operands) - 3),
            cost(part_rows * LANES),
        )(*operands)

    own_sum, partner_sum = local_call(0, ())
    ghost_lists = [tiles(value) for value in (ghost_owner, ghost_index, ghost_mask)]
    ghost_step = math.gcd(ghost_owner.shape[0] // (QUAD * CHUNK), 4)
    fetched = [pltpu.SemaphoreType.DMA((blocks,))]
    own_sum, ghost_forces = call(
        functools.partial(ghost_kernel, ghost_step, channels, bases, sizes),
        (whole((groups * 8, GROUP), f32), whole((3 * (blocks + 1), send_count), f32)),
        "ghost_pairs",
        [pltpu.VMEM((blocks, rows, send_count), bf16)]
        + fetched
        + [
            pltpu.VMEM((blocks * rows, GROUP), bf16),
            pltpu.VMEM(((blocks + blocks % 2) * 8, GROUP), f32),
        ]
        + scratch(ghost_step),
        [whole_spec] * 9 + [remain],
        cost(ghost_owner.shape[0]),
    )(*ghost_lists, own, *weights, own_sum, gathered)
    returned = lax.all_gather(ghost_forces, names)
    own_sum, partner_sum = local_call(1, (own_sum, partner_sum))
    forces, energy = call(
        functools.partial(final_kernel, sizes),
        (whole((3, own_count), f32), whole((1, own_count), f32)),
        "totals",
        [pltpu.VMEM((blocks, 3 * (blocks + 1), send_count), f32)] + fetched,
        [whole_spec] * 3 + [remain],
    )(own_sum, partner_sum, send, returned)
    return forces, energy.reshape(own_count)


def solution(mesh):
    names = ("gx", "gy", "gz")
    sizes = tuple((name, mesh.shape[name]) for name in names)
    split = P(names)
    cols = P(None, names)
    in_specs = (cols, cols, split) + (P(),) * 7 + (split,) * 7
    return jax.shard_map(
        functools.partial(on_device, sizes),
        mesh=mesh,
        in_specs=in_specs,
        out_specs=(cols, split),
        check_vma=False,
    )
```

time: 80.5 us -> 182 us (2.26)
  blocking collectives: 0 us -> 73.6 us
  waiting for transfers between devices: 0.42 us -> 44.9 us
  starting transfers between devices: 19.7 us -> 0.04 us
  Pallas kernels: 53.8 us -> 36.8 us
  between operations: 0.83 us -> 14.1 us
  local copies, waits for them, and re-layouts: 5.29 us -> 11.7 us
    all_gather x0 -> x1, blocking collectives: none -> 73.6 us  [on_device(): returned = lax.all_gather(ghost_forces, names)]
    all_gather x0 -> x1, waiting for transfers between devices: none -> 44.9 us  [on_device(): gathered = lax.all_gather(offered, names)]
    ppermute x14 -> x0, starting transfers between devices: 19.7 us -> none  [shifted(): return lax.ppermute(value, used, pairs)]
    pallas_call x4, Pallas kernels: 53.5 us -> 35.9 us  [the longest x2 19.4 us: local_call(): call(functools.partial(local_kernel, local_step, channels, bases, bool(st...]
    unnamed x35 -> x44, local copies, waits for them, and re-layouts: 5.29 us -> 11.7 us
  transfers between devices with their start and end apart: 14 -> 1, of which waited for: 1 -> 1; matrix products, arithmetic and copies ran while one was open for 0% -> 0% of each run, Pallas kernels for 37% -> 5%
where the time goes in v2:
time: 182 us; the launch traced here: 181 us
  blocking collectives  73.6 us (40%)
  waiting for transfers between devices  44.9 us (25%)
  Pallas kernels  36.8 us (20%)
  between operations  14.1 us (8%)
  local copies, waits for them, and re-layouts  11.7 us (6%)
    all_gather x1, blocking collectives, on_device(): returned = lax.all_gather(ghost_forces, names)  73.6 us
    all_gather x1, waiting for transfers between devices, on_device(): gathered = lax.all_gather(offered, names)  44.9 us
    pallas_call x2, Pallas kernels, local_call(): call(functools.partial(local_kernel, local_step, channels, bases, bool(st...  19.4 us
    pallas_call x1, Pallas kernels, on_device(): call(functools.partial(ghost_kernel, ghost_step, channels, bases, sizes),...  15.4 us
    unnamed x44, local copies, waits for them, and re-layouts  11.7 us
  transfers between devices with their start and end apart: 1, of which 1 were waited for; matrix products, arithmetic and copies ran while one was open for 0% of the time, Pallas kernels for 5%

profile of v2, /device:TPU:0, one launch (start us, length us, event | category | flops | bytes accessed | tf_op | source)
XLA Modules:
  0.0 181.2 jit_solution(10440534219648949797)
XLA Ops:
  7.2 0.0 all-gather.4.cloned.1.call-start
  7.2 0.0 copy-start
  7.2 0.8 copy-done
  8.1 0.0 copy-start.1
  8.1 0.7 copy-done.1
  8.8 0.0 copy-start.2
  8.8 0.7 copy-done.2
  9.5 0.0 copy-start.3
  9.5 0.7 copy-done.3
  10.2 0.0 copy-start.4
  10.2 0.7 copy-done.4
  10.9 0.0 copy-start.5
  10.9 0.7 copy-done.5
  11.6 0.0 copy-start.6
  11.6 0.7 copy-done.6
  12.3 0.0 copy-start.8
  12.3 0.7 copy-done.8
  13.0 0.0 copy-start.9
  13.0 0.7 copy-done.9
  13.7 0.0 copy-start.10
  13.7 0.7 copy-done.10
  14.3 0.0 copy-start.11
  14.3 0.7 copy-done.11
  15.0 0.9 tables.1
  15.9 0.0 all-gather.4.cloned.1.call-update
  15.9 0.0 copy-start.13
  16.0 0.9 copy-done.13
  16.8 0.0 copy-start.15
  16.8 0.9 copy-done.15
  17.7 0.0 copy-start.17
  17.7 0.9 copy-done.17
  18.6 0.0 copy-start.19
  18.6 0.0 copy-start.20
  18.6 0.0 copy-start.21
  18.6 9.7 %local_pairs.2 = (f32[16,256]{1,0:T(8,128)S(1)}, f32[16,256]{1,0:T(8,128)S(1)}) custom-call(s32[160,128]{1,0:T(8,128)S(1)} %bitcast.22, s32[160,128]{1,0:T(8,128)S(1)} %bitcast.24, s32[160,128]{1,0:T(8,128)S(1)} %bitcast.26, bf16[160,256]{1,0:T(8,128)(2,1)S(1)} %get-tuple-element.17.refs_3_, bf16[160,256]{1,0:T(8,128)(2,1)S(1)} %get-tuple-element.18.refs_4_, ...), custom_call_target="tpu_custom_call" | custom-call | flops 4096000000 | bytes 122880 | tf_op jit(solution)/shard_map/local_pairs/pallas_call | solution.py:518
  28.3 44.9 %all-gather.4.cloned.1.call-done = bf16[2560,256]{1,0:T(8,128)(2,1)} async-done(((bf16[80,256]{1,0:T(8,128)(2,1)}), bf16[2560,256]{1,0:T(8,128)(2,1)}) %all-gather.4.cloned.1.call-update) | async-done | bytes 1310736 | tf_op jit(solution)/shard_map/all_gather | solution.py:493
  73.2 0.0 copy-done.19
  73.2 0.0 copy-done.20
  73.2 0.0 copy-done.21
  73.2 0.0 copy-start.12
  73.2 1.3 copy-done.12
  74.5 0.0 copy-start.14
  74.5 0.0 copy-start.16
  74.5 0.0 copy-start.18
  74.5 15.4 %ghost_pairs.1 = (f32[16,256]{1,0:T(8,128)S(1)}, f32[24,256]{1,0:T(8,128)S(1)}) custom-call(s32[96,128]{1,0:T(8,128)S(1)} %bitcast.28, s32[96,128]{1,0:T(8,128)S(1)} %bitcast.29, s32[96,128]{1,0:T(8,128)S(1)} %bitcast.30, bf16[160,256]{1,0:T(8,128)(2,1)S(1)} %get-tuple-element.17.refs_3_, bf16[1024,256]{1,0:T(8,128)(2,1)S(1)} %get-tuple-element.19.refs_5_.refs_4_, ...), custom_call_target="tpu_custom_call" | custom-call | flops 4915200000 | bytes 147456 | tf_op jit(solution)/shard_map/ghost_pairs/pallas_call | solution.py:531
  89.9 73.6 %all-gather.1 = f32[768,256]{1,0:T(8,128)S(1)} all-gather(f32[24,256]{1,0:T(8,128)S(1)} %get-tuple-element.29), channel_id=3, replica_groups=mesh['gx'=2,'gy'=4,'gz'=4] {'gx','gy','gz'}, dimensions={0}, use_global_device_ids=true | all-gather | bytes 811008 | tf_op jit(solution)/shard_map/all_gather | solution.py:545
  163.5 0.0 copy-done.14
  163.5 0.0 copy-done.16
  163.5 0.0 copy-done.18
  163.5 0.0 copy-start.7
  163.5 9.7 %local_pairs.3 = (f32[16,256]{1,0:T(8,128)S(1)}, f32[16,256]{1,0:T(8,128)S(1)}) custom-call(s32[160,128]{1,0:T(8,128)S(1)} %bitcast.23, s32[160,128]{1,0:T(8,128)S(1)} %bitcast.25, s32[160,128]{1,0:T(8,128)S(1)} %bitcast.27, bf16[160,256]{1,0:T(8,128)(2,1)S(1)} %get-tuple-element.17.refs_3_, bf16[160,256]{1,0:T(8,128)(2,1)S(1)} %get-tuple-element.18.refs_4_, ...), custom_call_target="tpu_custom_call" | custom-call | flops 4096000000 | bytes 122880 | tf_op jit(solution)/shard_map/local_pairs/pallas_call | solution.py:518
  173.2 0.0 copy-done.7
  173.2 1.1 totals.1
Async XLA Ops:
  7.2 66.0 %all-gather.4.cloned.1.call-start = ((), (), s32[]{:S(2)}) async-start(), calls=%async_computation | async-start | bytes 1351680 | tf_op jit(solution)/shard_map/all_gather | solution.py:493
  7.2 0.8 copy-start
  8.1 0.7 copy-start.1
  8.8 0.7 copy-start.2
  9.5 0.7 copy-start.3
  10.2 0.7 copy-start.4
  10.9 0.7 copy-start.5
  11.6 0.7 copy-start.6
  12.3 0.7 copy-start.8
  13.0 0.7 copy-start.9
  13.7 0.7 copy-start.10
  14.3 0.7 copy-start.11
  15.9 0.9 copy-start.13
  16.8 0.9 copy-start.15
  17.7 0.9 copy-start.17
  18.6 54.6 %copy-start.19 = (s32[12288]{0:T(1024)S(1)}, s32[12288]{0:T(1024)}, u32[]{:S(2)}) copy-start(s32[12288]{0:T(1024)} %param.31) | copy-start | bytes 147460
  18.6 54.6 %copy-start.20 = (s32[12288]{0:T(1024)S(1)}, s32[12288]{0:T(1024)}, u32[]{:S(2)}) copy-start(s32[12288]{0:T(1024)} %param.32) | copy-start | bytes 147460
  18.6 54.6 %copy-start.21 = (s32[12288]{0:T(1024)S(1)}, s32[12288]{0:T(1024)}, u32[]{:S(2)}) copy-start(s32[12288]{0:T(1024)} %param.33) | copy-start | bytes 147460
  73.2 1.3 copy-start.12
  74.5 89.0 %copy-start.14 = (s32[20480]{0:T(1024)S(1)}, s32[20480]{0:T(1024)}, u32[]{:S(2)}) copy-start(s32[20480]{0:T(1024)} %param.28) | copy-start | bytes 245764
  74.5 89.0 %copy-start.16 = (s32[20480]{0:T(1024)S(1)}, s32[20480]{0:T(1024)}, u32[]{:S(2)}) copy-start(s32[20480]{0:T(1024)} %param.29) | copy-start | bytes 245764
  74.5 89.0 %copy-start.18 = (s32[20480]{0:T(1024)S(1)}, s32[20480]{0:T(1024)}, u32[]{:S(2)}) copy-start(s32[20480]{0:T(1024)} %param.30) | copy-start | bytes 245764
  163.5 9.7 %copy-start.7 = (s32[256]{0:T(256)S(1)}, s32[256]{0:T(256)}, u32[]{:S(2)}) copy-start(s32[256]{0:T(256)} %param.27) | copy-start | bytes 3076
Sparse Core Ops, SparseCore 0:
  16.1 57.0 all-gather.3

commit v3 on v2

--- a/solution.py
+++ b/solution.py
@@ -55,26 +55,32 @@
     return (iota((count, count), 0) == iota((count, count), 1)).astype(bf16)
 
 
-def prep_kernel(
-    positions_ref,
-    features_ref,
-    species_ref,
-    scale_ref,
-    w_first_ref,
-    w_second_ref,
-    radial_w_ref,
-    w_mid_ref,
-    w_last_ref,
-    w_out_ref,
-    send_ref,
-    own_ref,
-    right_ref,
-    offered_ref,
-    mats_ref,
-    radial_ref,
-    radial_t_ref,
-    out_ref,
-):
+def prep_kernel(*refs):
+    sources = refs[:14]
+    own_ref, right_ref, offered_ref, mats_ref, radial_ref, radial_t_ref, out_ref = refs[14:21]
+    targets = refs[25:35] + refs[21:25]
+    landed = refs[35]
+    copies = [
+        pltpu.make_async_copy(source, target, landed.at[place])
+        for place, (source, target) in enumerate(zip(sources, targets))
+    ]
+    for copy in copies:
+        copy.start()
+    for copy in copies:
+        copy.wait()
+    (
+        positions_ref,
+        features_ref,
+        species_ref,
+        scale_ref,
+        w_first_ref,
+        w_second_ref,
+        radial_w_ref,
+        w_mid_ref,
+        w_last_ref,
+        w_out_ref,
+        send_ref,
+    ) = targets[:11]
     channels = features_ref.shape[0]
     count = features_ref.shape[1]
     rows = channels + EXTRA
@@ -146,6 +152,8 @@
 
 def pair_body(
     per_step,
+    first_row,
+    row_count,
     own_groups,
     partner_groups,
     channels,
@@ -170,7 +178,7 @@
     line = CHUNK // LANES
     block = QUAD * line
     wide = QUAD * channels
-    steps = owner_ref.shape[0] // (per_step * block)
+    steps = row_count // (per_step * block)
     w_out = jnp.concatenate([out_ref[...]] * line, 1)
     centers = iota((bases, CHUNK), 0).astype(f32) * (1.0 / (bases - 1))
     sub = iota((8, CHUNK), 0)
@@ -282,7 +290,7 @@
         partner_acc[...] += dot_nt(jnp.concatenate(partner_parts, 1), hot_partner[number])
 
     def step(index, unused):
-        base = pl.multiple_of(index * (per_step * block), per_step * block)
+        base = pl.multiple_of(first_row + index * (per_step * block), block)
         running = []
         waiting = [chunk(base, number) for number in range(per_step)]
         while running or waiting:
@@ -295,7 +303,7 @@
     lax.fori_loop(0, steps, step, 0)
 
 
-def local_kernel(per_step, channels, bases, with_start, *refs):
+def local_kernel(per_step, channels, bases, first_row, row_count, with_start, *refs):
     if with_start:
         (owner, partner, mask, own, right, mats, radial, radial_t, out, own_in, partner_in) = refs[:11]
         own_acc, partner_acc, *scratch = refs[11:]
@@ -309,6 +317,8 @@
     groups = own.shape[0] // (channels + EXTRA)
     pair_body(
         per_step,
+        first_row,
+        row_count,
         groups,
         groups,
         channels,
@@ -328,42 +338,21 @@
     )
 
 
-def neighbour(sizes, offset, sign):
-    flat = 0
-    for (name, size), step in zip(sizes, offset):
-        place = lax.axis_index(name)
-        if step:
-            place = lax.rem(place + (sign % size), size)
-        flat = flat * size + place
-    return flat
-
-
-def fetch(sizes, sign, gathered, landed, arrived):
-    copies = [
-        pltpu.make_async_copy(
-            gathered.at[neighbour(sizes, offset, sign)], landed.at[block], arrived.at[block]
-        )
-        for block, offset in enumerate(ghost_offsets)
-    ]
-    for copy in copies:
-        copy.start()
-    for copy in copies:
-        copy.wait()
-
-
-def ghost_kernel(per_step, channels, bases, sizes, *refs):
+def ghost_kernel(per_step, channels, bases, *refs):
     blocks = len(ghost_offsets)
-    (owner, partner, mask, own, mats, radial, radial_t, out, own_in, gathered) = refs[:10]
-    own_acc, forces, landed, arrived, table, partner_acc, *scratch = refs[10:]
+    (owner, partner, mask, own, mats, radial, radial_t, out, own_in) = refs[:9]
+    arrived = refs[9 : 9 + blocks]
+    own_acc = refs[9 + blocks]
+    forces = refs[10 + blocks : 10 + 2 * blocks]
+    table, partner_acc, *scratch = refs[10 + 2 * blocks :]
     rows = channels + EXTRA
     groups = own.shape[0] // rows
-    fetch(sizes, 1, gathered, landed, arrived)
     own_acc[...] = own_in[...]
     partner_acc[...] = jnp.zeros_like(partner_acc)
     for block, offset in enumerate(ghost_offsets):
         start = block * rows
-        table[start : start + channels, :] = landed[block, 0:channels, :]
-        extra = landed[block, channels:rows, :].astype(f32)
+        table[start : start + channels, :] = arrived[block][0:channels, :]
+        extra = arrived[block][channels:rows, :].astype(f32)
         coords = extra[0:8] + extra[8:16]
         moved = jnp.concatenate(
             [coords[axis : axis + 1] + domain_edge * offset[axis] for axis in range(3)], 0
@@ -371,6 +360,8 @@
         table[start + channels : start + rows, :] = coord_rows(moved, coords[4:5]).astype(bf16)
     pair_body(
         per_step,
+        0,
+        owner.shape[0],
         groups,
         blocks,
         channels,
@@ -388,19 +379,19 @@
         partner_acc,
         *scratch,
     )
-    forces[...] = jnp.zeros_like(forces)
     for block in range(blocks):
         both = partner_acc[block * 8 : block * 8 + 8, :]
-        forces[3 * block : 3 * block + 3, :] = -(both[:3] + both[4:7])
-
-
-def final_kernel(sizes, *refs):
-    own_ref, partner_ref, send_ref, gathered, forces_ref, energy_ref, landed, arrived = refs
-    fetch(sizes, -1, gathered, landed, arrived)
-    incoming = landed[0, 0:3, :]
-    for block in range(1, len(ghost_offsets)):
-        incoming = incoming + landed[block, 3 * block : 3 * block + 3, :]
-    high, low = split_two(jnp.concatenate([incoming, jnp.zeros_like(incoming[:1])], 0))
+        forces[block][...] = -(both + jnp.concatenate([both[4:], both[:4]], 0))
+
+
+def final_kernel(blocks, *refs):
+    own_ref, partner_ref, send_ref = refs[:3]
+    arrived = refs[3 : 3 + blocks]
+    forces_ref, energy_ref = refs[3 + blocks :]
+    incoming = arrived[0][...]
+    for block in range(1, blocks):
+        incoming = incoming + arrived[block][...]
+    high, low = split_two(incoming[:4])
     send = send_ref[...]
     groups = own_ref.shape[0] // 8
     values = spread_groups(jnp.concatenate([high, low], 0), send // GROUP, groups)
@@ -432,6 +423,22 @@
         name=name,
         **more,
     )
+
+
+def shifted(value, offset, sizes, sign):
+    used = tuple(axis for axis, step in zip(sizes, offset) if step)
+    dims = [size for name, size in used]
+    pairs = []
+    for flat in range(math.prod(dims)):
+        place, rest = [], flat
+        for size in reversed(dims):
+            place.insert(0, rest % size)
+            rest //= size
+        target = 0
+        for at, size in zip(place, dims):
+            target = target * size + (at - sign) % size
+        pairs.append((flat, target))
+    return lax.ppermute(value, tuple(name for name, size in used), pairs)
 
 
 def on_device(
@@ -460,24 +467,12 @@
     rows = channels + EXTRA
     groups = own_count // GROUP
     blocks = len(ghost_offsets)
-    names = tuple(name for name, size in sizes)
     send = ghost_send.reshape(1, send_count)
     whole_spec = pl.BlockSpec(memory_space=pltpu.VMEM)
-    remain = pl.BlockSpec(memory_space=pl.ANY)
-    own, right, offered, mats, radial, radial_t, out = call(
-        prep_kernel,
-        (
-            whole((groups * rows, GROUP), bf16),
-            whole((groups * rows, GROUP), bf16),
-            whole((rows, send_count), bf16),
-            whole((4 * QUAD * channels, QUAD * channels), bf16),
-            whole((QUAD * channels, QUAD * 4 * bases), bf16),
-            whole((QUAD * 2 * bases, QUAD * channels), bf16),
-            whole((channels, LANES), f32),
-        ),
-        "tables",
-        specs=[whole_spec] * 11,
-    )(
+    def tiles(value):
+        return value.reshape(value.shape[0] // LANES, LANES)
+
+    small = (
         positions,
         features,
         species.reshape(1, own_count),
@@ -488,12 +483,26 @@
         w_mid,
         w_last,
         w_out.reshape(1, channels),
-        send,
     )
-    gathered = lax.all_gather(offered, names)
-
-    def tiles(value):
-        return value.reshape(value.shape[0] // LANES, LANES)
+    lists = [send] + [tiles(value) for value in (local_first, local_second, local_mask)]
+    own, right, offered, mats, radial, radial_t, out, send, *local = call(
+        prep_kernel,
+        (
+            whole((groups * rows, GROUP), bf16),
+            whole((groups * rows, GROUP), bf16),
+            whole((rows, send_count), bf16),
+            whole((4 * QUAD * channels, QUAD * channels), bf16),
+            whole((QUAD * channels, QUAD * 4 * bases), bf16),
+            whole((QUAD * 2 * bases, QUAD * channels), bf16),
+            whole((channels, LANES), f32),
+            *[whole(value.shape, value.dtype) for value in lists],
+        ),
+        "tables",
+        [pltpu.VMEM(value.shape, value.dtype) for value in small]
+        + [pltpu.SemaphoreType.DMA((len(small) + len(lists),))],
+        [pl.BlockSpec(memory_space=pltpu.HBM)] * (len(small) + len(lists)),
+    )(*[pltpu.with_memory_space_constraint(value, pltpu.HBM) for value in (*small, *lists)])
+    arrived = [shifted(offered, offset, sizes, 1) for offset in ghost_offsets]
 
     def scratch(per_step):
         return [
@@ -506,51 +515,45 @@
     def cost(slots):
         return pl.CostEstimate(flops=slots * 400000, bytes_accessed=slots * 12, transcendentals=slots * 200)
 
-    local = [tiles(value) for value in (local_first, local_second, local_mask)]
     parts = 2
     part_rows = local[0].shape[0] // parts
     weights = (mats, radial, radial_t, out)
-    local_step = math.gcd(part_rows * LANES // (QUAD * CHUNK), 5)
+    local_step = part_rows * LANES // (QUAD * CHUNK)
 
     def local_call(part, start):
-        cut = pl.BlockSpec((part_rows, LANES), lambda step: (part, 0))
         operands = [*local, own, right, *weights, *start]
         return call(
-            functools.partial(local_kernel, local_step, channels, bases, bool(start)),
+            functools.partial(local_kernel, local_step, channels, bases, part * part_rows, part_rows, bool(start)),
             (whole((groups * 8, GROUP), f32), whole((groups * 8, GROUP), f32)),
             "local_pairs",
             scratch(local_step),
-            [cut] * 3 + [whole_spec] * (len(operands) - 3),
+            [whole_spec] * len(operands),
             cost(part_rows * LANES),
         )(*operands)
 
     own_sum, partner_sum = local_call(0, ())
     ghost_lists = [tiles(value) for value in (ghost_owner, ghost_index, ghost_mask)]
-    ghost_step = math.gcd(ghost_owner.shape[0] // (QUAD * CHUNK), 4)
-    fetched = [pltpu.SemaphoreType.DMA((blocks,))]
-    own_sum, ghost_forces = call(
-        functools.partial(ghost_kernel, ghost_step, channels, bases, sizes),
-        (whole((groups * 8, GROUP), f32), whole((3 * (blocks + 1), send_count), f32)),
+    ghost_step = ghost_owner.shape[0] // (QUAD * CHUNK)
+    own_sum, *ghost_forces = call(
+        functools.partial(ghost_kernel, ghost_step, channels, bases),
+        (whole((groups * 8, GROUP), f32),) + (whole((8, send_count), f32),) * blocks,
         "ghost_pairs",
-        [pltpu.VMEM((blocks, rows, send_count), bf16)]
-        + fetched
-        + [
+        [
             pltpu.VMEM((blocks * rows, GROUP), bf16),
             pltpu.VMEM(((blocks + blocks % 2) * 8, GROUP), f32),
         ]
         + scratch(ghost_step),
-        [whole_spec] * 9 + [remain],
+        [whole_spec] * (9 + blocks),
         cost(ghost_owner.shape[0]),
-    )(*ghost_lists, own, *weights, own_sum, gathered)
-    returned = lax.all_gather(ghost_forces, names)
+    )(*ghost_lists, own, *weights, own_sum, *arrived)
+    returned = [shifted(force, offset, sizes, -1) for force, offset in zip(ghost_forces, ghost_offsets)]
     own_sum, partner_sum = local_call(1, (own_sum, partner_sum))
     forces, energy = call(
-        functools.partial(final_kernel, sizes),
+        functools.partial(final_kernel, blocks),
         (whole((3, own_count), f32), whole((1, own_count), f32)),
         "totals",
-        [pltpu.VMEM((blocks, 3 * (blocks + 1), send_count), f32)] + fetched,
-        [whole_spec] * 3 + [remain],
-    )(own_sum, partner_sum, send, returned)
+        specs=[whole_spec] * (3 + blocks),
+    )(own_sum, partner_sum, send, *returned)
     return forces, energy.reshape(own_count)
 
 

time: 182 us -> 56.4 us (0.31)
  blocking collectives: 73.6 us -> 0 us
  waiting for transfers between devices: 44.9 us -> 0.44 us
  starting transfers between devices: 0.04 us -> 19.7 us
  between operations: 14.1 us -> 0.75 us
  local copies, waits for them, and re-layouts: 11.7 us -> 0.01 us
    all_gather x1 -> x0, blocking collectives: 73.6 us -> none  [on_device(): returned = lax.all_gather(ghost_forces, names)]
    all_gather x1 -> x0, waiting for transfers between devices: 44.9 us -> none  [on_device(): gathered = lax.all_gather(offered, names)]
    ppermute x0 -> x14, starting transfers between devices: none -> 19.7 us  [shifted(): return lax.ppermute(value, tuple((name for name, size in used)), pairs)]
    unnamed x44 -> x6, local copies, waits for them, and re-layouts: 11.7 us -> 0.01 us
    pallas_call x4, Pallas kernels: 35.9 us -> 33.5 us  [the longest x2 18.7 us: local_call(): call(functools.partial(local_kernel, local_step, channels, bases, part *...]
  transfers between devices with their start and end apart: 1 -> 14, of which waited for: 1 -> 1; matrix products, arithmetic and copies ran while one was open for 0% -> 0% of each run, Pallas kernels for 5% -> 33%
where the time goes in v3:
time: 56.4 us; the launch traced here: 56.2 us
  Pallas kernels  35.2 us (62%)
  starting transfers between devices  19.7 us (35%)
  between operations  0.75 us (1%)
    ppermute x14, starting transfers between devices, shifted(): return lax.ppermute(value, tuple((name for name, size in used)), pairs)  19.7 us
    pallas_call x2, Pallas kernels, local_call(): call(functools.partial(local_kernel, local_step, channels, bases, part *...  18.7 us
    pallas_call x1, Pallas kernels, on_device(): call(functools.partial(ghost_kernel, ghost_step, channels, bases), (whole...  13.9 us
    pallas_call x1, Pallas kernels, on_device(): call(prep_kernel, (whole((groups * rows, GROUP), bf16), whole((groups * r...  1.74 us
  transfers between devices with their start and end apart: 14, of which 1 were waited for; matrix products, arithmetic and copies ran while one was open for 0% of the time, Pallas kernels for 33%

profile of v3, /device:TPU:0, one launch (start us, length us, event | category | flops | bytes accessed | tf_op | source)
XLA Modules:
  0.0 56.2 jit_solution(18017048468690402238)
XLA Ops:
  0.6 1.7 %tables.1 = (bf16[160,256]{1,0:T(8,128)(2,1)S(1)}, bf16[160,256]{1,0:T(8,128)(2,1)S(1)}, bf16[80,256]{1,0:T(8,128)(2,1)S(1)}, bf16[1024,256]{1,0:T(8,128)(2,1)S(...) custom-call(f32[3,512]{1,0:T(4,128)} %refs_0_.1, ...), custom_call_target="tpu_custom_call" | custom-call | tf_op jit(solution)/shard_map/tables/pallas_call | solution.py:488
  2.4 6.4 %collective-permute-start.6 = (bf16[80,256]{1,0:T(8,128)(2,1)S(1)}, bf16[80,256]{1,0:T(8,128)(2,1)S(1)}, u32[]{:S(2)}, u32[]{:S(2)}) collective-permute-start(bf16[80,256]{1,0:T(8,128)(2,1)S(1)} %get-tuple-element.37), channel_id=1, source_target_pairs={{0,31},{1,28},{2,29},{3,30},{4,19},{5,16},{6,17},{7,18},{8,23},{9,... | collective-permute-start | bytes 122888 | tf_op jit(solution)/shard_map/ppermute | solution.py:441
  8.8 0.7 %collective-permute-start.5 = (bf16[80,256]{1,0:T(8,128)(2,1)S(1)}, bf16[80,256]{1,0:T(8,128)(2,1)S(1)}, u32[]{:S(2)}, u32[]{:S(2)}) collective-permute-start(bf16[80,256]{1,0:T(8,128)(2,1)S(1)} %get-tuple-element.37), channel_id=1, source_target_pairs={{0,15},{1,12},{2,13},{3,14},{4,3},{5,0},{6,1},{7,2},{8,7},{9,4},{1... | collective-permute-start | bytes 122888 | tf_op jit(solution)/shard_map/ppermute | solution.py:441
  9.5 0.4 collective-permute-start.4
  10.0 0.8 %collective-permute-start.3 = (bf16[80,256]{1,0:T(8,128)(2,1)S(1)}, bf16[80,256]{1,0:T(8,128)(2,1)S(1)}, u32[]{:S(2)}, u32[]{:S(2)}) collective-permute-start(bf16[80,256]{1,0:T(8,128)(2,1)S(1)} %get-tuple-element.37), channel_id=1, source_target_pairs={{0,28},{4,16},{8,20},{12,24},{16,12},{20,0},{24,4},{28,8},{1,29},{... | collective-permute-start | bytes 122888 | tf_op jit(solution)/shard_map/ppermute | solution.py:441
  10.7 0.5 collective-permute-start.2
  11.2 0.0 collective-permute-done.6.refs_15_
  11.2 0.7 %collective-permute-start.1 = (bf16[80,256]{1,0:T(8,128)(2,1)S(1)}, bf16[80,256]{1,0:T(8,128)(2,1)S(1)}, u32[]{:S(2)}, u32[]{:S(2)}) collective-permute-start(bf16[80,256]{1,0:T(8,128)(2,1)S(1)} %get-tuple-element.37), channel_id=1, source_target_pairs={{0,12},{4,0},{8,4},{12,8},{1,13},{5,1},{9,5},{13,9},{2,14},{6,2},{... | collective-permute-start | bytes 122888 | tf_op jit(solution)/shard_map/ppermute | solution.py:441
  11.9 0.4 collective-permute-done.5.refs_14_
  12.2 0.5 collective-permute-start
  12.8 0.0 copy-start
  12.8 0.0 copy-start.1
  12.8 0.0 copy-start.2
  12.8 9.4 %local_pairs.2 = (f32[16,256]{1,0:T(8,128)S(1)}, f32[16,256]{1,0:T(8,128)S(1)}) custom-call(s32[160,128]{1,0:T(8,128)S(1)} %get-tuple-element.27.refs_0_, s32[160,128]{1,0:T(8,128)S(1)} %get-tuple-element.28.refs_1_, s32[160,128]{1,0:T(8,128)S(1)} %get-tuple-element.29.refs_2_, bf16[160,256]{1,0:T(8,128)(2,1)S(1)} %get-tuple-element.30.refs_3_, ...), custom_call_target="tpu_custom_call" | custom-call | flops 4096000000 | bytes 122880 | tf_op jit(solution)/shard_map/local_pairs/pallas_call | solution.py:525
  22.1 0.0 collective-permute-done.4.refs_13_
  22.1 0.0 collective-permute-done.3.refs_12_
  22.2 0.0 collective-permute-done.2.refs_11_
  22.2 0.0 collective-permute-done.1.refs_10_
  22.2 0.0 collective-permute-done.refs_9_
  22.2 0.0 copy-done
  22.2 0.0 copy-done.1
  22.2 0.0 copy-done.2
  22.2 13.9 %ghost_pairs.1 = (f32[16,256]{1,0:T(8,128)S(1)}, f32[8,256]{1,0:T(8,128)S(1)}, f32[8,256]{1,0:T(8,128)S(1)}, f32[8,256]{1,0:T(8,128)S(1)}, f32[8,256]{1,0:T(8,12...) custom-call(s32[96,128]{1,0:T(8,128)S(1)} %bitcast.12, s32[96,128]{1,0:T(8,128)S(1)} %bitcast.13, ...), custom_call_target="tpu_custom_call" | custom-call | flops 4915200000 | bytes 147456 | tf_op jit(solution)/shard_map/ghost_pairs/pallas_call | solution.py:537
  36.2 1.6 %collective-permute-start.7 = (f32[8,256]{1,0:T(8,128)S(1)}, f32[8,256]{1,0:T(8,128)S(1)}, u32[]{:S(2)}, u32[]{:S(2)}) collective-permute-start(f32[8,256]{1,0:T(8,128)S(1)} %get-tuple-element.43), channel_id=1, source_target_pairs={{0,16},{16,0},{1,17},{17,1},{2,18},{18,2},{3,19},{19,3},{4,20},{20... | collective-permute-start | bytes 24584 | tf_op jit(solution)/shard_map/ppermute | solution.py:441
  37.8 0.1 collective-permute-start.8
  37.8 1.1 %collective-permute-start.9 = (f32[8,256]{1,0:T(8,128)S(1)}, f32[8,256]{1,0:T(8,128)S(1)}, u32[]{:S(2)}, u32[]{:S(2)}) collective-permute-start(f32[8,256]{1,0:T(8,128)S(1)} %get-tuple-element.45), channel_id=1, source_target_pairs={{0,1},{1,2},{2,3},{3,0},{4,5},{5,6},{6,7},{7,4},{8,9},{9,10},{10,1... | collective-permute-start | bytes 24584 | tf_op jit(solution)/shard_map/ppermute | solution.py:441
  38.9 1.5 %collective-permute-start.10 = (f32[8,256]{1,0:T(8,128)S(1)}, f32[8,256]{1,0:T(8,128)S(1)}, u32[]{:S(2)}, u32[]{:S(2)}) collective-permute-start(f32[8,256]{1,0:T(8,128)S(1)} %get-tuple-element.46), channel_id=1, source_target_pairs={{0,20},{4,24},{8,28},{12,16},{16,4},{20,8},{24,12},{28,0},{1,21},{... | collective-permute-start | bytes 24584 | tf_op jit(solution)/shard_map/ppermute | solution.py:441
  40.4 2.5 %collective-permute-start.11 = (f32[8,256]{1,0:T(8,128)S(1)}, f32[8,256]{1,0:T(8,128)S(1)}, u32[]{:S(2)}, u32[]{:S(2)}) collective-permute-start(f32[8,256]{1,0:T(8,128)S(1)} %get-tuple-element.47), channel_id=1, source_target_pairs={{0,17},{1,18},{2,19},{3,16},{16,1},{17,2},{18,3},{19,0},{4,21},{5,... | collective-permute-start | bytes 24584 | tf_op jit(solution)/shard_map/ppermute | solution.py:441
  42.9 0.0 collective-permute-done.7.refs_3_
  42.9 1.0 %collective-permute-start.12 = (f32[8,256]{1,0:T(8,128)S(1)}, f32[8,256]{1,0:T(8,128)S(1)}, u32[]{:S(2)}, u32[]{:S(2)}) collective-permute-start(f32[8,256]{1,0:T(8,128)S(1)} %get-tuple-element.48), channel_id=1, source_target_pairs={{0,5},{1,6},{2,7},{3,4},{4,9},{5,10},{6,11},{7,8},{8,13},{9,14},{1... | collective-permute-start | bytes 24584 | tf_op jit(solution)/shard_map/ppermute | solution.py:441
  43.9 0.0 collective-permute-done.8.refs_4_
  44.0 2.0 %collective-permute-start.13 = (f32[8,256]{1,0:T(8,128)S(1)}, f32[8,256]{1,0:T(8,128)S(1)}, u32[]{:S(2)}, u32[]{:S(2)}) collective-permute-start(f32[8,256]{1,0:T(8,128)S(1)} %get-tuple-element.49), channel_id=1, source_target_pairs={{0,21},{1,22},{2,23},{3,20},{4,25},{5,26},{6,27},{7,24},{8,29},{9,... | collective-permute-start | bytes 24584 | tf_op jit(solution)/shard_map/ppermute | solution.py:441
  45.9 9.4 %local_pairs.3 = (f32[16,256]{1,0:T(8,128)S(1)}, f32[16,256]{1,0:T(8,128)S(1)}) custom-call(s32[160,128]{1,0:T(8,128)S(1)} %get-tuple-element.27.refs_0_, s32[160,128]{1,0:T(8,128)S(1)} %get-tuple-element.28.refs_1_, s32[160,128]{1,0:T(8,128)S(1)} %get-tuple-element.29.refs_2_, bf16[160,256]{1,0:T(8,128)(2,1)S(1)} %get-tuple-element.30.refs_3_, ...), custom_call_target="tpu_custom_call" | custom-call | flops 4096000000 | bytes 122880 | tf_op jit(solution)/shard_map/local_pairs/pallas_call | solution.py:525
  55.3 0.0 collective-permute-done.9.refs_5_
  55.3 0.0 collective-permute-done.10.refs_6_
  55.3 0.0 collective-permute-done.11.refs_7_
  55.3 0.0 collective-permute-done.12.refs_8_
  55.3 0.0 collective-permute-done.13.refs_9_
  55.4 0.8 %totals.1 = (f32[3,512]{1,0:T(4,128)}, f32[1,512]{1,0:T(1,128)}) custom-call(f32[16,256]{1,0:T(8,128)S(1)} %get-tuple-element.40.refs_0_, f32[16,256]{1,0:T(8,128)S(1)} %get-tuple-element.41.refs_1_, s32[1,256]{1,0:T(1,128)S(1)} %get-tuple-element.42.refs_2_, f32[8,256]{1,0:T(8,128)S(1)} %collective-permute-done.7.refs_3_, ...), custom_call_target="tpu_custom_call" | custom-call | tf_op jit(solution)/shard_map/totals/pallas_call | solution.py:551
Async XLA Ops:
  2.4 8.8 %collective-permute-start.6 = (bf16[80,256]{1,0:T(8,128)(2,1)S(1)}, bf16[80,256]{1,0:T(8,128)(2,1)S(1)}, u32[]{:S(2)}, u32[]{:S(2)}) collective-permute-start(bf16[80,256]{1,0:T(8,128)(2,1)S(1)} %get-tuple-element.37), channel_id=1, source_target_pairs={{0,31},{1,28},{2,29},{3,30},{4,19},{5,16},{6,17},{7,18},{8,23},{9,... | collective-permute-start | bytes 122888 | tf_op jit(solution)/shard_map/ppermute | solution.py:441
  8.8 3.4 %collective-permute-start.5 = (bf16[80,256]{1,0:T(8,128)(2,1)S(1)}, bf16[80,256]{1,0:T(8,128)(2,1)S(1)}, u32[]{:S(2)}, u32[]{:S(2)}) collective-permute-start(bf16[80,256]{1,0:T(8,128)(2,1)S(1)} %get-tuple-element.37), channel_id=1, source_target_pairs={{0,15},{1,12},{2,13},{3,14},{4,3},{5,0},{6,1},{7,2},{8,7},{9,4},{1... | collective-permute-start | bytes 122888 | tf_op jit(solution)/shard_map/ppermute | solution.py:441
  9.5 12.6 %collective-permute-start.4 = (bf16[80,256]{1,0:T(8,128)(2,1)S(1)}, bf16[80,256]{1,0:T(8,128)(2,1)S(1)}, u32[]{:S(2)}, u32[]{:S(2)}) collective-permute-start(bf16[80,256]{1,0:T(8,128)(2,1)S(1)} %get-tuple-element.37), channel_id=1, source_target_pairs={{0,19},{1,16},{2,17},{3,18},{16,3},{17,0},{18,1},{19,2},{4,23},{5,... | collective-permute-start | bytes 122888 | tf_op jit(solution)/shard_map/ppermute | solution.py:441
  10.0 12.2 %collective-permute-start.3 = (bf16[80,256]{1,0:T(8,128)(2,1)S(1)}, bf16[80,256]{1,0:T(8,128)(2,1)S(1)}, u32[]{:S(2)}, u32[]{:S(2)}) collective-permute-start(bf16[80,256]{1,0:T(8,128)(2,1)S(1)} %get-tuple-element.37), channel_id=1, source_target_pairs={{0,28},{4,16},{8,20},{12,24},{16,12},{20,0},{24,4},{28,8},{1,29},{... | collective-permute-start | bytes 122888 | tf_op jit(solution)/shard_map/ppermute | solution.py:441
  10.7 11.4 %collective-permute-start.2 = (bf16[80,256]{1,0:T(8,128)(2,1)S(1)}, bf16[80,256]{1,0:T(8,128)(2,1)S(1)}, u32[]{:S(2)}, u32[]{:S(2)}) collective-permute-start(bf16[80,256]{1,0:T(8,128)(2,1)S(1)} %get-tuple-element.37), channel_id=1, source_target_pairs={{0,3},{1,0},{2,1},{3,2},{4,7},{5,4},{6,5},{7,6},{8,11},{9,8},{10,9... | collective-permute-start | bytes 122888 | tf_op jit(solution)/shard_map/ppermute | solution.py:441
  11.2 11.0 %collective-permute-start.1 = (bf16[80,256]{1,0:T(8,128)(2,1)S(1)}, bf16[80,256]{1,0:T(8,128)(2,1)S(1)}, u32[]{:S(2)}, u32[]{:S(2)}) collective-permute-start(bf16[80,256]{1,0:T(8,128)(2,1)S(1)} %get-tuple-element.37), channel_id=1, source_target_pairs={{0,12},{4,0},{8,4},{12,8},{1,13},{5,1},{9,5},{13,9},{2,14},{6,2},{... | collective-permute-start | bytes 122888 | tf_op jit(solution)/shard_map/ppermute | solution.py:441
  12.2 10.0 %collective-permute-start = (bf16[80,256]{1,0:T(8,128)(2,1)S(1)}, bf16[80,256]{1,0:T(8,128)(2,1)S(1)}, u32[]{:S(2)}, u32[]{:S(2)}) collective-permute-start(bf16[80,256]{1,0:T(8,128)(2,1)S(1)} %get-tuple-element.37), channel_id=1, source_target_pairs={{0,16},{16,0},{1,17},{17,1},{2,18},{18,2},{3,19},{19,3},{4,20},{20... | collective-permute-start | bytes 122888 | tf_op jit(solution)/shard_map/ppermute | solution.py:441
  12.8 9.4 %copy-start = (s32[12288]{0:T(1024)S(1)}, s32[12288]{0:T(1024)}, u32[]{:S(2)}) copy-start(s32[12288]{0:T(1024)} %param.31) | copy-start | bytes 147460
  12.8 9.4 %copy-start.1 = (s32[12288]{0:T(1024)S(1)}, s32[12288]{0:T(1024)}, u32[]{:S(2)}) copy-start(s32[12288]{0:T(1024)} %param.32) | copy-start | bytes 147460
  12.8 9.5 %copy-start.2 = (s32[12288]{0:T(1024)S(1)}, s32[12288]{0:T(1024)}, u32[]{:S(2)}) copy-start(s32[12288]{0:T(1024)} %param.33) | copy-start | bytes 147460
  36.2 6.8 %collective-permute-start.7 = (f32[8,256]{1,0:T(8,128)S(1)}, f32[8,256]{1,0:T(8,128)S(1)}, u32[]{:S(2)}, u32[]{:S(2)}) collective-permute-start(f32[8,256]{1,0:T(8,128)S(1)} %get-tuple-element.43), channel_id=1, source_target_pairs={{0,16},{16,0},{1,17},{17,1},{2,18},{18,2},{3,19},{19,3},{4,20},{20... | collective-permute-start | bytes 24584 | tf_op jit(solution)/shard_map/ppermute | solution.py:441
  37.8 6.2 %collective-permute-start.8 = (f32[8,256]{1,0:T(8,128)S(1)}, f32[8,256]{1,0:T(8,128)S(1)}, u32[]{:S(2)}, u32[]{:S(2)}) collective-permute-start(f32[8,256]{1,0:T(8,128)S(1)} %get-tuple-element.44), channel_id=1, source_target_pairs={{0,4},{4,8},{8,12},{12,0},{1,5},{5,9},{9,13},{13,1},{2,6},{6,10},{... | collective-permute-start | bytes 24584 | tf_op jit(solution)/shard_map/ppermute | solution.py:441
  37.8 17.5 %collective-permute-start.9 = (f32[8,256]{1,0:T(8,128)S(1)}, f32[8,256]{1,0:T(8,128)S(1)}, u32[]{:S(2)}, u32[]{:S(2)}) collective-permute-start(f32[8,256]{1,0:T(8,128)S(1)} %get-tuple-element.45), channel_id=1, source_target_pairs={{0,1},{1,2},{2,3},{3,0},{4,5},{5,6},{6,7},{7,4},{8,9},{9,10},{10,1... | collective-permute-start | bytes 24584 | tf_op jit(solution)/shard_map/ppermute | solution.py:441
  38.9 16.4 %collective-permute-start.10 = (f32[8,256]{1,0:T(8,128)S(1)}, f32[8,256]{1,0:T(8,128)S(1)}, u32[]{:S(2)}, u32[]{:S(2)}) collective-permute-start(f32[8,256]{1,0:T(8,128)S(1)} %get-tuple-element.46), channel_id=1, source_target_pairs={{0,20},{4,24},{8,28},{12,16},{16,4},{20,8},{24,12},{28,0},{1,21},{... | collective-permute-start | bytes 24584 | tf_op jit(solution)/shard_map/ppermute | solution.py:441
  40.4 14.9 %collective-permute-start.11 = (f32[8,256]{1,0:T(8,128)S(1)}, f32[8,256]{1,0:T(8,128)S(1)}, u32[]{:S(2)}, u32[]{:S(2)}) collective-permute-start(f32[8,256]{1,0:T(8,128)S(1)} %get-tuple-element.47), channel_id=1, source_target_pairs={{0,17},{1,18},{2,19},{3,16},{16,1},{17,2},{18,3},{19,0},{4,21},{5,... | collective-permute-start | bytes 24584 | tf_op jit(solution)/shard_map/ppermute | solution.py:441
  42.9 12.4 %collective-permute-start.12 = (f32[8,256]{1,0:T(8,128)S(1)}, f32[8,256]{1,0:T(8,128)S(1)}, u32[]{:S(2)}, u32[]{:S(2)}) collective-permute-start(f32[8,256]{1,0:T(8,128)S(1)} %get-tuple-element.48), channel_id=1, source_target_pairs={{0,5},{1,6},{2,7},{3,4},{4,9},{5,10},{6,11},{7,8},{8,13},{9,14},{1... | collective-permute-start | bytes 24584 | tf_op jit(solution)/shard_map/ppermute | solution.py:441
  44.0 11.4 %collective-permute-start.13 = (f32[8,256]{1,0:T(8,128)S(1)}, f32[8,256]{1,0:T(8,128)S(1)}, u32[]{:S(2)}, u32[]{:S(2)}) collective-permute-start(f32[8,256]{1,0:T(8,128)S(1)} %get-tuple-element.49), channel_id=1, source_target_pairs={{0,21},{1,22},{2,23},{3,20},{4,25},{5,26},{6,27},{7,24},{8,29},{9,... | collective-permute-start | bytes 24584 | tf_op jit(solution)/shard_map/ppermute | solution.py:441

commit v4 on v3

--- a/solution.py
+++ b/solution.py
@@ -12,7 +12,8 @@
 domain_edge = 1.0
 ghost_offsets = ((1, 0, 0), (0, 1, 0), (0, 0, 1), (1, 1, 0), (1, 0, 1), (0, 1, 1), (1, 1, 1))
 
-EXTRA = 16
+EXTRA = 8
+OFFERED = 16
 GROUP = 256
 LANES = 128
 CHUNK = 256
@@ -36,8 +37,18 @@
     return lax.broadcasted_iota(jnp.int32, shape, dim)
 
 
-def one_hot(row, count):
-    return jnp.where(iota((count, row.shape[1]), 0) == row, 1.0, 0.0).astype(bf16)
+def one_hot(row, codes):
+    entry = jnp.broadcast_to(row.astype(f32), (16, row.shape[1])).astype(bf16)
+    entry = jnp.concatenate([entry] * (codes.shape[0] // 16), 0)
+    pieces = [
+        jnp.where(codes == entry[:, start : start + LANES], bf16(1), bf16(0))
+        for start in range(0, row.shape[1], LANES)
+    ]
+    return jnp.concatenate(pieces, 1)
+
+
+def row_codes(count):
+    return iota((count, LANES), 0).astype(f32).astype(bf16)
 
 
 def split_two(value):
@@ -47,8 +58,7 @@
 
 def coord_rows(coords, gain):
     high, low = split_two(coords)
-    none = jnp.zeros((1, coords.shape[1]), f32)
-    return jnp.concatenate([high, none, gain, none, none, none, low, none, none, none, none, none], 0)
+    return jnp.concatenate([high, gain, low, jnp.zeros_like(gain)], 0)
 
 
 def eye(count):
@@ -83,29 +93,27 @@
     ) = targets[:11]
     channels = features_ref.shape[0]
     count = features_ref.shape[1]
-    rows = channels + EXTRA
     species = species_ref[...]
     gain = jnp.zeros((1, count), f32)
     for kind in range(scale_ref.shape[1]):
         scale = scale_ref[:, kind : kind + 1].astype(f32)
         gain = jnp.where(species == kind, scale, gain)
-    extra = coord_rows(positions_ref[...], gain).astype(bf16)
+    positions = positions_ref[...]
     left = dot(w_first_ref[...], features_ref[...]).astype(bf16).astype(f32)
     right = dot(w_second_ref[...], features_ref[...]).astype(bf16).astype(f32)
-    left = (0.5 * left).astype(bf16)
-    right = (0.5 * right).astype(bf16)
-    groups = count // GROUP
-    for group in range(groups):
-        cols = slice(group * GROUP, (group + 1) * GROUP)
-        own_ref[group * rows : group * rows + channels, :] = left[:, cols]
-        own_ref[group * rows + channels : (group + 1) * rows, :] = extra[:, cols]
-        right_ref[group * rows : group * rows + channels, :] = right[:, cols]
-        right_ref[group * rows + channels : (group + 1) * rows, :] = extra[:, cols]
+    place = jnp.concatenate([positions, gain, jnp.zeros((EXTRA - 4, count), f32)], 0)
+    own_ref[0:channels, :] = 0.5 * left
+    own_ref[channels:, :] = place
+    right_ref[0:channels, :] = 0.5 * right
+    right_ref[channels:, :] = place
+    parts = coord_rows(positions, gain)
+    table = jnp.concatenate([0.5 * right, parts, jnp.zeros_like(parts)], 0).astype(bf16)
     send = send_ref[...]
-    picked = dot(right_ref[...], one_hot(send & (GROUP - 1), GROUP))
-    chosen = picked[:rows]
-    for group in range(1, groups):
-        chosen = jnp.where(send // GROUP == group, picked[group * rows : (group + 1) * rows], chosen)
+    hot = one_hot(send & (GROUP - 1), row_codes(GROUP))
+    chosen = dot(table[:, 0:GROUP], hot)
+    for group in range(1, count // GROUP):
+        picked = dot(table[:, group * GROUP : (group + 1) * GROUP], hot)
+        chosen = jnp.where(send // GROUP == group, picked, chosen)
     offered_ref[...] = chosen.astype(bf16)
 
     unit = eye(channels)
@@ -145,9 +153,19 @@
 
 def spread_groups(values, high, groups):
     pieces = [jnp.where(high == group, values, 0.0) for group in range(groups)]
-    if groups % 2:
-        pieces.append(jnp.zeros_like(values))
     return jnp.concatenate(pieces, 0).astype(bf16)
+
+
+def lane_pick(table_ref, row):
+    rows, count = table_ref.shape
+    lane = jnp.broadcast_to(row & (LANES - 1), (rows, LANES))
+    high = row // LANES
+    chosen = None
+    for group in range(count // LANES):
+        part = table_ref[:, group * LANES : (group + 1) * LANES]
+        picked = jnp.take_along_axis(part, lane, axis=1, mode="promise_in_bounds")
+        chosen = picked if chosen is None else jnp.where(high == group, picked, chosen)
+    return chosen
 
 
 def pair_body(
@@ -167,12 +185,12 @@
     radial_ref,
     radial_t_ref,
     out_ref,
-    own_acc,
-    partner_acc,
-    hot_own,
-    hot_partner,
+    sums,
+    hot,
+    hot_wide,
     slope_one,
     slope_two,
+    codes_ref,
 ):
     rows = channels + EXTRA
     line = CHUNK // LANES
@@ -183,6 +201,7 @@
     centers = iota((bases, CHUNK), 0).astype(f32) * (1.0 / (bases - 1))
     sub = iota((8, CHUNK), 0)
     quads = range(QUAD)
+    codes_ref[...] = row_codes(GROUP)
 
     def matrix(place):
         return mats_ref[place * wide : (place + 1) * wide, :]
@@ -212,26 +231,43 @@
             cols = slice(quad * CHUNK, (quad + 1) * CHUNK)
             owner = row_of(owner_rows, quad)
             partner = row_of(partner_rows, quad)
-            own_high.append(owner // GROUP)
-            partner_high.append(partner // GROUP)
-            hot_own[number, :, cols] = one_hot(owner & (GROUP - 1), GROUP)
-            hot_partner[number, :, cols] = one_hot(partner & (GROUP - 1), GROUP)
+            own_high.append(owner // LANES)
+            partner_high.append(partner // LANES)
+            hot[number, 0:LANES, cols] = one_hot(owner & (LANES - 1), codes_ref[0:LANES, :])
+            if hot_wide is None:
+                hot[number, LANES:, cols] = one_hot(partner & (LANES - 1), codes_ref[0:LANES, :])
+            else:
+                both = one_hot(partner & (GROUP - 1), codes_ref[...])
+                hot_wide[number, :, cols] = both
+                hot[number, LANES:, cols] = both[0:LANES] + both[LANES:]
             yield
         for quad in quads:
             cols = slice(quad * CHUNK, (quad + 1) * CHUNK)
-            own_vals = group_pick(
-                dot(own_ref[...], hot_own[number, :, cols]), own_high[quad], rows, own_groups
-            )
-            partner_vals = group_pick(
-                dot(right_ref[...], hot_partner[number, :, cols]), partner_high[quad], rows, partner_groups
-            )
+            pieces = []
+            for piece in range(line):
+                at_row = quad * line + piece
+                pieces.append(lane_pick(own_ref, owner_rows[at_row : at_row + 1, :]))
+            own_vals = jnp.concatenate(pieces, 1)
+            if hot_wide is None:
+                pieces = []
+                for piece in range(line):
+                    at_row = quad * line + piece
+                    pieces.append(lane_pick(right_ref, partner_rows[at_row : at_row + 1, :]))
+                partner_vals = jnp.concatenate(pieces, 1)
+                partner_coords = partner_vals[channels:]
+            else:
+                wide_high = row_of(partner_rows, quad) // GROUP
+                partner_vals = group_pick(
+                    dot(right_ref[...], hot_wide[number, :, cols]), wide_high, rows, partner_groups * LANES // GROUP
+                )
+                extra = partner_vals[channels:]
+                partner_coords = extra + jnp.concatenate([extra[4:], extra[:4]], 0)
             projected.append(own_vals[:channels] + partner_vals[:channels])
-            own_coords = own_vals[channels : channels + 8] + own_vals[channels + 8 :]
-            partner_coords = partner_vals[channels : channels + 8] + partner_vals[channels + 8 :]
+            own_coords = own_vals[channels:]
             shift = partner_coords - own_coords
             square = shift * shift
             squared = square[0:1] + square[1:2] + square[2:3]
-            weights.append(row_of(live_rows, quad) * own_coords[4:5] * partner_coords[4:5])
+            weights.append(row_of(live_rows, quad) * own_coords[3:4] * partner_coords[3:4])
             away = squared - centers
             basis = jnp.exp(-basis_width * (away * away))
             basis_high, basis_low = split_two(basis)
@@ -271,8 +307,7 @@
         pieces = [(part(back, quad) * slope_one[number, quad]).astype(bf16) for quad in quads]
         back = dot(radial_t_ref[...], jnp.concatenate(pieces, 0))
         yield
-        own_parts = []
-        partner_parts = []
+        parts = []
         for quad in quads:
             two = part(back, quad, 2 * bases)
             readout_slope = jnp.sum((two[:bases] + two[bases:]) * slopes[quad], axis=0, keepdims=True)
@@ -283,11 +318,15 @@
             push = (2.0 * slope) * shifts[quad]
             high, low = split_two(jnp.where(sub == 3, energy, push))
             values = jnp.concatenate([high[:4], low[:4]], 0)
-            own_parts.append(spread_groups(values, own_high[quad], own_groups))
-            partner_parts.append(spread_groups(values, partner_high[quad], partner_groups))
-        yield
-        own_acc[...] += dot_nt(jnp.concatenate(own_parts, 1), hot_own[number])
-        partner_acc[...] += dot_nt(jnp.concatenate(partner_parts, 1), hot_partner[number])
+            parts.append(
+                jnp.concatenate(
+                    [jnp.where(own_high[quad] == group, values, 0.0) for group in range(own_groups)]
+                    + [jnp.where(partner_high[quad] == group, values, 0.0) for group in range(partner_groups)],
+                    0,
+                ).astype(bf16)
+            )
+        yield
+        sums[...] += dot_nt(jnp.concatenate(parts, 1), hot[number])
 
     def step(index, unused):
         base = pl.multiple_of(first_row + index * (per_step * block), block)
@@ -304,17 +343,11 @@
 
 
 def local_kernel(per_step, channels, bases, first_row, row_count, with_start, *refs):
-    if with_start:
-        (owner, partner, mask, own, right, mats, radial, radial_t, out, own_in, partner_in) = refs[:11]
-        own_acc, partner_acc, *scratch = refs[11:]
-        own_acc[...] = own_in[...]
-        partner_acc[...] = partner_in[...]
-    else:
-        (owner, partner, mask, own, right, mats, radial, radial_t, out) = refs[:9]
-        own_acc, partner_acc, *scratch = refs[9:]
-        own_acc[...] = jnp.zeros_like(own_acc)
-        partner_acc[...] = jnp.zeros_like(partner_acc)
-    groups = own.shape[0] // (channels + EXTRA)
+    count = 9 + with_start
+    owner, partner, mask, own, right, *weights = refs[:9]
+    sums, hot, *scratch = refs[count:]
+    sums[...] = refs[9][...] if with_start else jnp.zeros_like(sums)
+    groups = own.shape[1] // LANES
     pair_body(
         per_step,
         first_row,
@@ -328,42 +361,40 @@
         mask,
         own,
         right,
-        mats,
-        radial,
-        radial_t,
-        out,
-        own_acc,
-        partner_acc,
+        *weights,
+        sums,
+        hot,
+        None,
         *scratch,
     )
 
 
 def ghost_kernel(per_step, channels, bases, *refs):
     blocks = len(ghost_offsets)
-    (owner, partner, mask, own, mats, radial, radial_t, out, own_in) = refs[:9]
+    owner, partner, mask, own, *weights = refs[:8]
+    sums_in = refs[8]
     arrived = refs[9 : 9 + blocks]
-    own_acc = refs[9 + blocks]
+    sums_out = refs[9 + blocks]
     forces = refs[10 + blocks : 10 + 2 * blocks]
-    table, partner_acc, *scratch = refs[10 + 2 * blocks :]
-    rows = channels + EXTRA
-    groups = own.shape[0] // rows
-    own_acc[...] = own_in[...]
-    partner_acc[...] = jnp.zeros_like(partner_acc)
+    table, sums, *scratch = refs[10 + 2 * blocks :]
+    groups = own.shape[1] // LANES
+    partner_groups = blocks * GROUP // LANES
+    sums[...] = jnp.zeros_like(sums)
+    pieces = []
     for block, offset in enumerate(ghost_offsets):
-        start = block * rows
-        table[start : start + channels, :] = arrived[block][0:channels, :]
-        extra = arrived[block][channels:rows, :].astype(f32)
-        coords = extra[0:8] + extra[8:16]
+        extra = arrived[block][channels : channels + OFFERED, :].astype(f32)
         moved = jnp.concatenate(
-            [coords[axis : axis + 1] + domain_edge * offset[axis] for axis in range(3)], 0
+            [extra[axis : axis + 1] + extra[axis + 4 : axis + 5] + domain_edge * offset[axis] for axis in range(3)], 0
         )
-        table[start + channels : start + rows, :] = coord_rows(moved, coords[4:5]).astype(bf16)
+        pieces += [arrived[block][0:channels, :].astype(f32), coord_rows(moved, extra[3:4])]
+    pieces.append(jnp.zeros((table.shape[0] - blocks * (channels + EXTRA), GROUP), f32))
+    table[...] = jnp.concatenate(pieces, 0).astype(bf16)
     pair_body(
         per_step,
         0,
         owner.shape[0],
         groups,
-        blocks,
+        partner_groups,
         channels,
         bases,
         owner,
@@ -371,39 +402,41 @@
         mask,
         own,
         table,
-        mats,
-        radial,
-        radial_t,
-        out,
-        own_acc,
-        partner_acc,
+        *weights,
+        sums,
         *scratch,
     )
+    first = groups * 8
+    sums_out[0:first, :] = sums_in[0:first, :] + sums[0:first, :]
+    sums_out[first:, :] = sums_in[first:, :]
     for block in range(blocks):
-        both = partner_acc[block * 8 : block * 8 + 8, :]
-        forces[block][...] = -(both + jnp.concatenate([both[4:], both[:4]], 0))
+        for half in range(GROUP // LANES):
+            start = first + (block * (GROUP // LANES) + half) * 8
+            both = sums[start : start + 8, LANES:]
+            forces[block][:, half * LANES : (half + 1) * LANES] = -(
+                both + jnp.concatenate([both[4:], both[:4]], 0)
+            )
 
 
 def final_kernel(blocks, *refs):
-    own_ref, partner_ref, send_ref = refs[:3]
-    arrived = refs[3 : 3 + blocks]
-    forces_ref, energy_ref = refs[3 + blocks :]
+    sums_ref, send_ref = refs[:2]
+    arrived = refs[2 : 2 + blocks]
+    forces_ref, energy_ref = refs[2 + blocks :]
     incoming = arrived[0][...]
     for block in range(1, blocks):
         incoming = incoming + arrived[block][...]
     high, low = split_two(incoming[:4])
     send = send_ref[...]
-    groups = own_ref.shape[0] // 8
-    values = spread_groups(jnp.concatenate([high, low], 0), send // GROUP, groups)
-    back = dot_nt(values, one_hot(send & (GROUP - 1), GROUP))
+    groups = sums_ref.shape[0] // 16
+    values = spread_groups(jnp.concatenate([high, low], 0), send // LANES, groups)
+    back = dot_nt(values, one_hot(send & (LANES - 1), row_codes(LANES)))
     for group in range(groups):
-        part = slice(group * 8, group * 8 + 8)
-        total = own_ref[part, :] - partner_ref[part, :] + back[part]
-        total = total[:4] + total[4:]
-        cols = slice(group * GROUP, (group + 1) * GROUP)
-        forces_ref[:, cols] = total[:3]
-        energy = own_ref[group * 8 + 3 : group * 8 + 4, :] + own_ref[group * 8 + 7 : group * 8 + 8, :]
-        energy_ref[:, cols] = energy
+        own = sums_ref[group * 8 : group * 8 + 8, 0:LANES]
+        partner = sums_ref[(groups + group) * 8 : (groups + group) * 8 + 8, LANES:]
+        total = own - partner + back[group * 8 : group * 8 + 8]
+        cols = slice(group * LANES, (group + 1) * LANES)
+        forces_ref[:, cols] = total[0:3] + total[4:7]
+        energy_ref[:, cols] = own[3:4] + own[7:8]
 
 
 def whole(shape, dtype):
@@ -465,7 +498,7 @@
     send_count = ghost_send.shape[0]
     bases = w_radial.shape[1]
     rows = channels + EXTRA
-    groups = own_count // GROUP
+    groups = own_count // LANES
     blocks = len(ghost_offsets)
     send = ghost_send.reshape(1, send_count)
     whole_spec = pl.BlockSpec(memory_space=pltpu.VMEM)
@@ -488,9 +521,9 @@
     own, right, offered, mats, radial, radial_t, out, send, *local = call(
         prep_kernel,
         (
-            whole((groups * rows, GROUP), bf16),
-            whole((groups * rows, GROUP), bf16),
-            whole((rows, send_count), bf16),
+            whole((rows, own_count), f32),
+            whole((rows, own_count), f32),
+            whole((channels + OFFERED, send_count), bf16),
             whole((4 * QUAD * channels, QUAD * channels), bf16),
             whole((QUAD * channels, QUAD * 4 * bases), bf16),
             whole((QUAD * 2 * bases, QUAD * channels), bf16),
@@ -504,12 +537,11 @@
     )(*[pltpu.with_memory_space_constraint(value, pltpu.HBM) for value in (*small, *lists)])
     arrived = [shifted(offered, offset, sizes, 1) for offset in ghost_offsets]
 
-    def scratch(per_step):
-        return [
-            pltpu.VMEM((per_step, GROUP, QUAD * CHUNK), bf16),
-            pltpu.VMEM((per_step, GROUP, QUAD * CHUNK), bf16),
+    def scratch(per_step, hots):
+        return [pltpu.VMEM((per_step, GROUP, QUAD * CHUNK), bf16) for _ in range(hots)] + [
             pltpu.VMEM((per_step, QUAD, channels, CHUNK), f32),
             pltpu.VMEM((per_step, QUAD, channels, CHUNK), f32),
+            pltpu.VMEM((GROUP, LANES), bf16),
         ]
 
     def cost(slots):
@@ -522,38 +554,40 @@
 
     def local_call(part, start):
         operands = [*local, own, right, *weights, *start]
-        return call(
-            functools.partial(local_kernel, local_step, channels, bases, part * part_rows, part_rows, bool(start)),
-            (whole((groups * 8, GROUP), f32), whole((groups * 8, GROUP), f32)),
+        (sums,) = call(
+            functools.partial(
+                local_kernel, local_step, channels, bases, part * part_rows, part_rows, len(start)
+            ),
+            (whole((groups * 16, GROUP), f32),),
             "local_pairs",
-            scratch(local_step),
+            scratch(local_step, 1),
             [whole_spec] * len(operands),
             cost(part_rows * LANES),
         )(*operands)
-
-    own_sum, partner_sum = local_call(0, ())
+        return sums
+
+    sums = local_call(0, ())
     ghost_lists = [tiles(value) for value in (ghost_owner, ghost_index, ghost_mask)]
     ghost_step = ghost_owner.shape[0] // (QUAD * CHUNK)
-    own_sum, *ghost_forces = call(
+    partner_rows = blocks * GROUP // LANES * 8
+    table_rows = -(-blocks * rows // 16) * 16
+    sums, *ghost_forces = call(
         functools.partial(ghost_kernel, ghost_step, channels, bases),
-        (whole((groups * 8, GROUP), f32),) + (whole((8, send_count), f32),) * blocks,
+        (whole((groups * 16, GROUP), f32),) + (whole((8, send_count), f32),) * blocks,
         "ghost_pairs",
-        [
-            pltpu.VMEM((blocks * rows, GROUP), bf16),
-            pltpu.VMEM(((blocks + blocks % 2) * 8, GROUP), f32),
-        ]
-        + scratch(ghost_step),
+        [pltpu.VMEM((table_rows, GROUP), bf16), pltpu.VMEM((groups * 8 + partner_rows, GROUP), f32)]
+        + scratch(ghost_step, 2),
         [whole_spec] * (9 + blocks),
         cost(ghost_owner.shape[0]),
-    )(*ghost_lists, own, *weights, own_sum, *arrived)
+    )(*ghost_lists, own, *weights, sums, *arrived)
     returned = [shifted(force, offset, sizes, -1) for force, offset in zip(ghost_forces, ghost_offsets)]
-    own_sum, partner_sum = local_call(1, (own_sum, partner_sum))
+    sums = local_call(1, (sums,))
     forces, energy = call(
         functools.partial(final_kernel, blocks),
         (whole((3, own_count), f32), whole((1, own_count), f32)),
         "totals",
-        specs=[whole_spec] * (3 + blocks),
-    )(own_sum, partner_sum, send, *returned)
+        specs=[whole_spec] * (2 + blocks),
+    )(sums, send, *returned)
     return forces, energy.reshape(own_count)
 
 

time: 56.4 us -> 57.7 us (1.023)
  Pallas kernels: 35.2 us -> 36.5 us
    pallas_call x2, Pallas kernels: 18.7 us -> 21.2 us  [local_call(): call(functools.partial(local_kernel, local_step, channels, bases, part *...]
    pallas_call x1, Pallas kernels: 13.9 us -> 12.7 us  [on_device(): call(functools.partial(ghost_kernel, ghost_step, channels, bases), (whole...]
  transfers between devices with their start and end apart: 14 -> 14, of which waited for: 1 -> 1; matrix products, arithmetic and copies ran while one was open for 0% -> 0% of each run, Pallas kernels for 33% -> 37%
where the time goes in v4:
time: 57.7 us; the launch traced here: 57.5 us
  Pallas kernels  36.5 us (63%)
  starting transfers between devices  19.7 us (34%)
  between operations  0.78 us (1%)
    pallas_call x2, Pallas kernels, local_call(): call(functools.partial(local_kernel, local_step, channels, bases, part *...  21.2 us
    ppermute x14, starting transfers between devices, shifted(): return lax.ppermute(value, tuple((name for name, size in used)), pairs)  19.7 us
    pallas_call x1, Pallas kernels, on_device(): call(functools.partial(ghost_kernel, ghost_step, channels, bases), (whole...  12.7 us
    pallas_call x1, Pallas kernels, on_device(): call(prep_kernel, (whole((rows, own_count), f32), whole((rows, own_count)...  1.84 us
  transfers between devices with their start and end apart: 14, of which 1 were waited for; matrix products, arithmetic and copies ran while one was open for 0% of the time, Pallas kernels for 37%

profile of v4, /device:TPU:0, one launch (start us, length us, event | category | flops | bytes accessed | tf_op | source)
XLA Modules:
  0.0 57.5 jit_solution(8484565198042129587)
XLA Ops:
  0.6 1.8 %tables.1 = (f32[72,512]{1,0:T(8,128)S(1)}, f32[72,512]{1,0:T(8,128)S(1)}, bf16[80,256]{1,0:T(8,128)(2,1)S(1)}, bf16[1024,256]{1,0:T(8,128)(2,1)S(1)}, bf16[256,...) custom-call(f32[3,512]{1,0:T(4,128)} %refs_0_.1, ...), custom_call_target="tpu_custom_call" | custom-call | tf_op jit(solution)/shard_map/tables/pallas_call | solution.py:521
  2.5 6.4 %collective-permute-start.6 = (bf16[80,256]{1,0:T(8,128)(2,1)S(1)}, bf16[80,256]{1,0:T(8,128)(2,1)S(1)}, u32[]{:S(2)}, u32[]{:S(2)}) collective-permute-start(bf16[80,256]{1,0:T(8,128)(2,1)S(1)} %get-tuple-element.32), channel_id=1, source_target_pairs={{0,31},{1,28},{2,29},{3,30},{4,19},{5,16},{6,17},{7,18},{8,23},{9,... | collective-permute-start | bytes 122888 | tf_op jit(solution)/shard_map/ppermute | solution.py:474
  8.9 0.7 %collective-permute-start.5 = (bf16[80,256]{1,0:T(8,128)(2,1)S(1)}, bf16[80,256]{1,0:T(8,128)(2,1)S(1)}, u32[]{:S(2)}, u32[]{:S(2)}) collective-permute-start(bf16[80,256]{1,0:T(8,128)(2,1)S(1)} %get-tuple-element.32), channel_id=1, source_target_pairs={{0,15},{1,12},{2,13},{3,14},{4,3},{5,0},{6,1},{7,2},{8,7},{9,4},{1... | collective-permute-start | bytes 122888 | tf_op jit(solution)/shard_map/ppermute | solution.py:474
  9.6 0.4 collective-permute-start.4
  10.1 0.8 %collective-permute-start.3 = (bf16[80,256]{1,0:T(8,128)(2,1)S(1)}, bf16[80,256]{1,0:T(8,128)(2,1)S(1)}, u32[]{:S(2)}, u32[]{:S(2)}) collective-permute-start(bf16[80,256]{1,0:T(8,128)(2,1)S(1)} %get-tuple-element.32), channel_id=1, source_target_pairs={{0,28},{4,16},{8,20},{12,24},{16,12},{20,0},{24,4},{28,8},{1,29},{... | collective-permute-start | bytes 122888 | tf_op jit(solution)/shard_map/ppermute | solution.py:474
  10.8 0.5 collective-permute-start.2
  11.3 0.0 collective-permute-done.6.refs_15_
  11.3 0.7 %collective-permute-start.1 = (bf16[80,256]{1,0:T(8,128)(2,1)S(1)}, bf16[80,256]{1,0:T(8,128)(2,1)S(1)}, u32[]{:S(2)}, u32[]{:S(2)}) collective-permute-start(bf16[80,256]{1,0:T(8,128)(2,1)S(1)} %get-tuple-element.32), channel_id=1, source_target_pairs={{0,12},{4,0},{8,4},{12,8},{1,13},{5,1},{9,5},{13,9},{2,14},{6,2},{... | collective-permute-start | bytes 122888 | tf_op jit(solution)/shard_map/ppermute | solution.py:474
  12.0 0.4 collective-permute-done.5.refs_14_
  12.3 0.5 collective-permute-start
  12.9 0.0 copy-start
  12.9 0.0 copy-start.1
  12.9 0.0 copy-start.2
  12.9 10.6 %local_pairs.2.refs_8_ = f32[64,256]{1,0:T(8,128)S(1)} custom-call(s32[160,128]{1,0:T(8,128)S(1)} %get-tuple-element.23.refs_0_, s32[160,128]{1,0:T(8,128)S(1)} %get-tuple-element.24.refs_1_, s32[160,128]{1,0:T(8,128)S(1)} %get-tuple-element.25.refs_2_, f32[72,512]{1,0:T(8,128)S(1)} %get-tuple-element.26.refs_3_, f32[72,512]{1,0:T(8,128)S(1)} %get-tuple-element.27.refs_4_, ...), custom_call_target="tpu_custom_call" | custom-call | flops 4096000000 | bytes 122880 | tf_op jit(solution)/shard_map/local_pairs/pallas_call | solution.py:557
  23.5 0.0 collective-permute-done.4.refs_13_
  23.5 0.0 collective-permute-done.3.refs_12_
  23.5 0.0 collective-permute-done.2.refs_11_
  23.5 0.0 collective-permute-done.1.refs_10_
  23.5 0.0 collective-permute-done.refs_9_
  23.6 0.0 copy-done
  23.6 0.0 copy-done.1
  23.6 0.0 copy-done.2
  23.6 12.7 %ghost_pairs.1 = (f32[64,256]{1,0:T(8,128)S(1)}, f32[8,256]{1,0:T(8,128)S(1)}, f32[8,256]{1,0:T(8,128)S(1)}, f32[8,256]{1,0:T(8,128)S(1)}, f32[8,256]{1,0:T(8,12...) custom-call(s32[96,128]{1,0:T(8,128)S(1)} %bitcast.12, s32[96,128]{1,0:T(8,128)S(1)} %bitcast.13, ...), custom_call_target="tpu_custom_call" | custom-call | flops 4915200000 | bytes 147456 | tf_op jit(solution)/shard_map/ghost_pairs/pallas_call | solution.py:574
  36.3 1.6 %collective-permute-start.7 = (f32[8,256]{1,0:T(8,128)S(1)}, f32[8,256]{1,0:T(8,128)S(1)}, u32[]{:S(2)}, u32[]{:S(2)}) collective-permute-start(f32[8,256]{1,0:T(8,128)S(1)} %get-tuple-element.35), channel_id=1, source_target_pairs={{0,16},{16,0},{1,17},{17,1},{2,18},{18,2},{3,19},{19,3},{4,20},{20... | collective-permute-start | bytes 24584 | tf_op jit(solution)/shard_map/ppermute | solution.py:474
  37.9 0.1 collective-permute-start.8
  37.9 1.1 %collective-permute-start.9 = (f32[8,256]{1,0:T(8,128)S(1)}, f32[8,256]{1,0:T(8,128)S(1)}, u32[]{:S(2)}, u32[]{:S(2)}) collective-permute-start(f32[8,256]{1,0:T(8,128)S(1)} %get-tuple-element.37), channel_id=1, source_target_pairs={{0,1},{1,2},{2,3},{3,0},{4,5},{5,6},{6,7},{7,4},{8,9},{9,10},{10,1... | collective-permute-start | bytes 24584 | tf_op jit(solution)/shard_map/ppermute | solution.py:474
  39.0 1.5 %collective-permute-start.10 = (f32[8,256]{1,0:T(8,128)S(1)}, f32[8,256]{1,0:T(8,128)S(1)}, u32[]{:S(2)}, u32[]{:S(2)}) collective-permute-start(f32[8,256]{1,0:T(8,128)S(1)} %get-tuple-element.38), channel_id=1, source_target_pairs={{0,20},{4,24},{8,28},{12,16},{16,4},{20,8},{24,12},{28,0},{1,21},{... | collective-permute-start | bytes 24584 | tf_op jit(solution)/shard_map/ppermute | solution.py:474
  40.5 2.5 %collective-permute-start.11 = (f32[8,256]{1,0:T(8,128)S(1)}, f32[8,256]{1,0:T(8,128)S(1)}, u32[]{:S(2)}, u32[]{:S(2)}) collective-permute-start(f32[8,256]{1,0:T(8,128)S(1)} %get-tuple-element.39), channel_id=1, source_target_pairs={{0,17},{1,18},{2,19},{3,16},{16,1},{17,2},{18,3},{19,0},{4,21},{5,... | collective-permute-start | bytes 24584 | tf_op jit(solution)/shard_map/ppermute | solution.py:474
  43.0 0.0 collective-permute-done.7.refs_2_
  43.0 1.0 %collective-permute-start.12 = (f32[8,256]{1,0:T(8,128)S(1)}, f32[8,256]{1,0:T(8,128)S(1)}, u32[]{:S(2)}, u32[]{:S(2)}) collective-permute-start(f32[8,256]{1,0:T(8,128)S(1)} %get-tuple-element.40), channel_id=1, source_target_pairs={{0,5},{1,6},{2,7},{3,4},{4,9},{5,10},{6,11},{7,8},{8,13},{9,14},{1... | collective-permute-start | bytes 24584 | tf_op jit(solution)/shard_map/ppermute | solution.py:474
  44.0 0.0 collective-permute-done.8.refs_3_
  44.1 2.0 %collective-permute-start.13 = (f32[8,256]{1,0:T(8,128)S(1)}, f32[8,256]{1,0:T(8,128)S(1)}, u32[]{:S(2)}, u32[]{:S(2)}) collective-permute-start(f32[8,256]{1,0:T(8,128)S(1)} %get-tuple-element.41), channel_id=1, source_target_pairs={{0,21},{1,22},{2,23},{3,20},{4,25},{5,26},{6,27},{7,24},{8,29},{9,... | collective-permute-start | bytes 24584 | tf_op jit(solution)/shard_map/ppermute | solution.py:474
  46.0 10.6 %local_pairs.3.refs_0_ = f32[64,256]{1,0:T(8,128)S(1)} custom-call(s32[160,128]{1,0:T(8,128)S(1)} %get-tuple-element.23.refs_0_, s32[160,128]{1,0:T(8,128)S(1)} %get-tuple-element.24.refs_1_, s32[160,128]{1,0:T(8,128)S(1)} %get-tuple-element.25.refs_2_, f32[72,512]{1,0:T(8,128)S(1)} %get-tuple-element.26.refs_3_, f32[72,512]{1,0:T(8,128)S(1)} %get-tuple-element.27.refs_4_, ...), custom_call_target="tpu_custom_call" | custom-call | flops 4096000000 | bytes 122880 | tf_op jit(solution)/shard_map/local_pairs/pallas_call | solution.py:557
  56.7 0.0 collective-permute-done.9.refs_4_
  56.7 0.0 collective-permute-done.10.refs_5_
  56.7 0.0 collective-permute-done.11.refs_6_
  56.7 0.0 collective-permute-done.12.refs_7_
  56.7 0.0 collective-permute-done.13.refs_8_
  56.7 0.8 %totals.1 = (f32[3,512]{1,0:T(4,128)}, f32[1,512]{1,0:T(1,128)}) custom-call(f32[64,256]{1,0:T(8,128)S(1)} %local_pairs.3.refs_0_, s32[1,256]{1,0:T(1,128)S(1)} %get-tuple-element.34.refs_1_, f32[8,256]{1,0:T(8,128)S(1)} %collective-permute-done.7.refs_2_, f32[8,256]{1,0:T(8,128)S(1)} %collective-permute-done.8.refs_3_, ...), custom_call_target="tpu_custom_call" | custom-call | tf_op jit(solution)/shard_map/totals/pallas_call | solution.py:585
Async XLA Ops:
  2.5 8.8 %collective-permute-start.6 = (bf16[80,256]{1,0:T(8,128)(2,1)S(1)}, bf16[80,256]{1,0:T(8,128)(2,1)S(1)}, u32[]{:S(2)}, u32[]{:S(2)}) collective-permute-start(bf16[80,256]{1,0:T(8,128)(2,1)S(1)} %get-tuple-element.32), channel_id=1, source_target_pairs={{0,31},{1,28},{2,29},{3,30},{4,19},{5,16},{6,17},{7,18},{8,23},{9,... | collective-permute-start | bytes 122888 | tf_op jit(solution)/shard_map/ppermute | solution.py:474
  8.9 3.4 %collective-permute-start.5 = (bf16[80,256]{1,0:T(8,128)(2,1)S(1)}, bf16[80,256]{1,0:T(8,128)(2,1)S(1)}, u32[]{:S(2)}, u32[]{:S(2)}) collective-permute-start(bf16[80,256]{1,0:T(8,128)(2,1)S(1)} %get-tuple-element.32), channel_id=1, source_target_pairs={{0,15},{1,12},{2,13},{3,14},{4,3},{5,0},{6,1},{7,2},{8,7},{9,4},{1... | collective-permute-start | bytes 122888 | tf_op jit(solution)/shard_map/ppermute | solution.py:474
  9.6 13.9 %collective-permute-start.4 = (bf16[80,256]{1,0:T(8,128)(2,1)S(1)}, bf16[80,256]{1,0:T(8,128)(2,1)S(1)}, u32[]{:S(2)}, u32[]{:S(2)}) collective-permute-start(bf16[80,256]{1,0:T(8,128)(2,1)S(1)} %get-tuple-element.32), channel_id=1, source_target_pairs={{0,19},{1,16},{2,17},{3,18},{16,3},{17,0},{18,1},{19,2},{4,23},{5,... | collective-permute-start | bytes 122888 | tf_op jit(solution)/shard_map/ppermute | solution.py:474
  10.1 13.5 %collective-permute-start.3 = (bf16[80,256]{1,0:T(8,128)(2,1)S(1)}, bf16[80,256]{1,0:T(8,128)(2,1)S(1)}, u32[]{:S(2)}, u32[]{:S(2)}) collective-permute-start(bf16[80,256]{1,0:T(8,128)(2,1)S(1)} %get-tuple-element.32), channel_id=1, source_target_pairs={{0,28},{4,16},{8,20},{12,24},{16,12},{20,0},{24,4},{28,8},{1,29},{... | collective-permute-start | bytes 122888 | tf_op jit(solution)/shard_map/ppermute | solution.py:474
  10.8 12.7 %collective-permute-start.2 = (bf16[80,256]{1,0:T(8,128)(2,1)S(1)}, bf16[80,256]{1,0:T(8,128)(2,1)S(1)}, u32[]{:S(2)}, u32[]{:S(2)}) collective-permute-start(bf16[80,256]{1,0:T(8,128)(2,1)S(1)} %get-tuple-element.32), channel_id=1, source_target_pairs={{0,3},{1,0},{2,1},{3,2},{4,7},{5,4},{6,5},{7,6},{8,11},{9,8},{10,9... | collective-permute-start | bytes 122888 | tf_op jit(solution)/shard_map/ppermute | solution.py:474
  11.3 12.3 %collective-permute-start.1 = (bf16[80,256]{1,0:T(8,128)(2,1)S(1)}, bf16[80,256]{1,0:T(8,128)(2,1)S(1)}, u32[]{:S(2)}, u32[]{:S(2)}) collective-permute-start(bf16[80,256]{1,0:T(8,128)(2,1)S(1)} %get-tuple-element.32), channel_id=1, source_target_pairs={{0,12},{4,0},{8,4},{12,8},{1,13},{5,1},{9,5},{13,9},{2,14},{6,2},{... | collective-permute-start | bytes 122888 | tf_op jit(solution)/shard_map/ppermute | solution.py:474
  12.3 11.2 %collective-permute-start = (bf16[80,256]{1,0:T(8,128)(2,1)S(1)}, bf16[80,256]{1,0:T(8,128)(2,1)S(1)}, u32[]{:S(2)}, u32[]{:S(2)}) collective-permute-start(bf16[80,256]{1,0:T(8,128)(2,1)S(1)} %get-tuple-element.32), channel_id=1, source_target_pairs={{0,16},{16,0},{1,17},{17,1},{2,18},{18,2},{3,19},{19,3},{4,20},{20... | collective-permute-start | bytes 122888 | tf_op jit(solution)/shard_map/ppermute | solution.py:474
  12.9 10.7 %copy-start = (s32[12288]{0:T(1024)S(1)}, s32[12288]{0:T(1024)}, u32[]{:S(2)}) copy-start(s32[12288]{0:T(1024)} %param.31) | copy-start | bytes 147460
  12.9 10.7 %copy-start.1 = (s32[12288]{0:T(1024)S(1)}, s32[12288]{0:T(1024)}, u32[]{:S(2)}) copy-start(s32[12288]{0:T(1024)} %param.32) | copy-start | bytes 147460
  12.9 10.7 %copy-start.2 = (s32[12288]{0:T(1024)S(1)}, s32[12288]{0:T(1024)}, u32[]{:S(2)}) copy-start(s32[12288]{0:T(1024)} %param.33) | copy-start | bytes 147460
  36.3 6.8 %collective-permute-start.7 = (f32[8,256]{1,0:T(8,128)S(1)}, f32[8,256]{1,0:T(8,128)S(1)}, u32[]{:S(2)}, u32[]{:S(2)}) collective-permute-start(f32[8,256]{1,0:T(8,128)S(1)} %get-tuple-element.35), channel_id=1, source_target_pairs={{0,16},{16,0},{1,17},{17,1},{2,18},{18,2},{3,19},{19,3},{4,20},{20... | collective-permute-start | bytes 24584 | tf_op jit(solution)/shard_map/ppermute | solution.py:474
  37.9 6.2 %collective-permute-start.8 = (f32[8,256]{1,0:T(8,128)S(1)}, f32[8,256]{1,0:T(8,128)S(1)}, u32[]{:S(2)}, u32[]{:S(2)}) collective-permute-start(f32[8,256]{1,0:T(8,128)S(1)} %get-tuple-element.36), channel_id=1, source_target_pairs={{0,4},{4,8},{8,12},{12,0},{1,5},{5,9},{9,13},{13,1},{2,6},{6,10},{... | collective-permute-start | bytes 24584 | tf_op jit(solution)/shard_map/ppermute | solution.py:474
  37.9 18.7 %collective-permute-start.9 = (f32[8,256]{1,0:T(8,128)S(1)}, f32[8,256]{1,0:T(8,128)S(1)}, u32[]{:S(2)}, u32[]{:S(2)}) collective-permute-start(f32[8,256]{1,0:T(8,128)S(1)} %get-tuple-element.37), channel_id=1, source_target_pairs={{0,1},{1,2},{2,3},{3,0},{4,5},{5,6},{6,7},{7,4},{8,9},{9,10},{10,1... | collective-permute-start | bytes 24584 | tf_op jit(solution)/shard_map/ppermute | solution.py:474
  39.0 17.6 %collective-permute-start.10 = (f32[8,256]{1,0:T(8,128)S(1)}, f32[8,256]{1,0:T(8,128)S(1)}, u32[]{:S(2)}, u32[]{:S(2)}) collective-permute-start(f32[8,256]{1,0:T(8,128)S(1)} %get-tuple-element.38), channel_id=1, source_target_pairs={{0,20},{4,24},{8,28},{12,16},{16,4},{20,8},{24,12},{28,0},{1,21},{... | collective-permute-start | bytes 24584 | tf_op jit(solution)/shard_map/ppermute | solution.py:474
  40.5 16.2 %collective-permute-start.11 = (f32[8,256]{1,0:T(8,128)S(1)}, f32[8,256]{1,0:T(8,128)S(1)}, u32[]{:S(2)}, u32[]{:S(2)}) collective-permute-start(f32[8,256]{1,0:T(8,128)S(1)} %get-tuple-element.39), channel_id=1, source_target_pairs={{0,17},{1,18},{2,19},{3,16},{16,1},{17,2},{18,3},{19,0},{4,21},{5,... | collective-permute-start | bytes 24584 | tf_op jit(solution)/shard_map/ppermute | solution.py:474
  43.0 13.7 %collective-permute-start.12 = (f32[8,256]{1,0:T(8,128)S(1)}, f32[8,256]{1,0:T(8,128)S(1)}, u32[]{:S(2)}, u32[]{:S(2)}) collective-permute-start(f32[8,256]{1,0:T(8,128)S(1)} %get-tuple-element.40), channel_id=1, source_target_pairs={{0,5},{1,6},{2,7},{3,4},{4,9},{5,10},{6,11},{7,8},{8,13},{9,14},{1... | collective-permute-start | bytes 24584 | tf_op jit(solution)/shard_map/ppermute | solution.py:474
  44.1 12.6 %collective-permute-start.13 = (f32[8,256]{1,0:T(8,128)S(1)}, f32[8,256]{1,0:T(8,128)S(1)}, u32[]{:S(2)}, u32[]{:S(2)}) collective-permute-start(f32[8,256]{1,0:T(8,128)S(1)} %get-tuple-element.41), channel_id=1, source_target_pairs={{0,21},{1,22},{2,23},{3,20},{4,25},{5,26},{6,27},{7,24},{8,29},{9,... | collective-permute-start | bytes 24584 | tf_op jit(solution)/shard_map/ppermute | solution.py:474

commit v5 on v4

--- a/solution.py
+++ b/solution.py
@@ -101,19 +101,21 @@
     positions = positions_ref[...]
     left = dot(w_first_ref[...], features_ref[...]).astype(bf16).astype(f32)
     right = dot(w_second_ref[...], features_ref[...]).astype(bf16).astype(f32)
-    place = jnp.concatenate([positions, gain, jnp.zeros((EXTRA - 4, count), f32)], 0)
     own_ref[0:channels, :] = 0.5 * left
-    own_ref[channels:, :] = place
-    right_ref[0:channels, :] = 0.5 * right
-    right_ref[channels:, :] = place
-    parts = coord_rows(positions, gain)
-    table = jnp.concatenate([0.5 * right, parts, jnp.zeros_like(parts)], 0).astype(bf16)
+    own_ref[channels:, :] = jnp.concatenate([positions, gain, jnp.zeros((EXTRA - 4, count), f32)], 0)
+    column = jnp.concatenate([0.5 * right, coord_rows(positions, gain)], 0)
+    groups = count // GROUP
+    rows = channels + EXTRA
+    table = jnp.concatenate([column[:, group * GROUP : (group + 1) * GROUP] for group in range(groups)], 0)
+    spare = right_ref.shape[0] - groups * rows
+    if spare:
+        table = jnp.concatenate([table, jnp.zeros((spare, GROUP), f32)], 0)
+    table = table.astype(bf16)
+    right_ref[...] = table
     send = send_ref[...]
-    hot = one_hot(send & (GROUP - 1), row_codes(GROUP))
-    chosen = dot(table[:, 0:GROUP], hot)
-    for group in range(1, count // GROUP):
-        picked = dot(table[:, group * GROUP : (group + 1) * GROUP], hot)
-        chosen = jnp.where(send // GROUP == group, picked, chosen)
+    picked = dot(table, one_hot(send & (GROUP - 1), row_codes(GROUP)))
+    chosen = group_pick(picked, send // GROUP, rows, groups)
+    chosen = jnp.concatenate([chosen, jnp.zeros((OFFERED - EXTRA, chosen.shape[1]), f32)], 0)
     offered_ref[...] = chosen.astype(bf16)
 
     unit = eye(channels)
@@ -364,7 +366,6 @@
         *weights,
         sums,
         hot,
-        None,
         *scratch,
     )
 
@@ -522,7 +523,7 @@
         prep_kernel,
         (
             whole((rows, own_count), f32),
-            whole((rows, own_count), f32),
+            whole((-(-own_count // GROUP * rows // 16) * 16, GROUP), bf16),
             whole((channels + OFFERED, send_count), bf16),
             whole((4 * QUAD * channels, QUAD * channels), bf16),
             whole((QUAD * channels, QUAD * 4 * bases), bf16),
@@ -560,7 +561,7 @@
             ),
             (whole((groups * 16, GROUP), f32),),
             "local_pairs",
-            scratch(local_step, 1),
+            scratch(local_step, 2),
             [whole_spec] * len(operands),
             cost(part_rows * LANES),
         )(*operands)
@@ -580,7 +581,9 @@
         [whole_spec] * (9 + blocks),
         cost(ghost_owner.shape[0]),
     )(*ghost_lists, own, *weights, sums, *arrived)
-    returned = [shifted(force, offset, sizes, -1) for force, offset in zip(ghost_forces, ghost_offsets)]
+    returned = [
+        shifted(force, offset, sizes, -1) for force, offset in reversed(list(zip(ghost_forces, ghost_offsets)))
+    ]
     sums = local_call(1, (sums,))
     forces, energy = call(
         functools.partial(final_kernel, blocks),

time: 57.7 us -> 53 us (0.919)
  Pallas kernels: 36.5 us -> 32 us
    pallas_call x2, Pallas kernels: 21.2 us -> 17.1 us  [local_call(): call(functools.partial(local_kernel, local_step, channels, bases, part *...]
  transfers between devices with their start and end apart: 14 -> 14, of which waited for: 1 -> 1; matrix products, arithmetic and copies ran while one was open for 0% -> 0% of each run, Pallas kernels for 37% -> 32%
where the time goes in v5:
time: 53 us; the launch traced here: 52.8 us
  Pallas kernels  32 us (60%)
  starting transfers between devices  19.6 us (37%)
  between operations  0.78 us (1%)
    ppermute x14, starting transfers between devices, shifted(): return lax.ppermute(value, tuple((name for name, size in used)), pairs)  19.6 us
    pallas_call x2, Pallas kernels, local_call(): call(functools.partial(local_kernel, local_step, channels, bases, part *...  17.1 us
    pallas_call x1, Pallas kernels, on_device(): call(functools.partial(ghost_kernel, ghost_step, channels, bases), (whole...  12.4 us
    pallas_call x1, Pallas kernels, on_device(): call(prep_kernel, (whole((rows, own_count), f32), whole((-(-own_count //...  1.73 us
  transfers between devices with their start and end apart: 14, of which 1 were waited for; matrix products, arithmetic and copies ran while one was open for 0% of the time, Pallas kernels for 32%

profile of v5, /device:TPU:0, one launch (start us, length us, event | category | flops | bytes accessed | tf_op | source)
XLA Modules:
  0.0 52.8 jit_solution(158301012737231070)
XLA Ops:
  0.6 1.7 %tables.1 = (f32[72,512]{1,0:T(8,128)S(1)}, bf16[144,256]{1,0:T(8,128)(2,1)S(1)}, bf16[80,256]{1,0:T(8,128)(2,1)S(1)}, bf16[1024,256]{1,0:T(8,128)(2,1)S(1)}, bf...) custom-call(f32[3,512]{1,0:T(4,128)} %refs_0_.1, ...), custom_call_target="tpu_custom_call" | custom-call | tf_op jit(solution)/shard_map/tables/pallas_call | solution.py:522
  2.4 6.4 %collective-permute-start.6 = (bf16[80,256]{1,0:T(8,128)(2,1)S(1)}, bf16[80,256]{1,0:T(8,128)(2,1)S(1)}, u32[]{:S(2)}, u32[]{:S(2)}) collective-permute-start(bf16[80,256]{1,0:T(8,128)(2,1)S(1)} %get-tuple-element.32), channel_id=1, source_target_pairs={{0,31},{1,28},{2,29},{3,30},{4,19},{5,16},{6,17},{7,18},{8,23},{9,... | collective-permute-start | bytes 122888 | tf_op jit(solution)/shard_map/ppermute | solution.py:475
  8.8 0.7 %collective-permute-start.5 = (bf16[80,256]{1,0:T(8,128)(2,1)S(1)}, bf16[80,256]{1,0:T(8,128)(2,1)S(1)}, u32[]{:S(2)}, u32[]{:S(2)}) collective-permute-start(bf16[80,256]{1,0:T(8,128)(2,1)S(1)} %get-tuple-element.32), channel_id=1, source_target_pairs={{0,15},{1,12},{2,13},{3,14},{4,3},{5,0},{6,1},{7,2},{8,7},{9,4},{1... | collective-permute-start | bytes 122888 | tf_op jit(solution)/shard_map/ppermute | solution.py:475
  9.5 0.4 collective-permute-start.4
  10.0 0.8 %collective-permute-start.3 = (bf16[80,256]{1,0:T(8,128)(2,1)S(1)}, bf16[80,256]{1,0:T(8,128)(2,1)S(1)}, u32[]{:S(2)}, u32[]{:S(2)}) collective-permute-start(bf16[80,256]{1,0:T(8,128)(2,1)S(1)} %get-tuple-element.32), channel_id=1, source_target_pairs={{0,28},{4,16},{8,20},{12,24},{16,12},{20,0},{24,4},{28,8},{1,29},{... | collective-permute-start | bytes 122888 | tf_op jit(solution)/shard_map/ppermute | solution.py:475
  10.7 0.5 collective-permute-start.2
  11.2 0.0 collective-permute-done.6.refs_15_
  11.2 0.7 %collective-permute-start.1 = (bf16[80,256]{1,0:T(8,128)(2,1)S(1)}, bf16[80,256]{1,0:T(8,128)(2,1)S(1)}, u32[]{:S(2)}, u32[]{:S(2)}) collective-permute-start(bf16[80,256]{1,0:T(8,128)(2,1)S(1)} %get-tuple-element.32), channel_id=1, source_target_pairs={{0,12},{4,0},{8,4},{12,8},{1,13},{5,1},{9,5},{13,9},{2,14},{6,2},{... | collective-permute-start | bytes 122888 | tf_op jit(solution)/shard_map/ppermute | solution.py:475
  11.8 0.4 collective-permute-done.5.refs_14_
  12.2 0.5 %collective-permute-start = (bf16[80,256]{1,0:T(8,128)(2,1)S(1)}, bf16[80,256]{1,0:T(8,128)(2,1)S(1)}, u32[]{:S(2)}, u32[]{:S(2)}) collective-permute-start(bf16[80,256]{1,0:T(8,128)(2,1)S(1)} %get-tuple-element.32), channel_id=1, source_target_pairs={{0,16},{16,0},{1,17},{17,1},{2,18},{18,2},{3,19},{19,3},{4,20},{20... | collective-permute-start | bytes 122888 | tf_op jit(solution)/shard_map/ppermute | solution.py:475
  12.8 0.0 copy-start
  12.8 0.0 copy-start.1
  12.8 0.0 copy-start.2
  12.8 8.6 %local_pairs.2.refs_8_ = f32[64,256]{1,0:T(8,128)S(1)} custom-call(s32[160,128]{1,0:T(8,128)S(1)} %get-tuple-element.23.refs_0_, s32[160,128]{1,0:T(8,128)S(1)} %get-tuple-element.24.refs_1_, s32[160,128]{1,0:T(8,128)S(1)} %get-tuple-element.25.refs_2_, f32[72,512]{1,0:T(8,128)S(1)} %get-tuple-element.26.refs_3_, ...), custom_call_target="tpu_custom_call" | custom-call | flops 4096000000 | bytes 122880 | tf_op jit(solution)/shard_map/local_pairs/pallas_call | solution.py:558
  21.3 0.0 collective-permute-done.4.refs_13_
  21.3 0.0 collective-permute-done.3.refs_12_
  21.4 0.0 collective-permute-done.2.refs_11_
  21.4 0.0 collective-permute-done.1.refs_10_
  21.4 0.0 collective-permute-done.refs_9_
  21.4 0.0 copy-done
  21.4 0.0 copy-done.1
  21.4 0.0 copy-done.2
  21.4 12.4 %ghost_pairs.1 = (f32[64,256]{1,0:T(8,128)S(1)}, f32[8,256]{1,0:T(8,128)S(1)}, f32[8,256]{1,0:T(8,128)S(1)}, f32[8,256]{1,0:T(8,128)S(1)}, f32[8,256]{1,0:T(8,12...) custom-call(s32[96,128]{1,0:T(8,128)S(1)} %bitcast.12, s32[96,128]{1,0:T(8,128)S(1)} %bitcast.13, ...), custom_call_target="tpu_custom_call" | custom-call | flops 4915200000 | bytes 147456 | tf_op jit(solution)/shard_map/ghost_pairs/pallas_call | solution.py:575
  33.8 1.5 %collective-permute-start.7 = (f32[8,256]{1,0:T(8,128)S(1)}, f32[8,256]{1,0:T(8,128)S(1)}, u32[]{:S(2)}, u32[]{:S(2)}) collective-permute-start(f32[8,256]{1,0:T(8,128)S(1)} %get-tuple-element.35), channel_id=1, source_target_pairs={{0,21},{1,22},{2,23},{3,20},{4,25},{5,26},{6,27},{7,24},{8,29},{9,... | collective-permute-start | bytes 24584 | tf_op jit(solution)/shard_map/ppermute | solution.py:475
  35.3 3.0 %collective-permute-start.8 = (f32[8,256]{1,0:T(8,128)S(1)}, f32[8,256]{1,0:T(8,128)S(1)}, u32[]{:S(2)}, u32[]{:S(2)}) collective-permute-start(f32[8,256]{1,0:T(8,128)S(1)} %get-tuple-element.36), channel_id=1, source_target_pairs={{0,5},{1,6},{2,7},{3,4},{4,9},{5,10},{6,11},{7,8},{8,13},{9,14},{1... | collective-permute-start | bytes 24584 | tf_op jit(solution)/shard_map/ppermute | solution.py:475
  38.3 2.0 %collective-permute-start.9 = (f32[8,256]{1,0:T(8,128)S(1)}, f32[8,256]{1,0:T(8,128)S(1)}, u32[]{:S(2)}, u32[]{:S(2)}) collective-permute-start(f32[8,256]{1,0:T(8,128)S(1)} %get-tuple-element.37), channel_id=1, source_target_pairs={{0,17},{1,18},{2,19},{3,16},{16,1},{17,2},{18,3},{19,0},{4,21},{5,... | collective-permute-start | bytes 24584 | tf_op jit(solution)/shard_map/ppermute | solution.py:475
  40.3 0.5 collective-permute-start.10
  40.8 1.1 %collective-permute-start.11 = (f32[8,256]{1,0:T(8,128)S(1)}, f32[8,256]{1,0:T(8,128)S(1)}, u32[]{:S(2)}, u32[]{:S(2)}) collective-permute-start(f32[8,256]{1,0:T(8,128)S(1)} %get-tuple-element.39), channel_id=1, source_target_pairs={{0,1},{1,2},{2,3},{3,0},{4,5},{5,6},{6,7},{7,4},{8,9},{9,10},{10,1... | collective-permute-start | bytes 24584 | tf_op jit(solution)/shard_map/ppermute | solution.py:475
  41.9 0.0 collective-permute-done.7.refs_2_
  41.9 0.0 collective-permute-start.12
  41.9 0.0 collective-permute-done.8.refs_3_
  41.9 1.5 %collective-permute-start.13 = (f32[8,256]{1,0:T(8,128)S(1)}, f32[8,256]{1,0:T(8,128)S(1)}, u32[]{:S(2)}, u32[]{:S(2)}) collective-permute-start(f32[8,256]{1,0:T(8,128)S(1)} %get-tuple-element.41), channel_id=1, source_target_pairs={{0,16},{16,0},{1,17},{17,1},{2,18},{18,2},{3,19},{19,3},{4,20},{20... | collective-permute-start | bytes 24584 | tf_op jit(solution)/shard_map/ppermute | solution.py:475
  43.4 8.6 %local_pairs.3.refs_0_ = f32[64,256]{1,0:T(8,128)S(1)} custom-call(s32[160,128]{1,0:T(8,128)S(1)} %get-tuple-element.23.refs_0_, s32[160,128]{1,0:T(8,128)S(1)} %get-tuple-element.24.refs_1_, s32[160,128]{1,0:T(8,128)S(1)} %get-tuple-element.25.refs_2_, f32[72,512]{1,0:T(8,128)S(1)} %get-tuple-element.26.refs_3_, ...), custom_call_target="tpu_custom_call" | custom-call | flops 4096000000 | bytes 122880 | tf_op jit(solution)/shard_map/local_pairs/pallas_call | solution.py:558
  52.0 0.0 collective-permute-done.9.refs_4_
  52.0 0.0 collective-permute-done.10.refs_5_
  52.0 0.0 collective-permute-done.11.refs_6_
  52.0 0.0 collective-permute-done.12.refs_7_
  52.0 0.0 collective-permute-done.13.refs_8_
  52.0 0.8 %totals.1 = (f32[3,512]{1,0:T(4,128)}, f32[1,512]{1,0:T(1,128)}) custom-call(f32[64,256]{1,0:T(8,128)S(1)} %local_pairs.3.refs_0_, s32[1,256]{1,0:T(1,128)S(1)} %get-tuple-element.34.refs_1_, f32[8,256]{1,0:T(8,128)S(1)} %collective-permute-done.7.refs_2_, f32[8,256]{1,0:T(8,128)S(1)} %collective-permute-done.8.refs_3_, ...), custom_call_target="tpu_custom_call" | custom-call | tf_op jit(solution)/shard_map/totals/pallas_call | solution.py:588
Async XLA Ops:
  2.4 8.8 %collective-permute-start.6 = (bf16[80,256]{1,0:T(8,128)(2,1)S(1)}, bf16[80,256]{1,0:T(8,128)(2,1)S(1)}, u32[]{:S(2)}, u32[]{:S(2)}) collective-permute-start(bf16[80,256]{1,0:T(8,128)(2,1)S(1)} %get-tuple-element.32), channel_id=1, source_target_pairs={{0,31},{1,28},{2,29},{3,30},{4,19},{5,16},{6,17},{7,18},{8,23},{9,... | collective-permute-start | bytes 122888 | tf_op jit(solution)/shard_map/ppermute | solution.py:475
  8.8 3.4 %collective-permute-start.5 = (bf16[80,256]{1,0:T(8,128)(2,1)S(1)}, bf16[80,256]{1,0:T(8,128)(2,1)S(1)}, u32[]{:S(2)}, u32[]{:S(2)}) collective-permute-start(bf16[80,256]{1,0:T(8,128)(2,1)S(1)} %get-tuple-element.32), channel_id=1, source_target_pairs={{0,15},{1,12},{2,13},{3,14},{4,3},{5,0},{6,1},{7,2},{8,7},{9,4},{1... | collective-permute-start | bytes 122888 | tf_op jit(solution)/shard_map/ppermute | solution.py:475
  9.5 11.8 %collective-permute-start.4 = (bf16[80,256]{1,0:T(8,128)(2,1)S(1)}, bf16[80,256]{1,0:T(8,128)(2,1)S(1)}, u32[]{:S(2)}, u32[]{:S(2)}) collective-permute-start(bf16[80,256]{1,0:T(8,128)(2,1)S(1)} %get-tuple-element.32), channel_id=1, source_target_pairs={{0,19},{1,16},{2,17},{3,18},{16,3},{17,0},{18,1},{19,2},{4,23},{5,... | collective-permute-start | bytes 122888 | tf_op jit(solution)/shard_map/ppermute | solution.py:475
  10.0 11.4 %collective-permute-start.3 = (bf16[80,256]{1,0:T(8,128)(2,1)S(1)}, bf16[80,256]{1,0:T(8,128)(2,1)S(1)}, u32[]{:S(2)}, u32[]{:S(2)}) collective-permute-start(bf16[80,256]{1,0:T(8,128)(2,1)S(1)} %get-tuple-element.32), channel_id=1, source_target_pairs={{0,28},{4,16},{8,20},{12,24},{16,12},{20,0},{24,4},{28,8},{1,29},{... | collective-permute-start | bytes 122888 | tf_op jit(solution)/shard_map/ppermute | solution.py:475
  10.7 10.6 %collective-permute-start.2 = (bf16[80,256]{1,0:T(8,128)(2,1)S(1)}, bf16[80,256]{1,0:T(8,128)(2,1)S(1)}, u32[]{:S(2)}, u32[]{:S(2)}) collective-permute-start(bf16[80,256]{1,0:T(8,128)(2,1)S(1)} %get-tuple-element.32), channel_id=1, source_target_pairs={{0,3},{1,0},{2,1},{3,2},{4,7},{5,4},{6,5},{7,6},{8,11},{9,8},{10,9... | collective-permute-start | bytes 122888 | tf_op jit(solution)/shard_map/ppermute | solution.py:475
  11.2 10.2 %collective-permute-start.1 = (bf16[80,256]{1,0:T(8,128)(2,1)S(1)}, bf16[80,256]{1,0:T(8,128)(2,1)S(1)}, u32[]{:S(2)}, u32[]{:S(2)}) collective-permute-start(bf16[80,256]{1,0:T(8,128)(2,1)S(1)} %get-tuple-element.32), channel_id=1, source_target_pairs={{0,12},{4,0},{8,4},{12,8},{1,13},{5,1},{9,5},{13,9},{2,14},{6,2},{... | collective-permute-start | bytes 122888 | tf_op jit(solution)/shard_map/ppermute | solution.py:475
  12.2 9.1 %collective-permute-start = (bf16[80,256]{1,0:T(8,128)(2,1)S(1)}, bf16[80,256]{1,0:T(8,128)(2,1)S(1)}, u32[]{:S(2)}, u32[]{:S(2)}) collective-permute-start(bf16[80,256]{1,0:T(8,128)(2,1)S(1)} %get-tuple-element.32), channel_id=1, source_target_pairs={{0,16},{16,0},{1,17},{17,1},{2,18},{18,2},{3,19},{19,3},{4,20},{20... | collective-permute-start | bytes 122888 | tf_op jit(solution)/shard_map/ppermute | solution.py:475
  12.8 8.6 %copy-start = (s32[12288]{0:T(1024)S(1)}, s32[12288]{0:T(1024)}, u32[]{:S(2)}) copy-start(s32[12288]{0:T(1024)} %param.31) | copy-start | bytes 147460
  12.8 8.6 %copy-start.1 = (s32[12288]{0:T(1024)S(1)}, s32[12288]{0:T(1024)}, u32[]{:S(2)}) copy-start(s32[12288]{0:T(1024)} %param.32) | copy-start | bytes 147460
  12.8 8.6 %copy-start.2 = (s32[12288]{0:T(1024)S(1)}, s32[12288]{0:T(1024)}, u32[]{:S(2)}) copy-start(s32[12288]{0:T(1024)} %param.33) | copy-start | bytes 147460
  33.8 8.1 %collective-permute-start.7 = (f32[8,256]{1,0:T(8,128)S(1)}, f32[8,256]{1,0:T(8,128)S(1)}, u32[]{:S(2)}, u32[]{:S(2)}) collective-permute-start(f32[8,256]{1,0:T(8,128)S(1)} %get-tuple-element.35), channel_id=1, source_target_pairs={{0,21},{1,22},{2,23},{3,20},{4,25},{5,26},{6,27},{7,24},{8,29},{9,... | collective-permute-start | bytes 24584 | tf_op jit(solution)/shard_map/ppermute | solution.py:475
  35.3 6.6 %collective-permute-start.8 = (f32[8,256]{1,0:T(8,128)S(1)}, f32[8,256]{1,0:T(8,128)S(1)}, u32[]{:S(2)}, u32[]{:S(2)}) collective-permute-start(f32[8,256]{1,0:T(8,128)S(1)} %get-tuple-element.36), channel_id=1, source_target_pairs={{0,5},{1,6},{2,7},{3,4},{4,9},{5,10},{6,11},{7,8},{8,13},{9,14},{1... | collective-permute-start | bytes 24584 | tf_op jit(solution)/shard_map/ppermute | solution.py:475
  38.3 13.7 %collective-permute-start.9 = (f32[8,256]{1,0:T(8,128)S(1)}, f32[8,256]{1,0:T(8,128)S(1)}, u32[]{:S(2)}, u32[]{:S(2)}) collective-permute-start(f32[8,256]{1,0:T(8,128)S(1)} %get-tuple-element.37), channel_id=1, source_target_pairs={{0,17},{1,18},{2,19},{3,16},{16,1},{17,2},{18,3},{19,0},{4,21},{5,... | collective-permute-start | bytes 24584 | tf_op jit(solution)/shard_map/ppermute | solution.py:475
  40.3 11.7 %collective-permute-start.10 = (f32[8,256]{1,0:T(8,128)S(1)}, f32[8,256]{1,0:T(8,128)S(1)}, u32[]{:S(2)}, u32[]{:S(2)}) collective-permute-start(f32[8,256]{1,0:T(8,128)S(1)} %get-tuple-element.38), channel_id=1, source_target_pairs={{0,20},{4,24},{8,28},{12,16},{16,4},{20,8},{24,12},{28,0},{1,21},{... | collective-permute-start | bytes 24584 | tf_op jit(solution)/shard_map/ppermute | solution.py:475
  40.8 11.2 %collective-permute-start.11 = (f32[8,256]{1,0:T(8,128)S(1)}, f32[8,256]{1,0:T(8,128)S(1)}, u32[]{:S(2)}, u32[]{:S(2)}) collective-permute-start(f32[8,256]{1,0:T(8,128)S(1)} %get-tuple-element.39), channel_id=1, source_target_pairs={{0,1},{1,2},{2,3},{3,0},{4,5},{5,6},{6,7},{7,4},{8,9},{9,10},{10,1... | collective-permute-start | bytes 24584 | tf_op jit(solution)/shard_map/ppermute | solution.py:475
  41.9 10.1 %collective-permute-start.12 = (f32[8,256]{1,0:T(8,128)S(1)}, f32[8,256]{1,0:T(8,128)S(1)}, u32[]{:S(2)}, u32[]{:S(2)}) collective-permute-start(f32[8,256]{1,0:T(8,128)S(1)} %get-tuple-element.40), channel_id=1, source_target_pairs={{0,4},{4,8},{8,12},{12,0},{1,5},{5,9},{9,13},{13,1},{2,6},{6,10},{... | collective-permute-start | bytes 24584 | tf_op jit(solution)/shard_map/ppermute | solution.py:475
  41.9 10.1 %collective-permute-start.13 = (f32[8,256]{1,0:T(8,128)S(1)}, f32[8,256]{1,0:T(8,128)S(1)}, u32[]{:S(2)}, u32[]{:S(2)}) collective-permute-start(f32[8,256]{1,0:T(8,128)S(1)} %get-tuple-element.41), channel_id=1, source_target_pairs={{0,16},{16,0},{1,17},{17,1},{2,18},{18,2},{3,19},{19,3},{4,20},{20... | collective-permute-start | bytes 24584 | tf_op jit(solution)/shard_map/ppermute | solution.py:475

commit v6 on v5

--- a/solution.py
+++ b/solution.py
@@ -12,6 +12,7 @@
 domain_edge = 1.0
 ghost_offsets = ((1, 0, 0), (0, 1, 0), (0, 0, 1), (1, 1, 0), (1, 0, 1), (0, 1, 1), (1, 1, 1))
 
+PLANAR = ((1, 0), (0, 1), (1, 1))
 EXTRA = 8
 OFFERED = 16
 GROUP = 256
@@ -65,11 +66,7 @@
     return (iota((count, count), 0) == iota((count, count), 1)).astype(bf16)
 
 
-def prep_kernel(*refs):
-    sources = refs[:14]
-    own_ref, right_ref, offered_ref, mats_ref, radial_ref, radial_t_ref, out_ref = refs[14:21]
-    targets = refs[25:35] + refs[21:25]
-    landed = refs[35]
+def fetch(sources, targets, landed):
     copies = [
         pltpu.make_async_copy(source, target, landed.at[place])
         for place, (source, target) in enumerate(zip(sources, targets))
@@ -78,19 +75,12 @@
         copy.start()
     for copy in copies:
         copy.wait()
-    (
-        positions_ref,
-        features_ref,
-        species_ref,
-        scale_ref,
-        w_first_ref,
-        w_second_ref,
-        radial_w_ref,
-        w_mid_ref,
-        w_last_ref,
-        w_out_ref,
-        send_ref,
-    ) = targets[:11]
+
+
+def tables_kernel(*refs):
+    own_ref, right_ref, offered_ref, send_ref = refs[7:11]
+    fetch(refs[:7], refs[11:17] + (send_ref,), refs[17])
+    positions_ref, features_ref, species_ref, scale_ref, w_first_ref, w_second_ref = refs[11:17]
     channels = features_ref.shape[0]
     count = features_ref.shape[1]
     species = species_ref[...]
@@ -118,6 +108,12 @@
     chosen = jnp.concatenate([chosen, jnp.zeros((OFFERED - EXTRA, chosen.shape[1]), f32)], 0)
     offered_ref[...] = chosen.astype(bf16)
 
+
+def weights_kernel(*refs):
+    mats_ref, radial_ref, radial_t_ref, out_ref = refs[7:11]
+    fetch(refs[:7], refs[14:18] + refs[11:14], refs[18])
+    radial_w_ref, w_mid_ref, w_last_ref, w_out_ref = refs[14:18]
+    channels = w_mid_ref.shape[0]
     unit = eye(channels)
     w_mid = w_mid_ref[...]
     w_last = w_last_ref[...]
@@ -154,8 +150,10 @@
 
 
 def spread_groups(values, high, groups):
-    pieces = [jnp.where(high == group, values, 0.0) for group in range(groups)]
-    return jnp.concatenate(pieces, 0).astype(bf16)
+    twice = jnp.concatenate([values, values], 0)
+    second = iota(twice.shape, 0) // 4
+    pieces = [jnp.where(high == second + group, twice, 0.0) for group in range(0, groups, 2)]
+    return jnp.concatenate(pieces, 0)
 
 
 def lane_pick(table_ref, row):
@@ -318,12 +316,13 @@
             energy = weight_near * near * readouts[quad]
             slope = weight_near * (near * readout_slope - 2.0 * readouts[quad])
             push = (2.0 * slope) * shifts[quad]
-            high, low = split_two(jnp.where(sub == 3, energy, push))
-            values = jnp.concatenate([high[:4], low[:4]], 0)
+            values = jnp.where(sub == 3, energy, push)[:4]
             parts.append(
                 jnp.concatenate(
-                    [jnp.where(own_high[quad] == group, values, 0.0) for group in range(own_groups)]
-                    + [jnp.where(partner_high[quad] == group, values, 0.0) for group in range(partner_groups)],
+                    [
+                        spread_groups(values, own_high[quad], own_groups),
+                        spread_groups(values, partner_high[quad], partner_groups),
+                    ],
                     0,
                 ).astype(bf16)
             )
@@ -345,7 +344,7 @@
 
 
 def local_kernel(per_step, channels, bases, first_row, row_count, with_start, *refs):
-    count = 9 + with_start
+    count = 10 + with_start
     owner, partner, mask, own, right, *weights = refs[:9]
     sums, hot, *scratch = refs[count:]
     sums[...] = refs[9][...] if with_start else jnp.zeros_like(sums)
@@ -374,20 +373,23 @@
     blocks = len(ghost_offsets)
     owner, partner, mask, own, *weights = refs[:8]
     sums_in = refs[8]
-    arrived = refs[9 : 9 + blocks]
-    sums_out = refs[9 + blocks]
-    forces = refs[10 + blocks : 10 + 2 * blocks]
-    table, sums, *scratch = refs[10 + 2 * blocks :]
+    arrived = refs[9 : 10 + len(PLANAR)]
+    sums_out, upward, *level = refs[10 + len(PLANAR) : 12 + 2 * len(PLANAR)]
+    table, sums, *scratch = refs[12 + 2 * len(PLANAR) :]
     groups = own.shape[1] // LANES
     partner_groups = blocks * GROUP // LANES
     sums[...] = jnp.zeros_like(sums)
     pieces = []
-    for block, offset in enumerate(ghost_offsets):
-        extra = arrived[block][channels : channels + OFFERED, :].astype(f32)
+    for offset in ghost_offsets:
+        if offset[:2] == (0, 0):
+            source, start = arrived[0], 0
+        else:
+            source, start = arrived[1 + PLANAR.index(offset[:2])], offset[2] * (channels + OFFERED)
+        extra = source[start + channels : start + channels + OFFERED, :].astype(f32)
         moved = jnp.concatenate(
             [extra[axis : axis + 1] + extra[axis + 4 : axis + 5] + domain_edge * offset[axis] for axis in range(3)], 0
         )
-        pieces += [arrived[block][0:channels, :].astype(f32), coord_rows(moved, extra[3:4])]
+        pieces += [source[start : start + channels, :].astype(f32), coord_rows(moved, extra[3:4])]
     pieces.append(jnp.zeros((table.shape[0] - blocks * (channels + EXTRA), GROUP), f32))
     table[...] = jnp.concatenate(pieces, 0).astype(bf16)
     pair_body(
@@ -407,37 +409,57 @@
         sums,
         *scratch,
     )
-    first = groups * 8
+    first = groups * 4
     sums_out[0:first, :] = sums_in[0:first, :] + sums[0:first, :]
     sums_out[first:, :] = sums_in[first:, :]
-    for block in range(blocks):
+    for block, offset in enumerate(ghost_offsets):
+        halves = []
         for half in range(GROUP // LANES):
-            start = first + (block * (GROUP // LANES) + half) * 8
-            both = sums[start : start + 8, LANES:]
-            forces[block][:, half * LANES : (half + 1) * LANES] = -(
-                both + jnp.concatenate([both[4:], both[:4]], 0)
-            )
-
-
-def final_kernel(blocks, *refs):
-    sums_ref, send_ref = refs[:2]
-    arrived = refs[2 : 2 + blocks]
-    forces_ref, energy_ref = refs[2 + blocks :]
+            start = first + (block * (GROUP // LANES) + half) * 4
+            halves.append(sums[start : start + 4, LANES:])
+        force = -jnp.concatenate(halves, 1)
+        force = jnp.concatenate([force, jnp.zeros_like(force)], 0)
+        if offset[2]:
+            place = 0 if offset[:2] == (0, 0) else 1 + PLANAR.index(offset[:2])
+            upward[place * 8 : place * 8 + 8, :] = force
+        else:
+            level[PLANAR.index(offset[:2])][...] = force
+
+
+def pair_kernel(offered_ref, from_z_ref, both_ref):
+    count = offered_ref.shape[0]
+    both_ref[0:count, :] = offered_ref[...]
+    both_ref[count:, :] = from_z_ref[...]
+
+
+def merge_kernel(*refs):
+    upward, *level = refs[: 1 + len(PLANAR)]
+    outs = refs[1 + len(PLANAR) :]
+    outs[0][...] = upward[0:8, :]
+    for place, part in enumerate(level):
+        outs[1 + place][...] = part[...] + upward[8 * place + 8 : 8 * place + 16, :]
+
+
+def final_kernel(*refs):
+    sums_ref, send_ref, *arrived = refs[:-2]
+    forces_ref, energy_ref = refs[-2:]
     incoming = arrived[0][...]
-    for block in range(1, blocks):
-        incoming = incoming + arrived[block][...]
+    for part in arrived[1:]:
+        incoming = incoming + part[...]
     high, low = split_two(incoming[:4])
     send = send_ref[...]
-    groups = sums_ref.shape[0] // 16
-    values = spread_groups(jnp.concatenate([high, low], 0), send // LANES, groups)
-    back = dot_nt(values, one_hot(send & (LANES - 1), row_codes(LANES)))
+    groups = sums_ref.shape[0] // 8
+    hot = one_hot(send & (LANES - 1), row_codes(LANES))
+    spread = [spread_groups(value, send // LANES, groups).astype(bf16) for value in (high, low)]
+    back = dot_nt(jnp.concatenate(spread, 0), hot)
+    back = back[: groups * 4] + back[groups * 4 :]
     for group in range(groups):
-        own = sums_ref[group * 8 : group * 8 + 8, 0:LANES]
-        partner = sums_ref[(groups + group) * 8 : (groups + group) * 8 + 8, LANES:]
-        total = own - partner + back[group * 8 : group * 8 + 8]
+        own = sums_ref[group * 4 : group * 4 + 4, 0:LANES]
+        partner = sums_ref[(groups + group) * 4 : (groups + group) * 4 + 4, LANES:]
+        total = own - partner + back[group * 4 : group * 4 + 4]
         cols = slice(group * LANES, (group + 1) * LANES)
-        forces_ref[:, cols] = total[0:3] + total[4:7]
-        energy_ref[:, cols] = own[3:4] + own[7:8]
+        forces_ref[:, cols] = total[0:3]
+        energy_ref[:, cols] = own[3:4]
 
 
 def whole(shape, dtype):
@@ -501,42 +523,67 @@
     rows = channels + EXTRA
     groups = own_count // LANES
     blocks = len(ghost_offsets)
-    send = ghost_send.reshape(1, send_count)
     whole_spec = pl.BlockSpec(memory_space=pltpu.VMEM)
     def tiles(value):
         return value.reshape(value.shape[0] // LANES, LANES)
 
-    small = (
-        positions,
-        features,
-        species.reshape(1, own_count),
-        species_scale.reshape(1, species_scale.shape[0]),
-        w_first,
-        w_second,
-        w_radial.T,
-        w_mid,
-        w_last,
-        w_out.reshape(1, channels),
-    )
-    lists = [send] + [tiles(value) for value in (local_first, local_second, local_mask)]
-    own, right, offered, mats, radial, radial_t, out, send, *local = call(
-        prep_kernel,
+    def fetching(kernel, name, outs, operands, kept):
+        here = [pltpu.with_memory_space_constraint(value, pltpu.HBM) for value in operands]
+        landing = operands[: len(operands) - kept]
+        return call(
+            kernel,
+            outs + tuple(whole(value.shape, value.dtype) for value in operands[len(landing) :]),
+            name,
+            [pltpu.VMEM(value.shape, value.dtype) for value in landing]
+            + [pltpu.SemaphoreType.DMA((len(operands),))],
+            [pl.BlockSpec(memory_space=pltpu.HBM)] * len(operands),
+        )(*here)
+
+    own, right, offered, send = fetching(
+        tables_kernel,
+        "tables",
         (
             whole((rows, own_count), f32),
             whole((-(-own_count // GROUP * rows // 16) * 16, GROUP), bf16),
             whole((channels + OFFERED, send_count), bf16),
+        ),
+        (
+            positions,
+            features,
+            species.reshape(1, own_count),
+            species_scale.reshape(1, species_scale.shape[0]),
+            w_first,
+            w_second,
+            ghost_send.reshape(1, send_count),
+        ),
+        1,
+    )
+    from_z = shifted(offered, (0, 0, 1), sizes, 1)
+    *weights, local_first, local_second, local_mask = fetching(
+        weights_kernel,
+        "weights",
+        (
             whole((4 * QUAD * channels, QUAD * channels), bf16),
             whole((QUAD * channels, QUAD * 4 * bases), bf16),
             whole((QUAD * 2 * bases, QUAD * channels), bf16),
             whole((channels, LANES), f32),
-            *[whole(value.shape, value.dtype) for value in lists],
         ),
-        "tables",
-        [pltpu.VMEM(value.shape, value.dtype) for value in small]
-        + [pltpu.SemaphoreType.DMA((len(small) + len(lists),))],
-        [pl.BlockSpec(memory_space=pltpu.HBM)] * (len(small) + len(lists)),
-    )(*[pltpu.with_memory_space_constraint(value, pltpu.HBM) for value in (*small, *lists)])
-    arrived = [shifted(offered, offset, sizes, 1) for offset in ghost_offsets]
+        (
+            w_radial.T,
+            w_mid,
+            w_last,
+            w_out.reshape(1, channels),
+            tiles(local_first),
+            tiles(local_second),
+            tiles(local_mask),
+        ),
+        3,
+    )
+    local = (local_first, local_second, local_mask)
+    (both,) = call(
+        pair_kernel, (whole((2 * offered.shape[0], send_count), bf16),), "two_blocks", specs=[whole_spec] * 2
+    )(offered, from_z)
+    arrived = [from_z] + [shifted(both, (*step, 0), sizes, 1) for step in PLANAR]
 
     def scratch(per_step, hots):
         return [pltpu.VMEM((per_step, GROUP, QUAD * CHUNK), bf16) for _ in range(hots)] + [
@@ -550,16 +597,15 @@
 
     parts = 2
     part_rows = local[0].shape[0] // parts
-    weights = (mats, radial, radial_t, out)
     local_step = part_rows * LANES // (QUAD * CHUNK)
 
-    def local_call(part, start):
-        operands = [*local, own, right, *weights, *start]
+    def local_call(part, start, after):
+        operands = [*local, own, right, *weights, *start, after]
         (sums,) = call(
             functools.partial(
                 local_kernel, local_step, channels, bases, part * part_rows, part_rows, len(start)
             ),
-            (whole((groups * 16, GROUP), f32),),
+            (whole((groups * 8, GROUP), f32),),
             "local_pairs",
             scratch(local_step, 2),
             [whole_spec] * len(operands),
@@ -567,30 +613,33 @@
         )(*operands)
         return sums
 
-    sums = local_call(0, ())
+    sums = local_call(0, (), both)
     ghost_lists = [tiles(value) for value in (ghost_owner, ghost_index, ghost_mask)]
     ghost_step = ghost_owner.shape[0] // (QUAD * CHUNK)
-    partner_rows = blocks * GROUP // LANES * 8
+    partner_rows = blocks * GROUP // LANES * 4
     table_rows = -(-blocks * rows // 16) * 16
-    sums, *ghost_forces = call(
+    force = whole((8, send_count), f32)
+    sums, upward, *level = call(
         functools.partial(ghost_kernel, ghost_step, channels, bases),
-        (whole((groups * 16, GROUP), f32),) + (whole((8, send_count), f32),) * blocks,
+        (whole((groups * 8, GROUP), f32), whole((8 + 8 * len(PLANAR), send_count), f32)) + (force,) * len(PLANAR),
         "ghost_pairs",
-        [pltpu.VMEM((table_rows, GROUP), bf16), pltpu.VMEM((groups * 8 + partner_rows, GROUP), f32)]
+        [pltpu.VMEM((table_rows, GROUP), bf16), pltpu.VMEM((groups * 4 + partner_rows, GROUP), f32)]
         + scratch(ghost_step, 2),
-        [whole_spec] * (9 + blocks),
+        [whole_spec] * (9 + len(arrived)),
         cost(ghost_owner.shape[0]),
     )(*ghost_lists, own, *weights, sums, *arrived)
-    returned = [
-        shifted(force, offset, sizes, -1) for force, offset in reversed(list(zip(ghost_forces, ghost_offsets)))
-    ]
-    sums = local_call(1, (sums,))
+    upward = shifted(upward, (0, 0, 1), sizes, -1)
+    mine, *level = call(
+        merge_kernel, (force,) * (1 + len(PLANAR)), "forces_upward", specs=[whole_spec] * (1 + len(PLANAR))
+    )(upward, *level)
+    returned = [shifted(part, (*step, 0), sizes, -1) for part, step in zip(level, PLANAR)]
+    sums = local_call(1, (sums,), mine)
     forces, energy = call(
-        functools.partial(final_kernel, blocks),
+        final_kernel,
         (whole((3, own_count), f32), whole((1, own_count), f32)),
         "totals",
-        specs=[whole_spec] * (2 + blocks),
-    )(sums, send, *returned)
+        specs=[whole_spec] * (3 + len(returned)),
+    )(sums, send, mine, *returned)
     return forces, energy.reshape(own_count)
 
 

time: 53 us -> 51.1 us (0.964)
  starting transfers between devices: 19.6 us -> 11 us
  waiting for transfers between devices: 0.42 us -> 5.96 us
  Pallas kernels: 32 us -> 33.2 us
    ppermute x14 -> x8, starting transfers between devices: 19.6 us -> 11 us  [shifted(): return lax.ppermute(value, tuple((name for name, size in used)), pairs)]
    ppermute x14 -> x8, waiting for transfers between devices: 0.42 us -> 5.96 us  [shifted(): return lax.ppermute(value, tuple((name for name, size in used)), pairs)]
    pallas_call x2 -> x5, Pallas kernels: 2.5 us -> 3.52 us  [the longest x2 2.75 us: fetching(): call(kernel, outs + tuple((whole(value.shape, value.dtype) for value in o...]
  transfers between devices with their start and end apart: 14 -> 8, of which waited for: 1 -> 2; matrix products, arithmetic and copies ran while one was open for 0% -> 0% of each run, Pallas kernels for 32% -> 37%
where the time goes in v6:
time: 51.1 us; the launch traced here: 50.9 us
  Pallas kernels  33.2 us (65%)
  starting transfers between devices  11 us (22%)
  waiting for transfers between devices  5.96 us (12%)
  between operations  0.73 us (1%)
    pallas_call x2, Pallas kernels, local_call(): call(functools.partial(local_kernel, local_step, channels, bases, part *...  17.5 us
    pallas_call x1, Pallas kernels, on_device(): call(functools.partial(ghost_kernel, ghost_step, channels, bases), (whole...  12.2 us
    ppermute x8, starting transfers between devices, shifted(): return lax.ppermute(value, tuple((name for name, size in used)), pairs)  11 us
    ppermute x8, waiting for transfers between devices, shifted(): return lax.ppermute(value, tuple((name for name, size in used)), pairs)  5.96 us
    pallas_call x2, Pallas kernels, fetching(): call(kernel, outs + tuple((whole(value.shape, value.dtype) for value in o...  2.75 us
  transfers between devices with their start and end apart: 8, of which 2 were waited for; matrix products, arithmetic and copies ran while one was open for 0% of the time, Pallas kernels for 37%

profile of v6, /device:TPU:0, one launch (start us, length us, event | category | flops | bytes accessed | tf_op | source)
XLA Modules:
  0.0 50.9 jit_solution(10711245424150943723)
XLA Ops:
  0.6 1.2 %tables.1 = (f32[72,512]{1,0:T(8,128)S(1)}, bf16[144,256]{1,0:T(8,128)(2,1)S(1)}, bf16[80,256]{1,0:T(8,128)(2,1)S(1)}, s32[1,256]{1,0:T(1,128)S(1)}) custom-call(f32[3,512]{1,0:T(4,128)} %refs_0_.1, bf16[64,512]{1,0:T(8,128)(2,1)} %refs_1_.3, s32[1,512]{1,0:T(1,128)} %bitcast.19, bf16[1,4]{1,0:T(2,128)(2,1)} %bitcast.21, bf16[64,64]{1,0:T(8,128)(2,1)} %refs_4_.1, ...), custom_call_target="tpu_custom_call" | custom-call | tf_op jit(solution)/shard_map/tables/pallas_call | solution.py:533
  1.9 5.1 %collective-permute-start = (bf16[80,256]{1,0:T(8,128)(2,1)S(1)}, bf16[80,256]{1,0:T(8,128)(2,1)S(1)}, u32[]{:S(2)}, u32[]{:S(2)}) collective-permute-start(bf16[80,256]{1,0:T(8,128)(2,1)S(1)} %get-tuple-element.33.offered_ref), channel_id=1, source_target_pairs={{0,3},{1,0},{2,1},{3,2},{4,7},{5,4},{6,5},{7,6},{8,11},{9,8},{10,9... | collective-permute-start | bytes 122888 | tf_op jit(solution)/shard_map/ppermute | solution.py:497
  7.0 1.5 %weights.1 = (bf16[1024,256]{1,0:T(8,128)(2,1)S(1)}, bf16[256,128]{1,0:T(8,128)(2,1)S(1)}, bf16[64,256]{1,0:T(8,128)(2,1)S(1)}, f32[64,128]{1,0:T(8,128)S(1)}, s...) custom-call(f32[8,64]{1,0:T(8,128)} %bitcast.18, bf16[64,64]{1,0:T(8,128)(2,1)} %refs_1_.2, ...), custom_call_target="tpu_custom_call" | custom-call | tf_op jit(solution)/shard_map/weights/pallas_call | solution.py:533
  8.5 0.2 collective-permute-done.from_z_ref.refs_9_
  8.7 1.5 %collective-permute-start.3 = (bf16[160,256]{1,0:T(8,128)(2,1)S(1)}, bf16[160,256]{1,0:T(8,128)(2,1)S(1)}, u32[]{:S(2)}, u32[]{:S(2)}) collective-permute-start(bf16[160,256]{1,0:T(8,128)(2,1)S(1)} %two_blocks.1.refs_9_), channel_id=1, source_target_pairs={{0,28},{4,16},{8,20},{12,24},{16,12},{20,0},{24,4},{28,8},{1,29},{... | collective-permute-start | bytes 245768 | tf_op jit(solution)/shard_map/ppermute | solution.py:497
  10.2 1.2 %collective-permute-start.2 = (bf16[160,256]{1,0:T(8,128)(2,1)S(1)}, bf16[160,256]{1,0:T(8,128)(2,1)S(1)}, u32[]{:S(2)}, u32[]{:S(2)}) collective-permute-start(bf16[160,256]{1,0:T(8,128)(2,1)S(1)} %two_blocks.1.refs_9_), channel_id=1, source_target_pairs={{0,12},{4,0},{8,4},{12,8},{1,13},{5,1},{9,5},{13,9},{2,14},{6,2},{... | collective-permute-start | bytes 245768 | tf_op jit(solution)/shard_map/ppermute | solution.py:497
  11.4 0.5 %collective-permute-start.1 = (bf16[160,256]{1,0:T(8,128)(2,1)S(1)}, bf16[160,256]{1,0:T(8,128)(2,1)S(1)}, u32[]{:S(2)}, u32[]{:S(2)}) collective-permute-start(bf16[160,256]{1,0:T(8,128)(2,1)S(1)} %two_blocks.1.refs_9_), channel_id=1, source_target_pairs={{0,16},{16,0},{1,17},{17,1},{2,18},{18,2},{3,19},{19,3},{4,20},{20... | collective-permute-start | bytes 245768 | tf_op jit(solution)/shard_map/ppermute | solution.py:497
  11.9 0.0 copy-start
  11.9 0.0 copy-start.1
  11.9 0.0 copy-start.2
  11.9 8.7 %local_pairs.2.refs_8_ = f32[32,256]{1,0:T(8,128)S(1)} custom-call(s32[160,128]{1,0:T(8,128)S(1)} %get-tuple-element.24.refs_0_, s32[160,128]{1,0:T(8,128)S(1)} %get-tuple-element.25.refs_1_, s32[160,128]{1,0:T(8,128)S(1)} %get-tuple-element.26.refs_2_, f32[72,512]{1,0:T(8,128)S(1)} %get-tuple-element.27.refs_3_, ...), custom_call_target="tpu_custom_call" | custom-call | flops 4096000000 | bytes 122880 | tf_op jit(solution)/shard_map/local_pairs/pallas_call | solution.py:604
  20.7 0.0 collective-permute-done.3.refs_12_
  20.7 0.0 collective-permute-done.2.refs_11_
  20.7 0.0 collective-permute-done.1.refs_10_
  20.7 0.0 copy-done
  20.8 0.0 copy-done.1
  20.8 0.0 copy-done.2
  20.8 12.2 %ghost_pairs.1 = (f32[32,256]{1,0:T(8,128)S(1)}, f32[32,256]{1,0:T(8,128)S(1)}, f32[8,256]{1,0:T(8,128)S(1)}, f32[8,256]{1,0:T(8,128)S(1)}, f32[8,256]{1,0:T(8,128)S(1)}) custom-call(s32[96,128]{1,0:T(8,128)S(1)} %bitcast.12, s32[96,128]{1,0:T(8,128)S(1)} %bitcast.13, s32[96,128]{1,0:T(8,128)S(1)} %bitcast.14, f32[72,512]{1,0:T(8,128)S(1)} %get-tuple-element.27.refs_3_, ...), custom_call_target="tpu_custom_call" | custom-call | flops 4915200000 | bytes 147456 | tf_op jit(solution)/shard_map/ghost_pairs/pallas_call | solution.py:622
  33.0 0.3 collective-permute-start.4
  33.3 5.7 %collective-permute-done.4.refs_0_ = f32[32,256]{1,0:T(8,128)S(1)} collective-permute-done((f32[32,256]{1,0:T(8,128)S(1)}, f32[32,256]{1,0:T(8,128)S(1)}, u32[]{:S(2)}, u32[]{:S(2)}) %collective-permute-start.4) | collective-permute-done | bytes 32800 | tf_op jit(solution)/shard_map/ppermute | solution.py:497
  39.1 1.5 %collective-permute-start.5 = (f32[8,256]{1,0:T(8,128)S(1)}, f32[8,256]{1,0:T(8,128)S(1)}, u32[]{:S(2)}, u32[]{:S(2)}) collective-permute-start(f32[8,256]{1,0:T(8,128)S(1)} %get-tuple-element.41), channel_id=1, source_target_pairs={{0,16},{16,0},{1,17},{17,1},{2,18},{18,2},{3,19},{19,3},{4,20},{20... | collective-permute-start | bytes 24584 | tf_op jit(solution)/shard_map/ppermute | solution.py:497
  40.6 0.0 collective-permute-start.6
  40.6 0.8 %collective-permute-start.7 = (f32[8,256]{1,0:T(8,128)S(1)}, f32[8,256]{1,0:T(8,128)S(1)}, u32[]{:S(2)}, u32[]{:S(2)}) collective-permute-start(f32[8,256]{1,0:T(8,128)S(1)} %get-tuple-element.43), channel_id=1, source_target_pairs={{0,20},{4,24},{8,28},{12,16},{16,4},{20,8},{24,12},{28,0},{1,21},{... | collective-permute-start | bytes 24584 | tf_op jit(solution)/shard_map/ppermute | solution.py:497
  41.3 8.8 %local_pairs.3.refs_0_ = f32[32,256]{1,0:T(8,128)S(1)} custom-call(s32[160,128]{1,0:T(8,128)S(1)} %get-tuple-element.24.refs_0_, s32[160,128]{1,0:T(8,128)S(1)} %get-tuple-element.25.refs_1_, s32[160,128]{1,0:T(8,128)S(1)} %get-tuple-element.26.refs_2_, f32[72,512]{1,0:T(8,128)S(1)} %get-tuple-element.27.refs_3_, ...), custom_call_target="tpu_custom_call" | custom-call | flops 4096000000 | bytes 122880 | tf_op jit(solution)/shard_map/local_pairs/pallas_call | solution.py:604
  50.1 0.0 collective-permute-done.5.refs_3_
  50.1 0.0 collective-permute-done.6.refs_4_
  50.1 0.0 collective-permute-done.7.refs_5_
  50.1 0.8 %totals.1 = (f32[3,512]{1,0:T(4,128)}, f32[1,512]{1,0:T(1,128)}) custom-call(f32[32,256]{1,0:T(8,128)S(1)} %local_pairs.3.refs_0_, s32[1,256]{1,0:T(1,128)S(1)} %get-tuple-element.40.refs_1_, f32[8,256]{1,0:T(8,128)S(1)} %get-tuple-element.39.refs_10_.refs_2_, f32[8,256]{1,0:T(8,128)S(1)} %collective-permute-done.5.refs_3_, ...), custom_call_target="tpu_custom_call" | custom-call | tf_op jit(solution)/shard_map/totals/pallas_call | solution.py:637
  (2 shorter events, 0.0 us)
Async XLA Ops:
  1.9 6.8 %collective-permute-start = (bf16[80,256]{1,0:T(8,128)(2,1)S(1)}, bf16[80,256]{1,0:T(8,128)(2,1)S(1)}, u32[]{:S(2)}, u32[]{:S(2)}) collective-permute-start(bf16[80,256]{1,0:T(8,128)(2,1)S(1)} %get-tuple-element.33.offered_ref), channel_id=1, source_target_pairs={{0,3},{1,0},{2,1},{3,2},{4,7},{5,4},{6,5},{7,6},{8,11},{9,8},{10,9... | collective-permute-start | bytes 122888 | tf_op jit(solution)/shard_map/ppermute | solution.py:497
  8.7 12.0 %collective-permute-start.3 = (bf16[160,256]{1,0:T(8,128)(2,1)S(1)}, bf16[160,256]{1,0:T(8,128)(2,1)S(1)}, u32[]{:S(2)}, u32[]{:S(2)}) collective-permute-start(bf16[160,256]{1,0:T(8,128)(2,1)S(1)} %two_blocks.1.refs_9_), channel_id=1, source_target_pairs={{0,28},{4,16},{8,20},{12,24},{16,12},{20,0},{24,4},{28,8},{1,29},{... | collective-permute-start | bytes 245768 | tf_op jit(solution)/shard_map/ppermute | solution.py:497
  10.2 10.5 %collective-permute-start.2 = (bf16[160,256]{1,0:T(8,128)(2,1)S(1)}, bf16[160,256]{1,0:T(8,128)(2,1)S(1)}, u32[]{:S(2)}, u32[]{:S(2)}) collective-permute-start(bf16[160,256]{1,0:T(8,128)(2,1)S(1)} %two_blocks.1.refs_9_), channel_id=1, source_target_pairs={{0,12},{4,0},{8,4},{12,8},{1,13},{5,1},{9,5},{13,9},{2,14},{6,2},{... | collective-permute-start | bytes 245768 | tf_op jit(solution)/shard_map/ppermute | solution.py:497
  11.4 9.3 %collective-permute-start.1 = (bf16[160,256]{1,0:T(8,128)(2,1)S(1)}, bf16[160,256]{1,0:T(8,128)(2,1)S(1)}, u32[]{:S(2)}, u32[]{:S(2)}) collective-permute-start(bf16[160,256]{1,0:T(8,128)(2,1)S(1)} %two_blocks.1.refs_9_), channel_id=1, source_target_pairs={{0,16},{16,0},{1,17},{17,1},{2,18},{18,2},{3,19},{19,3},{4,20},{20... | collective-permute-start | bytes 245768 | tf_op jit(solution)/shard_map/ppermute | solution.py:497
  11.9 8.8 %copy-start = (s32[12288]{0:T(1024)S(1)}, s32[12288]{0:T(1024)}, u32[]{:S(2)}) copy-start(s32[12288]{0:T(1024)} %param.31) | copy-start | bytes 147460
  11.9 8.8 %copy-start.1 = (s32[12288]{0:T(1024)S(1)}, s32[12288]{0:T(1024)}, u32[]{:S(2)}) copy-start(s32[12288]{0:T(1024)} %param.32) | copy-start | bytes 147460
  11.9 8.8 %copy-start.2 = (s32[12288]{0:T(1024)S(1)}, s32[12288]{0:T(1024)}, u32[]{:S(2)}) copy-start(s32[12288]{0:T(1024)} %param.33) | copy-start | bytes 147460
  33.0 6.1 %collective-permute-start.4 = (f32[32,256]{1,0:T(8,128)S(1)}, f32[32,256]{1,0:T(8,128)S(1)}, u32[]{:S(2)}, u32[]{:S(2)}) collective-permute-start(f32[32,256]{1,0:T(8,128)S(1)} %get-tuple-element.35), channel_id=1, source_target_pairs={{0,1},{1,2},{2,3},{3,0},{4,5},{5,6},{6,7},{7,4},{8,9},{9,10},{10,1... | collective-permute-start | bytes 98312 | tf_op jit(solution)/shard_map/ppermute | solution.py:497
  39.1 11.0 %collective-permute-start.5 = (f32[8,256]{1,0:T(8,128)S(1)}, f32[8,256]{1,0:T(8,128)S(1)}, u32[]{:S(2)}, u32[]{:S(2)}) collective-permute-start(f32[8,256]{1,0:T(8,128)S(1)} %get-tuple-element.41), channel_id=1, source_target_pairs={{0,16},{16,0},{1,17},{17,1},{2,18},{18,2},{3,19},{19,3},{4,20},{20... | collective-permute-start | bytes 24584 | tf_op jit(solution)/shard_map/ppermute | solution.py:497
  40.6 9.6 %collective-permute-start.6 = (f32[8,256]{1,0:T(8,128)S(1)}, f32[8,256]{1,0:T(8,128)S(1)}, u32[]{:S(2)}, u32[]{:S(2)}) collective-permute-start(f32[8,256]{1,0:T(8,128)S(1)} %get-tuple-element.42), channel_id=1, source_target_pairs={{0,4},{4,8},{8,12},{12,0},{1,5},{5,9},{9,13},{13,1},{2,6},{6,10},{... | collective-permute-start | bytes 24584 | tf_op jit(solution)/shard_map/ppermute | solution.py:497
  40.6 9.6 %collective-permute-start.7 = (f32[8,256]{1,0:T(8,128)S(1)}, f32[8,256]{1,0:T(8,128)S(1)}, u32[]{:S(2)}, u32[]{:S(2)}) collective-permute-start(f32[8,256]{1,0:T(8,128)S(1)} %get-tuple-element.43), channel_id=1, source_target_pairs={{0,20},{4,24},{8,28},{12,16},{16,4},{20,8},{24,12},{28,0},{1,21},{... | collective-permute-start | bytes 24584 | tf_op jit(solution)/shard_map/ppermute | solution.py:497

commit v7 on v6

--- a/solution.py
+++ b/solution.py
@@ -38,12 +38,13 @@
     return lax.broadcasted_iota(jnp.int32, shape, dim)
 
 
-def one_hot(row, codes):
-    entry = jnp.broadcast_to(row.astype(f32), (16, row.shape[1])).astype(bf16)
+def one_hot(entry, codes):
+    entry = entry.astype(f32)
+    entry = jnp.concatenate([entry, entry], 0).astype(bf16)
     entry = jnp.concatenate([entry] * (codes.shape[0] // 16), 0)
     pieces = [
         jnp.where(codes == entry[:, start : start + LANES], bf16(1), bf16(0))
-        for start in range(0, row.shape[1], LANES)
+        for start in range(0, entry.shape[1], LANES)
     ]
     return jnp.concatenate(pieces, 1)
 
@@ -92,7 +93,7 @@
     left = dot(w_first_ref[...], features_ref[...]).astype(bf16).astype(f32)
     right = dot(w_second_ref[...], features_ref[...]).astype(bf16).astype(f32)
     own_ref[0:channels, :] = 0.5 * left
-    own_ref[channels:, :] = jnp.concatenate([positions, gain, jnp.zeros((EXTRA - 4, count), f32)], 0)
+    own_ref[channels:, :] = jnp.concatenate([positions, gain, positions, gain], 0)
     column = jnp.concatenate([0.5 * right, coord_rows(positions, gain)], 0)
     groups = count // GROUP
     rows = channels + EXTRA
@@ -102,7 +103,7 @@
         table = jnp.concatenate([table, jnp.zeros((spare, GROUP), f32)], 0)
     table = table.astype(bf16)
     right_ref[...] = table
-    send = send_ref[...]
+    send = jnp.broadcast_to(send_ref[...], (8, send_ref.shape[1]))
     picked = dot(table, one_hot(send & (GROUP - 1), row_codes(GROUP)))
     chosen = group_pick(picked, send // GROUP, rows, groups)
     chosen = jnp.concatenate([chosen, jnp.zeros((OFFERED - EXTRA, chosen.shape[1]), f32)], 0)
@@ -143,6 +144,7 @@
 
 
 def group_pick(values, high, rows, groups):
+    high = jnp.concatenate([high] * (rows // 8), 0)
     chosen = values[:rows]
     for group in range(1, groups):
         chosen = jnp.where(high == group, values[group * rows : (group + 1) * rows], chosen)
@@ -150,22 +152,27 @@
 
 
 def spread_groups(values, high, groups):
-    twice = jnp.concatenate([values, values], 0)
-    second = iota(twice.shape, 0) // 4
-    pieces = [jnp.where(high == second + group, twice, 0.0) for group in range(0, groups, 2)]
+    second = iota(values.shape, 0) // 4
+    pieces = [jnp.where(high == second + group, values, 0.0) for group in range(0, groups, 2)]
     return jnp.concatenate(pieces, 0)
 
 
-def lane_pick(table_ref, row):
+def lane_pick(table_ref, place):
     rows, count = table_ref.shape
-    lane = jnp.broadcast_to(row & (LANES - 1), (rows, LANES))
-    high = row // LANES
+    lane = jnp.concatenate([place & (LANES - 1)] * (rows // 8), 0)
+    high = jnp.concatenate([place // LANES] * (rows // 8), 0)
     chosen = None
     for group in range(count // LANES):
         part = table_ref[:, group * LANES : (group + 1) * LANES]
         picked = jnp.take_along_axis(part, lane, axis=1, mode="promise_in_bounds")
         chosen = picked if chosen is None else jnp.where(high == group, picked, chosen)
     return chosen
+
+
+def sum_rows(values, steps):
+    for step in steps:
+        values = values + pltpu.roll(values, step, 0)
+    return values
 
 
 def pair_body(
@@ -199,7 +206,8 @@
     steps = row_count // (per_step * block)
     w_out = jnp.concatenate([out_ref[...]] * line, 1)
     centers = iota((bases, CHUNK), 0).astype(f32) * (1.0 / (bases - 1))
-    sub = iota((8, CHUNK), 0)
+    last = iota((8, CHUNK), 0) % 4 == 3
+    partner_bits = (partner_groups * LANES - 1).bit_length()
     quads = range(QUAD)
     codes_ref[...] = row_codes(GROUP)
 
@@ -217,57 +225,47 @@
 
     def chunk(base, number):
         at = pl.multiple_of(base + number * block, block)
-        owner_rows = owner_ref[pl.ds(at, block), :]
-        partner_rows = partner_ref[pl.ds(at, block), :]
-        live_rows = mask_ref[pl.ds(at, block), :].astype(f32)
-
-        def row_of(values, quad):
-            return jnp.concatenate(
-                [values[quad * line + piece : quad * line + piece + 1, :] for piece in range(line)], 1
-            )
-
-        own_high, partner_high, projected, shifts, squares, weights, stacks, slopes = ([] for _ in range(8))
+        code_rows = owner_ref[pl.ds(at, block), :] * 2**partner_bits + partner_ref[pl.ds(at, block), :]
+        code_rows = code_rows * 2 + mask_ref[pl.ds(at, block), :]
+        owners, partners, lives, projected, shifts, squares, weights, stacks, slopes = ([] for _ in range(9))
         for quad in quads:
             cols = slice(quad * CHUNK, (quad + 1) * CHUNK)
-            owner = row_of(owner_rows, quad)
-            partner = row_of(partner_rows, quad)
-            own_high.append(owner // LANES)
-            partner_high.append(partner // LANES)
+            code = jnp.concatenate(
+                [
+                    jnp.broadcast_to(code_rows[row : row + 1, :], (8, LANES))
+                    for row in range(quad * line, (quad + 1) * line)
+                ],
+                1,
+            )
+            lives.append((code & 1).astype(f32))
+            partner = (code >> 1) & (2**partner_bits - 1)
+            owner = code >> (partner_bits + 1)
+            owners.append(owner)
+            partners.append(partner)
             hot[number, 0:LANES, cols] = one_hot(owner & (LANES - 1), codes_ref[0:LANES, :])
-            if hot_wide is None:
-                hot[number, LANES:, cols] = one_hot(partner & (LANES - 1), codes_ref[0:LANES, :])
-            else:
-                both = one_hot(partner & (GROUP - 1), codes_ref[...])
-                hot_wide[number, :, cols] = both
-                hot[number, LANES:, cols] = both[0:LANES] + both[LANES:]
+            wide = one_hot(partner & (GROUP - 1), codes_ref[...])
+            hot_wide[number, :, cols] = wide
+            hot[number, LANES:, cols] = wide[0:LANES] + wide[LANES:]
             yield
         for quad in quads:
             cols = slice(quad * CHUNK, (quad + 1) * CHUNK)
-            pieces = []
-            for piece in range(line):
-                at_row = quad * line + piece
-                pieces.append(lane_pick(own_ref, owner_rows[at_row : at_row + 1, :]))
-            own_vals = jnp.concatenate(pieces, 1)
-            if hot_wide is None:
-                pieces = []
-                for piece in range(line):
-                    at_row = quad * line + piece
-                    pieces.append(lane_pick(right_ref, partner_rows[at_row : at_row + 1, :]))
-                partner_vals = jnp.concatenate(pieces, 1)
-                partner_coords = partner_vals[channels:]
-            else:
-                wide_high = row_of(partner_rows, quad) // GROUP
-                partner_vals = group_pick(
-                    dot(right_ref[...], hot_wide[number, :, cols]), wide_high, rows, partner_groups * LANES // GROUP
-                )
-                extra = partner_vals[channels:]
-                partner_coords = extra + jnp.concatenate([extra[4:], extra[:4]], 0)
+            own_vals = jnp.concatenate(
+                [lane_pick(own_ref, owners[quad][:, start : start + LANES]) for start in range(0, CHUNK, LANES)], 1
+            )
+            partner_vals = group_pick(
+                dot(right_ref[...], hot_wide[number, :, cols]),
+                partners[quad] // GROUP,
+                rows,
+                partner_groups * LANES // GROUP,
+            )
             projected.append(own_vals[:channels] + partner_vals[:channels])
             own_coords = own_vals[channels:]
+            extra = partner_vals[channels:]
+            partner_coords = extra + pltpu.roll(extra, 4, 0)
             shift = partner_coords - own_coords
-            square = shift * shift
-            squared = square[0:1] + square[1:2] + square[2:3]
-            weights.append(row_of(live_rows, quad) * own_coords[3:4] * partner_coords[3:4])
+            squared = sum_rows(jnp.where(last, 0.0, shift * shift), (2, 1))
+            gain = sum_rows(jnp.where(last, own_coords * partner_coords, 0.0), (2, 1))
+            weights.append(lives[quad] * gain)
             away = squared - centers
             basis = jnp.exp(-basis_width * (away * away))
             basis_high, basis_low = split_two(basis)
@@ -296,7 +294,9 @@
         readouts = []
         for quad in quads:
             hidden, slope = silu_pair(part(half, quad))
-            readouts.append(jnp.sum(w_out * hidden, axis=0, keepdims=True))
+            terms = w_out * hidden
+            terms = sum(terms[start : start + 8] for start in range(8, channels, 8)) + terms[:8]
+            readouts.append(sum_rows(terms, (4, 2, 1)))
             pieces.append(((0.5 * w_out) * slope).astype(bf16))
         yield
         back = dot(matrix(2), jnp.concatenate(pieces, 0))
@@ -310,18 +310,18 @@
         parts = []
         for quad in quads:
             two = part(back, quad, 2 * bases)
-            readout_slope = jnp.sum((two[:bases] + two[bases:]) * slopes[quad], axis=0, keepdims=True)
+            readout_slope = sum_rows((two[:bases] + two[bases:]) * slopes[quad], (4, 2, 1))
             near = jnp.maximum(1.0 - squares[quad], 0.0)
             weight_near = weights[quad] * near
             energy = weight_near * near * readouts[quad]
             slope = weight_near * (near * readout_slope - 2.0 * readouts[quad])
             push = (2.0 * slope) * shifts[quad]
-            values = jnp.where(sub == 3, energy, push)[:4]
+            values = jnp.where(last, energy, push)
             parts.append(
                 jnp.concatenate(
                     [
-                        spread_groups(values, own_high[quad], own_groups),
-                        spread_groups(values, partner_high[quad], partner_groups),
+                        spread_groups(values, owners[quad] // LANES, own_groups),
+                        spread_groups(values, partners[quad] // LANES, partner_groups),
                     ],
                     0,
                 ).astype(bf16)
@@ -343,11 +343,11 @@
     lax.fori_loop(0, steps, step, 0)
 
 
-def local_kernel(per_step, channels, bases, first_row, row_count, with_start, *refs):
-    count = 10 + with_start
+def local_kernel(per_step, channels, bases, first_row, row_count, counts, *refs):
+    count = 9 + sum(counts)
     owner, partner, mask, own, right, *weights = refs[:9]
     sums, hot, *scratch = refs[count:]
-    sums[...] = refs[9][...] if with_start else jnp.zeros_like(sums)
+    sums[...] = refs[9][...] if counts[0] else jnp.zeros_like(sums)
     groups = own.shape[1] // LANES
     pair_body(
         per_step,
@@ -426,7 +426,7 @@
             level[PLANAR.index(offset[:2])][...] = force
 
 
-def pair_kernel(offered_ref, from_z_ref, both_ref):
+def pair_kernel(offered_ref, from_z_ref, unused_ref, both_ref):
     count = offered_ref.shape[0]
     both_ref[0:count, :] = offered_ref[...]
     both_ref[count:, :] = from_z_ref[...]
@@ -434,7 +434,7 @@
 
 def merge_kernel(*refs):
     upward, *level = refs[: 1 + len(PLANAR)]
-    outs = refs[1 + len(PLANAR) :]
+    outs = refs[2 + len(PLANAR) :]
     outs[0][...] = upward[0:8, :]
     for place, part in enumerate(level):
         outs[1 + place][...] = part[...] + upward[8 * place + 8 : 8 * place + 16, :]
@@ -446,8 +446,8 @@
     incoming = arrived[0][...]
     for part in arrived[1:]:
         incoming = incoming + part[...]
-    high, low = split_two(incoming[:4])
-    send = send_ref[...]
+    high, low = split_two(jnp.concatenate([incoming[:4], incoming[:4]], 0))
+    send = jnp.broadcast_to(send_ref[...], (8, send_ref.shape[1]))
     groups = sums_ref.shape[0] // 8
     hot = one_hot(send & (LANES - 1), row_codes(LANES))
     spread = [spread_groups(value, send // LANES, groups).astype(bf16) for value in (high, low)]
@@ -580,11 +580,6 @@
         3,
     )
     local = (local_first, local_second, local_mask)
-    (both,) = call(
-        pair_kernel, (whole((2 * offered.shape[0], send_count), bf16),), "two_blocks", specs=[whole_spec] * 2
-    )(offered, from_z)
-    arrived = [from_z] + [shifted(both, (*step, 0), sizes, 1) for step in PLANAR]
-
     def scratch(per_step, hots):
         return [pltpu.VMEM((per_step, GROUP, QUAD * CHUNK), bf16) for _ in range(hots)] + [
             pltpu.VMEM((per_step, QUAD, channels, CHUNK), f32),
@@ -595,15 +590,15 @@
     def cost(slots):
         return pl.CostEstimate(flops=slots * 400000, bytes_accessed=slots * 12, transcendentals=slots * 200)
 
-    parts = 2
+    parts = 4
     part_rows = local[0].shape[0] // parts
     local_step = part_rows * LANES // (QUAD * CHUNK)
 
     def local_call(part, start, after):
-        operands = [*local, own, right, *weights, *start, after]
+        operands = [*local, own, right, *weights, *start, *after]
         (sums,) = call(
             functools.partial(
-                local_kernel, local_step, channels, bases, part * part_rows, part_rows, len(start)
+                local_kernel, local_step, channels, bases, part * part_rows, part_rows, (len(start), len(after))
             ),
             (whole((groups * 8, GROUP), f32),),
             "local_pairs",
@@ -613,7 +608,12 @@
         )(*operands)
         return sums
 
-    sums = local_call(0, (), both)
+    sums = local_call(0, (), ())
+    (both,) = call(
+        pair_kernel, (whole((2 * offered.shape[0], send_count), bf16),), "two_blocks", specs=[whole_spec] * 3
+    )(offered, from_z, sums)
+    arrived = [from_z] + [shifted(both, (*step, 0), sizes, 1) for step in PLANAR]
+    sums = local_call(1, (sums,), (both,))
     ghost_lists = [tiles(value) for value in (ghost_owner, ghost_index, ghost_mask)]
     ghost_step = ghost_owner.shape[0] // (QUAD * CHUNK)
     partner_rows = blocks * GROUP // LANES * 4
@@ -629,11 +629,12 @@
         cost(ghost_owner.shape[0]),
     )(*ghost_lists, own, *weights, sums, *arrived)
     upward = shifted(upward, (0, 0, 1), sizes, -1)
+    sums = local_call(2, (sums,), ())
     mine, *level = call(
-        merge_kernel, (force,) * (1 + len(PLANAR)), "forces_upward", specs=[whole_spec] * (1 + len(PLANAR))
-    )(upward, *level)
+        merge_kernel, (force,) * (1 + len(PLANAR)), "forces_upward", specs=[whole_spec] * (2 + len(PLANAR))
+    )(upward, *level, sums)
     returned = [shifted(part, (*step, 0), sizes, -1) for part, step in zip(level, PLANAR)]
-    sums = local_call(1, (sums,), mine)
+    sums = local_call(3, (sums,), (mine,))
     forces, energy = call(
         final_kernel,
         (whole((3, own_count), f32), whole((1, own_count), f32)),

time: 51.1 us -> 47.9 us (0.937)
  waiting for transfers between devices: 5.96 us -> 0.83 us
  Pallas kernels: 33.2 us -> 35.3 us
    ppermute x8, waiting for transfers between devices: 5.96 us -> 0.83 us  [shifted(): return lax.ppermute(value, tuple((name for name, size in used)), pairs)]
    pallas_call x2 -> x4, Pallas kernels: 17.5 us -> 19.7 us  [local_call(): call(functools.partial(local_kernel, local_step, channels, bases, part *...]
  transfers between devices with their start and end apart: 8 -> 8, of which waited for: 2 -> 1; matrix products, arithmetic and copies ran while one was open for 0% -> 0% of each run, Pallas kernels for 37% -> 45%
where the time goes in v7:
time: 47.9 us; the launch traced here: 47.6 us
  Pallas kernels  35.3 us (74%)
  starting transfers between devices  10.7 us (22%)
  waiting for transfers between devices  0.83 us (2%)
  between operations  0.77 us (2%)
    pallas_call x4, Pallas kernels, local_call(): call(functools.partial(local_kernel, local_step, channels, bases, part *...  19.7 us
    pallas_call x1, Pallas kernels, on_device(): call(functools.partial(ghost_kernel, ghost_step, channels, bases), (whole...  12 us
    ppermute x8, starting transfers between devices, shifted(): return lax.ppermute(value, tuple((name for name, size in used)), pairs)  10.7 us
    pallas_call x2, Pallas kernels, fetching(): call(kernel, outs + tuple((whole(value.shape, value.dtype) for value in o...  2.75 us
  transfers between devices with their start and end apart: 8, of which 1 were waited for; matrix products, arithmetic and copies ran while one was open for 0% of the time, Pallas kernels for 45%

profile of v7, /device:TPU:0, one launch (start us, length us, event | category | flops | bytes accessed | tf_op | source)
XLA Modules:
  0.0 47.6 jit_solution(11091889132850474141)
XLA Ops:
  0.6 1.2 %tables.1 = (f32[72,512]{1,0:T(8,128)S(1)}, bf16[144,256]{1,0:T(8,128)(2,1)S(1)}, bf16[80,256]{1,0:T(8,128)(2,1)S(1)}, s32[1,256]{1,0:T(1,128)S(1)}) custom-call(f32[3,512]{1,0:T(4,128)} %refs_0_.1, bf16[64,512]{1,0:T(8,128)(2,1)} %refs_1_.3, s32[1,512]{1,0:T(1,128)} %bitcast.19, bf16[1,4]{1,0:T(2,128)(2,1)} %bitcast.21, bf16[64,64]{1,0:T(8,128)(2,1)} %refs_4_.1, ...), custom_call_target="tpu_custom_call" | custom-call | tf_op jit(solution)/shard_map/tables/pallas_call | solution.py:533
  1.9 5.1 %collective-permute-start = (bf16[80,256]{1,0:T(8,128)(2,1)S(1)}, bf16[80,256]{1,0:T(8,128)(2,1)S(1)}, u32[]{:S(2)}, u32[]{:S(2)}) collective-permute-start(bf16[80,256]{1,0:T(8,128)(2,1)S(1)} %get-tuple-element.33.offered_ref), channel_id=1, source_target_pairs={{0,3},{1,0},{2,1},{3,2},{4,7},{5,4},{6,5},{7,6},{8,11},{9,8},{10,9... | collective-permute-start | bytes 122888 | tf_op jit(solution)/shard_map/ppermute | solution.py:497
  7.0 1.5 %weights.1 = (bf16[1024,256]{1,0:T(8,128)(2,1)S(1)}, bf16[256,128]{1,0:T(8,128)(2,1)S(1)}, bf16[64,256]{1,0:T(8,128)(2,1)S(1)}, f32[64,128]{1,0:T(8,128)S(1)}, s...) custom-call(f32[8,64]{1,0:T(8,128)} %bitcast.18, bf16[64,64]{1,0:T(8,128)(2,1)} %refs_1_.2, ...), custom_call_target="tpu_custom_call" | custom-call | tf_op jit(solution)/shard_map/weights/pallas_call | solution.py:533
  8.5 4.9 %local_pairs.4.unused_ref.refs_9_ = f32[32,256]{1,0:T(8,128)S(1)} custom-call(s32[160,128]{1,0:T(8,128)S(1)} %get-tuple-element.24.refs_0_, s32[160,128]{1,0:T(8,128)S(1)} %get-tuple-element.25.refs_1_, s32[160,128]{1,0:T(8,128)S(1)} %get-tuple-element.26.refs_2_, f32[72,512]{1,0:T(8,128)S(1)} %get-tuple-element.27.refs_3_, ...), custom_call_target="tpu_custom_call" | custom-call | flops 2048000000 | bytes 61440 | tf_op jit(solution)/shard_map/local_pairs/pallas_call | solution.py:599
  13.4 0.0 collective-permute-done.from_z_ref.refs_9_
  13.5 0.0 copy-start
  13.5 0.0 copy-start.1
  13.5 0.0 copy-start.2
  13.5 1.7 %collective-permute-start.3 = (bf16[160,256]{1,0:T(8,128)(2,1)S(1)}, bf16[160,256]{1,0:T(8,128)(2,1)S(1)}, u32[]{:S(2)}, u32[]{:S(2)}) collective-permute-start(bf16[160,256]{1,0:T(8,128)(2,1)S(1)} %two_blocks.1.refs_10_), channel_id=1, source_target_pairs={{0,28},{4,16},{8,20},{12,24},{16,12},{20,0},{24,4},{28,8},{1,29},{... | collective-permute-start | bytes 245768 | tf_op jit(solution)/shard_map/ppermute | solution.py:497
  15.2 1.1 %collective-permute-start.2 = (bf16[160,256]{1,0:T(8,128)(2,1)S(1)}, bf16[160,256]{1,0:T(8,128)(2,1)S(1)}, u32[]{:S(2)}, u32[]{:S(2)}) collective-permute-start(bf16[160,256]{1,0:T(8,128)(2,1)S(1)} %two_blocks.1.refs_10_), channel_id=1, source_target_pairs={{0,12},{4,0},{8,4},{12,8},{1,13},{5,1},{9,5},{13,9},{2,14},{6,2},{... | collective-permute-start | bytes 245768 | tf_op jit(solution)/shard_map/ppermute | solution.py:497
  16.3 0.5 %collective-permute-start.1 = (bf16[160,256]{1,0:T(8,128)(2,1)S(1)}, bf16[160,256]{1,0:T(8,128)(2,1)S(1)}, u32[]{:S(2)}, u32[]{:S(2)}) collective-permute-start(bf16[160,256]{1,0:T(8,128)(2,1)S(1)} %two_blocks.1.refs_10_), channel_id=1, source_target_pairs={{0,16},{16,0},{1,17},{17,1},{2,18},{18,2},{3,19},{19,3},{4,20},{20... | collective-permute-start | bytes 245768 | tf_op jit(solution)/shard_map/ppermute | solution.py:497
  16.8 4.9 %local_pairs.5.refs_8_ = f32[32,256]{1,0:T(8,128)S(1)} custom-call(s32[160,128]{1,0:T(8,128)S(1)} %get-tuple-element.24.refs_0_, s32[160,128]{1,0:T(8,128)S(1)} %get-tuple-element.25.refs_1_, s32[160,128]{1,0:T(8,128)S(1)} %get-tuple-element.26.refs_2_, f32[72,512]{1,0:T(8,128)S(1)} %get-tuple-element.27.refs_3_, ...), custom_call_target="tpu_custom_call" | custom-call | flops 2048000000 | bytes 61440 | tf_op jit(solution)/shard_map/local_pairs/pallas_call | solution.py:599
  21.8 0.0 collective-permute-done.3.refs_12_
  21.8 0.0 collective-permute-done.2.refs_11_
  21.8 0.0 collective-permute-done.1.refs_10_
  21.8 0.0 copy-done
  21.8 0.0 copy-done.1
  21.8 0.0 copy-done.2
  21.8 12.0 %ghost_pairs.1 = (f32[32,256]{1,0:T(8,128)S(1)}, f32[32,256]{1,0:T(8,128)S(1)}, f32[8,256]{1,0:T(8,128)S(1)}, f32[8,256]{1,0:T(8,128)S(1)}, f32[8,256]{1,0:T(8,128)S(1)}) custom-call(s32[96,128]{1,0:T(8,128)S(1)} %bitcast.12, s32[96,128]{1,0:T(8,128)S(1)} %bitcast.13, s32[96,128]{1,0:T(8,128)S(1)} %bitcast.14, f32[72,512]{1,0:T(8,128)S(1)} %get-tuple-element.27.refs_3_, ...), custom_call_target="tpu_custom_call" | custom-call | flops 4915200000 | bytes 147456 | tf_op jit(solution)/shard_map/ghost_pairs/pallas_call | solution.py:622
  33.9 0.1 collective-permute-start.4
  33.9 4.9 %local_pairs.6.refs_4_.refs_9_ = f32[32,256]{1,0:T(8,128)S(1)} custom-call(s32[160,128]{1,0:T(8,128)S(1)} %get-tuple-element.24.refs_0_, s32[160,128]{1,0:T(8,128)S(1)} %get-tuple-element.25.refs_1_, s32[160,128]{1,0:T(8,128)S(1)} %get-tuple-element.26.refs_2_, f32[72,512]{1,0:T(8,128)S(1)} %get-tuple-element.27.refs_3_, ...), custom_call_target="tpu_custom_call" | custom-call | flops 2048000000 | bytes 61440 | tf_op jit(solution)/shard_map/local_pairs/pallas_call | solution.py:599
  38.9 0.8 %collective-permute-done.4.refs_0_ = f32[32,256]{1,0:T(8,128)S(1)} collective-permute-done((f32[32,256]{1,0:T(8,128)S(1)}, f32[32,256]{1,0:T(8,128)S(1)}, u32[]{:S(2)}, u32[]{:S(2)}) %collective-permute-start.4) | collective-permute-done | bytes 32800 | tf_op jit(solution)/shard_map/ppermute | solution.py:497
  39.6 1.5 %collective-permute-start.5 = (f32[8,256]{1,0:T(8,128)S(1)}, f32[8,256]{1,0:T(8,128)S(1)}, u32[]{:S(2)}, u32[]{:S(2)}) collective-permute-start(f32[8,256]{1,0:T(8,128)S(1)} %get-tuple-element.41), channel_id=1, source_target_pairs={{0,16},{16,0},{1,17},{17,1},{2,18},{18,2},{3,19},{19,3},{4,20},{20... | collective-permute-start | bytes 24584 | tf_op jit(solution)/shard_map/ppermute | solution.py:497
  41.1 0.0 collective-permute-start.6
  41.1 0.8 %collective-permute-start.7 = (f32[8,256]{1,0:T(8,128)S(1)}, f32[8,256]{1,0:T(8,128)S(1)}, u32[]{:S(2)}, u32[]{:S(2)}) collective-permute-start(f32[8,256]{1,0:T(8,128)S(1)} %get-tuple-element.43), channel_id=1, source_target_pairs={{0,20},{4,24},{8,28},{12,16},{16,4},{20,8},{24,12},{28,0},{1,21},{... | collective-permute-start | bytes 24584 | tf_op jit(solution)/shard_map/ppermute | solution.py:497
  41.9 4.9 %local_pairs.7.refs_0_ = f32[32,256]{1,0:T(8,128)S(1)} custom-call(s32[160,128]{1,0:T(8,128)S(1)} %get-tuple-element.24.refs_0_, s32[160,128]{1,0:T(8,128)S(1)} %get-tuple-element.25.refs_1_, s32[160,128]{1,0:T(8,128)S(1)} %get-tuple-element.26.refs_2_, f32[72,512]{1,0:T(8,128)S(1)} %get-tuple-element.27.refs_3_, ...), custom_call_target="tpu_custom_call" | custom-call | flops 2048000000 | bytes 61440 | tf_op jit(solution)/shard_map/local_pairs/pallas_call | solution.py:599
  46.8 0.0 collective-permute-done.5.refs_3_
  46.9 0.0 collective-permute-done.6.refs_4_
  46.9 0.0 collective-permute-done.7.refs_5_
  46.9 0.8 %totals.1 = (f32[3,512]{1,0:T(4,128)}, f32[1,512]{1,0:T(1,128)}) custom-call(f32[32,256]{1,0:T(8,128)S(1)} %local_pairs.7.refs_0_, s32[1,256]{1,0:T(1,128)S(1)} %get-tuple-element.40.refs_1_, f32[8,256]{1,0:T(8,128)S(1)} %get-tuple-element.39.refs_10_.refs_2_, f32[8,256]{1,0:T(8,128)S(1)} %collective-permute-done.5.refs_3_, ...), custom_call_target="tpu_custom_call" | custom-call | tf_op jit(solution)/shard_map/totals/pallas_call | solution.py:638
  (2 shorter events, 0.0 us)
Async XLA Ops:
  1.9 11.5 %collective-permute-start = (bf16[80,256]{1,0:T(8,128)(2,1)S(1)}, bf16[80,256]{1,0:T(8,128)(2,1)S(1)}, u32[]{:S(2)}, u32[]{:S(2)}) collective-permute-start(bf16[80,256]{1,0:T(8,128)(2,1)S(1)} %get-tuple-element.33.offered_ref), channel_id=1, source_target_pairs={{0,3},{1,0},{2,1},{3,2},{4,7},{5,4},{6,5},{7,6},{8,11},{9,8},{10,9... | collective-permute-start | bytes 122888 | tf_op jit(solution)/shard_map/ppermute | solution.py:497
  13.5 8.3 %copy-start = (s32[12288]{0:T(1024)S(1)}, s32[12288]{0:T(1024)}, u32[]{:S(2)}) copy-start(s32[12288]{0:T(1024)} %param.31) | copy-start | bytes 147460
  13.5 8.3 %copy-start.1 = (s32[12288]{0:T(1024)S(1)}, s32[12288]{0:T(1024)}, u32[]{:S(2)}) copy-start(s32[12288]{0:T(1024)} %param.32) | copy-start | bytes 147460
  13.5 8.3 %copy-start.2 = (s32[12288]{0:T(1024)S(1)}, s32[12288]{0:T(1024)}, u32[]{:S(2)}) copy-start(s32[12288]{0:T(1024)} %param.33) | copy-start | bytes 147460
  13.5 8.3 %collective-permute-start.3 = (bf16[160,256]{1,0:T(8,128)(2,1)S(1)}, bf16[160,256]{1,0:T(8,128)(2,1)S(1)}, u32[]{:S(2)}, u32[]{:S(2)}) collective-permute-start(bf16[160,256]{1,0:T(8,128)(2,1)S(1)} %two_blocks.1.refs_10_), channel_id=1, source_target_pairs={{0,28},{4,16},{8,20},{12,24},{16,12},{20,0},{24,4},{28,8},{1,29},{... | collective-permute-start | bytes 245768 | tf_op jit(solution)/shard_map/ppermute | solution.py:497
  15.2 6.6 %collective-permute-start.2 = (bf16[160,256]{1,0:T(8,128)(2,1)S(1)}, bf16[160,256]{1,0:T(8,128)(2,1)S(1)}, u32[]{:S(2)}, u32[]{:S(2)}) collective-permute-start(bf16[160,256]{1,0:T(8,128)(2,1)S(1)} %two_blocks.1.refs_10_), channel_id=1, source_target_pairs={{0,12},{4,0},{8,4},{12,8},{1,13},{5,1},{9,5},{13,9},{2,14},{6,2},{... | collective-permute-start | bytes 245768 | tf_op jit(solution)/shard_map/ppermute | solution.py:497
  16.3 5.5 %collective-permute-start.1 = (bf16[160,256]{1,0:T(8,128)(2,1)S(1)}, bf16[160,256]{1,0:T(8,128)(2,1)S(1)}, u32[]{:S(2)}, u32[]{:S(2)}) collective-permute-start(bf16[160,256]{1,0:T(8,128)(2,1)S(1)} %two_blocks.1.refs_10_), channel_id=1, source_target_pairs={{0,16},{16,0},{1,17},{17,1},{2,18},{18,2},{3,19},{19,3},{4,20},{20... | collective-permute-start | bytes 245768 | tf_op jit(solution)/shard_map/ppermute | solution.py:497
  33.9 5.8 %collective-permute-start.4 = (f32[32,256]{1,0:T(8,128)S(1)}, f32[32,256]{1,0:T(8,128)S(1)}, u32[]{:S(2)}, u32[]{:S(2)}) collective-permute-start(f32[32,256]{1,0:T(8,128)S(1)} %get-tuple-element.35), channel_id=1, source_target_pairs={{0,1},{1,2},{2,3},{3,0},{4,5},{5,6},{6,7},{7,4},{8,9},{9,10},{10,1... | collective-permute-start | bytes 98312 | tf_op jit(solution)/shard_map/ppermute | solution.py:497
  39.6 7.2 %collective-permute-start.5 = (f32[8,256]{1,0:T(8,128)S(1)}, f32[8,256]{1,0:T(8,128)S(1)}, u32[]{:S(2)}, u32[]{:S(2)}) collective-permute-start(f32[8,256]{1,0:T(8,128)S(1)} %get-tuple-element.41), channel_id=1, source_target_pairs={{0,16},{16,0},{1,17},{17,1},{2,18},{18,2},{3,19},{19,3},{4,20},{20... | collective-permute-start | bytes 24584 | tf_op jit(solution)/shard_map/ppermute | solution.py:497
  41.1 5.7 %collective-permute-start.6 = (f32[8,256]{1,0:T(8,128)S(1)}, f32[8,256]{1,0:T(8,128)S(1)}, u32[]{:S(2)}, u32[]{:S(2)}) collective-permute-start(f32[8,256]{1,0:T(8,128)S(1)} %get-tuple-element.42), channel_id=1, source_target_pairs={{0,4},{4,8},{8,12},{12,0},{1,5},{5,9},{9,13},{13,1},{2,6},{6,10},{... | collective-permute-start | bytes 24584 | tf_op jit(solution)/shard_map/ppermute | solution.py:497
  41.1 5.7 %collective-permute-start.7 = (f32[8,256]{1,0:T(8,128)S(1)}, f32[8,256]{1,0:T(8,128)S(1)}, u32[]{:S(2)}, u32[]{:S(2)}) collective-permute-start(f32[8,256]{1,0:T(8,128)S(1)} %get-tuple-element.43), channel_id=1, source_target_pairs={{0,20},{4,24},{8,28},{12,16},{16,4},{20,8},{24,12},{28,0},{1,21},{... | collective-permute-start | bytes 24584 | tf_op jit(solution)/shard_map/ppermute | solution.py:497
